TPU v7x, 32 devices: a whole 2x2x4 slice. The times are simulated.
32 devices in a mesh: expert: 4 (over z), context: 2 (over core), dp: 4 (over y, x).
Axes of the slice: x: 2, y: 2, z: 4, core: 2. Of those that a mesh axis runs over, the one named last changes fastest.
Arguments:
- tokens: bfloat16 [4, 1024, 2048], P('dp', ('expert', 'context')), may hold values from -6 to 6
- cotangent: bfloat16 [4, 1024, 2048], P('dp', ('expert', 'context')), may hold values from -6 to 6
- segments: int32 [4, 1024], P('dp'), may hold values from 0 to 2, as said below
- expert_ids: int32 [4, 1024, 4], P('dp', ('expert', 'context')), may hold values from 0 to 7, all different within a row
- slot_order: int32 [4, 8, 512], P('dp', ('expert', 'context')), may hold values from 0 to 511, each once within a row
- gate_weights: float32 [4, 1024, 4], P('dp', ('expert', 'context')), may hold values from 0.1 to 0.4
- qkv_weight: bfloat16 [2048, 6144], P(('expert', 'context', 'dp')), may hold values from -0.125 to 0.125
- qkv_bias: bfloat16 [6144], P(('expert', 'context', 'dp')), may hold values from -4 to 4
- out_weight: bfloat16 [2048, 2048], P(('expert', 'context', 'dp')), may hold values from -2 to 2
- norm_attn: bfloat16 [2048], P(('expert', 'context', 'dp')), may hold values from 0.5 to 1.5
- norm_ffn: bfloat16 [2048], P(('expert', 'context', 'dp')), may hold values from 0.5 to 1.5
- shared_gate_up: bfloat16 [2, 2048, 5632], P(None, ('context', 'dp'), 'expert'), may hold values from -0.125 to 0.125
- shared_down: bfloat16 [5632, 2048], P('expert', ('context', 'dp')), may hold values from -0.15625 to 0.15625
- shared_gate: bfloat16 [2048], P(('expert', 'context', 'dp')), may hold values from -0.125 to 0.125
- expert_gate_up: bfloat16 [8, 2048, 2816], P('expert', ('context', 'dp')), may hold values from -0.125 to 0.125
- expert_down: bfloat16 [8, 1408, 2048], P('expert', ('context', 'dp')), may hold values from -0.3125 to 0.3125
Outputs:
- block_output: bfloat16 [4, 1024, 2048], P('dp', ('expert', 'context'))
- input_grad: float32 [4, 1024, 2048], P('dp', ('expert', 'context'))
- qkv_weight_grad: float32 [2048, 6144], P(('expert', 'context', 'dp'))
- qkv_bias_grad: float32 [6144], P(('expert', 'context', 'dp'))
- out_weight_grad: float32 [2048, 2048], P(('expert', 'context', 'dp'))
- norm_attn_grad: float32 [2048], P(('expert', 'context', 'dp'))
- norm_ffn_grad: float32 [2048], P(('expert', 'context', 'dp'))
- shared_gate_up_grad: float32 [2, 2048, 5632], P(None, ('context', 'dp'), 'expert')
- shared_down_grad: float32 [5632, 2048], P('expert', ('context', 'dp'))
- shared_gate_grad: float32 [2048], P(('expert', 'context', 'dp'))
- expert_gate_up_grad: float32 [8, 2048, 2816], P('expert', ('context', 'dp'))
- expert_down_grad: float32 [8, 1408, 2048], P('expert', ('context', 'dp'))
Inputs may be any that keep to these rules, and one draw needn't show every extreme that they name: `segments`: each sequence holds exactly three documents, numbered 0 to 2 in order of position, none empty. `expert_ids`: each row names 4 different experts. `slot_order`: each row is a permutation of the block's 128 * 4 pairs.
All inputs are finite; a program needn't handle non-finite values.
Results may differ from a plain program's by a relative error of at most 0.017.
Values may be sent and summed in bfloat16 or wider, within the bound.
No kernel may reach another device: no remote copies, remote signals or barrier semaphores. Data moves between devices by JAX's collectives and lax.ppermute only.
A program may use at most 640 MiB of HBM per device.

v0:
```python
import math

import jax
import jax.numpy as jnp
from jax import lax
from jax.sharding import PartitionSpec as P

HEADS = 16
HEAD_DIM = 128


eps_norm = 1e-06
neg_fill = -1e30
rope_base = 1000000.0
group_heads = 4


def rope_tables(positions, half):
    inverse = jnp.exp(
        jnp.arange(half).astype(jnp.float32) * (-2.0 * math.log(rope_base) / (2 * half))
    )
    angle = positions.astype(jnp.float32)[:, None] * inverse[None, :]
    return (jnp.cos(angle), jnp.sin(angle))


def rotate(values, cosine, sine):
    half = values.shape[-1] // 2
    front = values[..., :half]
    behind = values[..., half:]
    cosine = cosine[:, None, :]
    sine = sine[:, None, :]
    return jnp.concatenate(
        [front * cosine - behind * sine, behind * cosine + front * sine], axis=-1
    )


def rotate_back(grads, cosine, sine):
    half = grads.shape[-1] // 2
    front = grads[..., :half]
    behind = grads[..., half:]
    cosine = cosine[:, None, :]
    sine = sine[:, None, :]
    return jnp.concatenate(
        [front * cosine + behind * sine, behind * cosine - front * sine], axis=-1
    )


def route(expert_row, order_row, experts, capacity):
    count = expert_row.shape[0]
    same_expert = expert_row[:, None] == expert_row[None, :]
    earlier = order_row[None, :] < order_row[:, None]
    rank = jnp.sum((same_expert & earlier).astype(jnp.int32), axis=1)
    kept_pair = rank < capacity
    slot = jnp.where(kept_pair, expert_row * capacity + rank, experts * capacity)
    source = (
        jnp.full((experts * capacity + 1,), count, jnp.int32)
        .at[slot]
        .set(jnp.arange(count, dtype=jnp.int32))
    )
    source = source[: experts * capacity]
    return (kept_pair, slot, source, source < count)


def silu_parts(grad_hidden, gate_pre, up_pre):
    sigma = jax.nn.sigmoid(gate_pre)
    gate_grad = grad_hidden * up_pre * sigma * (1.0 + gate_pre * (1.0 - sigma))
    up_grad = grad_hidden * gate_pre * sigma
    return (gate_grad, up_grad)


def shared_compute(rows, row_grads, up_weights, down_weights):
    floats = jnp.float32
    pre = jnp.einsum("td,gdf->gtf", rows, up_weights, preferred_element_type=floats)
    hidden = (jax.nn.silu(pre[0]) * pre[1]).astype(jnp.bfloat16)
    out_part = jnp.dot(hidden, down_weights, preferred_element_type=floats)
    hidden_grad = jnp.dot(row_grads, down_weights.T, preferred_element_type=floats)
    gate_part, up_part = silu_parts(hidden_grad, pre[0], pre[1])
    pre_grad = jnp.stack([gate_part, up_part]).astype(jnp.bfloat16)
    input_part = jnp.einsum("gtf,gdf->td", pre_grad, up_weights, preferred_element_type=floats)
    up_term = jnp.einsum("td,gtf->gdf", rows, pre_grad, preferred_element_type=floats)
    down_term = lax.dot_general(
        hidden, row_grads, (((0,), (0,)), ((), ())), preferred_element_type=floats
    )
    return (out_part, input_part, up_term, down_term)


def shards(
    tokens,
    cotangent,
    segments,
    expert_ids,
    slot_order,
    gate_weights,
    qkv_weight,
    qkv_bias,
    out_weight,
    norm_attn,
    norm_ffn,
    shared_gate_up,
    shared_down,
    shared_gate,
    expert_gate_up,
    expert_down,
):
    floats = jnp.float32
    halves = jnp.bfloat16
    (
        query_key_value_weight,
        query_key_value_bias,
        output_weight,
        gain_attn,
        gain_ffn,
        shared_gate_weight,
    ) = (
        lax.all_gather(qkv_weight, ("expert", "context", "dp"), axis=0, tiled=True),
        lax.all_gather(qkv_bias, ("expert", "context", "dp"), axis=0, tiled=True),
        lax.all_gather(out_weight, ("expert", "context", "dp"), axis=0, tiled=True),
        lax.all_gather(norm_attn, ("expert", "context", "dp"), axis=0, tiled=True),
        lax.all_gather(norm_ffn, ("expert", "context", "dp"), axis=0, tiled=True),
        lax.all_gather(shared_gate, ("expert", "context", "dp"), axis=0, tiled=True),
    )
    up_local, down_local = (
        lax.all_gather(shared_gate_up, ("context", "dp"), axis=1, tiled=True),
        lax.all_gather(shared_down, ("context", "dp"), axis=1, tiled=True),
    )
    w_expert_up, w_expert_down = (
        lax.all_gather(expert_gate_up, ("context", "dp"), axis=1, tiled=True),
        lax.all_gather(expert_down, ("context", "dp"), axis=1, tiled=True),
    )
    tok_count = tokens.shape[1]
    width = tokens.shape[2]
    seq_len = segments.shape[1]
    head_groups = HEADS // group_heads
    block_place = lax.axis_index(("expert", "context"))
    positions = block_place * tok_count + jnp.arange(tok_count, dtype=jnp.int32)
    cosine, sine = rope_tables(positions, HEAD_DIM // 2)
    scale = 1.0 / math.sqrt(HEAD_DIM)
    residual_input = tokens[0].astype(floats)
    stat_attn = lax.rsqrt(
        jnp.mean(residual_input * residual_input, axis=-1, keepdims=True) + eps_norm
    )
    unit_attn = residual_input * stat_attn
    gain_one = gain_attn.astype(floats)
    attention_normed_input = (unit_attn * gain_one).astype(halves)
    projected_output = jnp.dot(
        attention_normed_input, query_key_value_weight, preferred_element_type=floats
    ) + query_key_value_bias.astype(floats)
    query_raw = projected_output[:, :width].reshape(tok_count, HEADS, HEAD_DIM)
    key_raw = projected_output[:, width : 2 * width].reshape(tok_count, HEADS, HEAD_DIM)
    value_raw = projected_output[:, 2 * width :].reshape(tok_count, HEADS, HEAD_DIM)
    query = (rotate(query_raw, cosine, sine) * scale).astype(halves)
    key_rot = rotate(key_raw, cosine, sine).astype(halves)
    value_low = value_raw.astype(halves)
    query_groups = query.reshape(tok_count, head_groups, group_heads, HEAD_DIM).transpose(
        1, 0, 2, 3
    )
    key_send = key_rot.reshape(tok_count, head_groups, group_heads, HEAD_DIM).transpose(1, 0, 2, 3)
    value_send = value_low.reshape(tok_count, head_groups, group_heads, HEAD_DIM).transpose(
        1, 0, 2, 3
    )
    key_all, value_all = (
        lax.all_gather(key_send, ("expert", "context"), axis=1, tiled=True),
        lax.all_gather(value_send, ("expert", "context"), axis=1, tiled=True),
    )
    seq_ids = segments[0]
    query_ids = lax.dynamic_slice_in_dim(seq_ids, block_place * tok_count, tok_count)
    key_places = jnp.arange(seq_len, dtype=jnp.int32)
    visible = (key_places[None, :] <= positions[:, None]) & (seq_ids[None, :] == query_ids[:, None])

    def attend_group(pieces):
        q_part, k_part, v_part = pieces
        scores = jnp.einsum("qhd,khd->hqk", q_part, k_part, preferred_element_type=floats)
        scores = jnp.where(visible[None], scores, neg_fill)
        top_score = jnp.max(scores, axis=-1, keepdims=True)
        weights = jnp.exp(scores - top_score)
        total = jnp.sum(weights, axis=-1, keepdims=True)
        probs_low = (weights / total).astype(halves)
        mixed = jnp.einsum("hqk,khd->qhd", probs_low, v_part, preferred_element_type=floats)
        return (mixed, top_score + jnp.log(total))

    mixed_groups, log_totals = lax.map(attend_group, (query_groups, key_all, value_all))
    attention_result = mixed_groups.transpose(1, 0, 2, 3).reshape(tok_count, width).astype(halves)
    residual_middle = residual_input + jnp.dot(
        attention_result, output_weight, preferred_element_type=floats
    )
    stat_ffn = lax.rsqrt(
        jnp.mean(residual_middle * residual_middle, axis=-1, keepdims=True) + eps_norm
    )
    unit_ffn = residual_middle * stat_ffn
    gain_two = gain_ffn.astype(floats)
    feedforward_normed_input = (unit_ffn * gain_two).astype(halves)
    shared_gate_matrix = jax.nn.sigmoid(
        jnp.dot(
            feedforward_normed_input, shared_gate_weight[:, None], preferred_element_type=floats
        )
    )
    grad_out = cotangent[0].astype(floats)
    shared_grad = (shared_gate_matrix * grad_out).astype(halves)
    up_full, down_full = (
        lax.all_gather(up_local, "expert", axis=2, tiled=True),
        lax.all_gather(down_local, "expert", axis=0, tiled=True),
    )
    shared_output, shared_input_part, up_term, down_term = shared_compute(
        feedforward_normed_input, shared_grad, up_full, down_full
    )
    up_term, down_term = (
        lax.psum_scatter(up_term, "expert", scatter_dimension=2, tiled=True),
        lax.psum_scatter(down_term, "expert", scatter_dimension=0, tiled=True),
    )
    shared_up_out, shared_down_out = (
        lax.psum_scatter(up_term, ("context", "dp"), scatter_dimension=1, tiled=True),
        lax.psum_scatter(down_term, ("context", "dp"), scatter_dimension=1, tiled=True),
    )
    topk = expert_ids.shape[2]
    pairs = tok_count * topk
    groups = lax.axis_size("expert")
    local_experts = expert_gate_up.shape[0]
    experts = local_experts * groups
    capacity = (9 * pairs + 8 * experts - 1) // (8 * experts)
    ff_width = w_expert_down.shape[1]
    kept_pair, slot, source, filled = route(
        expert_ids[0].reshape(pairs), slot_order[0, 0], experts, capacity
    )
    safe_source = jnp.minimum(source, pairs - 1)
    slot_token = safe_source // topk
    pair_gate = gate_weights[0].reshape(pairs) * kept_pair.astype(floats)
    send_rows = jnp.where(
        filled[:, None], feedforward_normed_input[slot_token], jnp.zeros((), halves)
    )
    send_rows = send_rows.reshape(groups, local_experts, capacity, width)
    slot_gate = jnp.where(filled, pair_gate[safe_source], 0.0)
    slot_grad = (
        (grad_out[slot_token] * slot_gate[:, None])
        .astype(halves)
        .reshape(groups, local_experts, capacity, width)
    )
    expert_in, expert_grad = (
        lax.all_to_all(send_rows, "expert", split_axis=0, concat_axis=0, tiled=True),
        lax.all_to_all(slot_grad, "expert", split_axis=0, concat_axis=0, tiled=True),
    )
    expert_pre = jnp.einsum("secd,edf->secf", expert_in, w_expert_up, preferred_element_type=floats)
    expert_g = expert_pre[..., :ff_width]
    expert_u = expert_pre[..., ff_width:]
    expert_hidden = (jax.nn.silu(expert_g) * expert_u).astype(halves)
    expert_result = jnp.einsum(
        "secf,efd->secd", expert_hidden, w_expert_down, preferred_element_type=floats
    ).astype(halves)
    expert_hidden_grad = jnp.einsum(
        "secd,efd->secf", expert_grad, w_expert_down, preferred_element_type=floats
    )
    gate_part, up_part = silu_parts(expert_hidden_grad, expert_g, expert_u)
    expert_pre_grad = jnp.concatenate([gate_part, up_part], axis=-1).astype(halves)
    slot_in_grad = jnp.einsum(
        "secf,edf->secd", expert_pre_grad, w_expert_up, preferred_element_type=floats
    ).astype(halves)
    expert_up_term = jnp.einsum(
        "secd,secf->edf", expert_in, expert_pre_grad, preferred_element_type=floats
    )
    expert_down_term = jnp.einsum(
        "secf,secd->efd", expert_hidden, expert_grad, preferred_element_type=floats
    )
    expert_up_out, expert_down_out = (
        lax.psum_scatter(expert_up_term, ("context", "dp"), scatter_dimension=1, tiled=True),
        lax.psum_scatter(expert_down_term, ("context", "dp"), scatter_dimension=1, tiled=True),
    )
    returned, back_rows = (
        lax.all_to_all(expert_result, "expert", split_axis=0, concat_axis=0, tiled=True),
        lax.all_to_all(slot_in_grad, "expert", split_axis=0, concat_axis=0, tiled=True),
    )
    returned = jnp.concatenate(
        [returned.reshape(experts * capacity, width), jnp.zeros((1, width), halves)], axis=0
    )
    back_rows = jnp.concatenate(
        [back_rows.reshape(experts * capacity, width), jnp.zeros((1, width), halves)], axis=0
    )
    routed = (
        (returned[slot].astype(floats) * pair_gate[:, None])
        .reshape(tok_count, topk, width)
        .sum(axis=1)
    )
    layer_sum = residual_middle + shared_gate_matrix * shared_output + routed
    logit_grad = (
        jnp.sum(grad_out * shared_output, axis=-1, keepdims=True)
        * shared_gate_matrix
        * (1.0 - shared_gate_matrix)
    )
    gate_vector_grad = jnp.dot(
        logit_grad[:, 0], feedforward_normed_input, preferred_element_type=floats
    )
    ffn_grad = shared_input_part + logit_grad * shared_gate_weight.astype(floats)[None, :]
    ffn_grad = ffn_grad + back_rows[slot].astype(floats).reshape(tok_count, topk, width).sum(axis=1)
    unit_grad_two = ffn_grad * gain_two
    gain_ffn_grad = jnp.sum(ffn_grad * unit_ffn, axis=0)
    mid_grad = grad_out + stat_ffn * (
        unit_grad_two - unit_ffn * jnp.mean(unit_grad_two * unit_ffn, axis=-1, keepdims=True)
    )
    mid_low = mid_grad.astype(halves)
    out_weight_term = jnp.dot(attention_result.T, mid_low, preferred_element_type=floats)
    attended_grad = jnp.dot(mid_low, output_weight.T, preferred_element_type=floats).astype(halves)
    grad_groups = attended_grad.reshape(tok_count, head_groups, group_heads, HEAD_DIM).transpose(
        1, 0, 2, 3
    )

    def attend_back(pieces):
        q_part, k_part, v_part, g_part, log_part = pieces
        scores = jnp.einsum("qhd,khd->hqk", q_part, k_part, preferred_element_type=floats)
        scores = jnp.where(visible[None], scores, neg_fill)
        probs = jnp.exp(scores - log_part)
        prob_grad = jnp.einsum("qhd,khd->hqk", g_part, v_part, preferred_element_type=floats)
        delta = jnp.sum(probs * prob_grad, axis=-1, keepdims=True)
        score_grad = (probs * (prob_grad - delta)).astype(halves)
        q_grad = jnp.einsum("hqk,khd->qhd", score_grad, k_part, preferred_element_type=floats)
        k_grad = jnp.einsum("hqk,qhd->khd", score_grad, q_part, preferred_element_type=floats)
        v_grad = jnp.einsum(
            "hqk,qhd->khd", probs.astype(halves), g_part, preferred_element_type=floats
        )
        return (q_grad, k_grad, v_grad)

    query_grads, key_grads, value_grads = lax.map(
        attend_back, (query_groups, key_all, value_all, grad_groups, log_totals)
    )
    key_grad, value_grad = (
        lax.psum_scatter(key_grads, ("expert", "context"), scatter_dimension=1, tiled=True),
        lax.psum_scatter(value_grads, ("expert", "context"), scatter_dimension=1, tiled=True),
    )
    query_grad = query_grads.transpose(1, 0, 2, 3).reshape(tok_count, HEADS, HEAD_DIM)
    key_grad = key_grad.transpose(1, 0, 2, 3).reshape(tok_count, HEADS, HEAD_DIM)
    value_grad = value_grad.transpose(1, 0, 2, 3).reshape(tok_count, width)
    proj_grad = jnp.concatenate(
        [
            rotate_back(query_grad * scale, cosine, sine).reshape(tok_count, width),
            rotate_back(key_grad, cosine, sine).reshape(tok_count, width),
            value_grad,
        ],
        axis=-1,
    ).astype(halves)
    bias_term = jnp.sum(proj_grad.astype(floats), axis=0)
    qkv_weight_term = jnp.dot(attention_normed_input.T, proj_grad, preferred_element_type=floats)
    attn_in_grad = jnp.dot(proj_grad, query_key_value_weight.T, preferred_element_type=floats)
    unit_grad_one = attn_in_grad * gain_one
    gain_attn_grad = jnp.sum(attn_in_grad * unit_attn, axis=0)
    input_grad = mid_grad + stat_attn * (
        unit_grad_one - unit_attn * jnp.mean(unit_grad_one * unit_attn, axis=-1, keepdims=True)
    )
    qkv_out, bias_out, out_weight_out, gain_attn_out, gain_ffn_out, gate_vector_out = (
        lax.psum_scatter(
            qkv_weight_term, ("expert", "context", "dp"), scatter_dimension=0, tiled=True
        ),
        lax.psum_scatter(bias_term, ("expert", "context", "dp"), scatter_dimension=0, tiled=True),
        lax.psum_scatter(
            out_weight_term, ("expert", "context", "dp"), scatter_dimension=0, tiled=True
        ),
        lax.psum_scatter(
            gain_attn_grad, ("expert", "context", "dp"), scatter_dimension=0, tiled=True
        ),
        lax.psum_scatter(
            gain_ffn_grad, ("expert", "context", "dp"), scatter_dimension=0, tiled=True
        ),
        lax.psum_scatter(
            gate_vector_grad, ("expert", "context", "dp"), scatter_dimension=0, tiled=True
        ),
    )
    return (
        layer_sum.astype(halves)[None],
        input_grad[None],
        qkv_out,
        bias_out,
        out_weight_out,
        gain_attn_out,
        gain_ffn_out,
        shared_up_out,
        shared_down_out,
        gate_vector_out,
        expert_up_out,
        expert_down_out,
    )


def solution(mesh):
    placed = (
        P("dp", ("expert", "context"), None),
        P("dp", ("expert", "context"), None),
        P("dp", None),
        P("dp", ("expert", "context"), None),
        P("dp", ("expert", "context"), None),
        P("dp", ("expert", "context"), None),
        P(("expert", "context", "dp"), None),
        P(("expert", "context", "dp")),
        P(("expert", "context", "dp"), None),
        P(("expert", "context", "dp")),
        P(("expert", "context", "dp")),
        P(None, ("context", "dp"), "expert"),
        P("expert", ("context", "dp")),
        P(("expert", "context", "dp")),
        P("expert", ("context", "dp"), None),
        P("expert", ("context", "dp"), None),
    )
    return jax.shard_map(
        shards,
        mesh=mesh,
        in_specs=placed,
        out_specs=(
            P("dp", ("expert", "context"), None),
            P("dp", ("expert", "context"), None),
            P(("expert", "context", "dp"), None),
            P(("expert", "context", "dp")),
            P(("expert", "context", "dp"), None),
            P(("expert", "context", "dp")),
            P(("expert", "context", "dp")),
            P(None, ("context", "dp"), "expert"),
            P("expert", ("context", "dp")),
            P(("expert", "context", "dp")),
            P("expert", ("context", "dp"), None),
            P("expert", ("context", "dp"), None),
        ),
        check_vma=False,
    )
```

profile of v0, /device:TPU:0, one launch (start us, length us, event | category | flops | bytes accessed | tf_op | source)
XLA Modules:
  0.0 5805.6 jit_solution(12367953564058434864)
XLA Ops:
  10.5 43.5 all-reduce.11
  54.3 115.4 %all-gather.11.cloned.1.call-done = bf16[2048,6144]{1,0:T(8,128)(2,1)} async-done(((bf16[64,6144]{1,0:T(8,128)(2,1)}), bf16[2048,6144]{1,0:T(8,128)(2,1)}) %all-gather.11.cloned.1.call-update) | async-done | bytes 25165840 | tf_op jit(solution)/shard_map/all_gather | solution.py:115
  189.8 47.6 all-gather.19.cloned.1.call-done
  237.5 46.2 all-gather.23.cloned.1.call-done
  288.1 44.8 all-gather.13.cloned.1.call-done
  332.9 47.9 all-gather.15.cloned.1.call-done
  380.9 21.1 while.30
  402.0 57.8 all-gather.17.cloned.1.call-done
  465.7 762.0 %all-gather.21.cloned.1.call-done = bf16[2,2048,5632]{2,1,0:T(8,128)(2,1)} async-done(((bf16[2,2048,1408]{2,1,0:T(8,128)(2,1)}), bf16[2,2048,5632]{2,1,0:T(8,128)(2,1)}) %all-gather.21.cloned.1.call-update) | async-done | bytes 46137360 | tf_op jit(solution)/shard_map/all_gather | solution.py:200
  1227.7 24.0 convolution_bitcast_fusion.5
  1251.7 366.9 %all-gather.25.cloned.1.call-done = bf16[5632,2048]{1,0:T(8,128)(2,1)} async-done(((bf16[1408,2048]{1,0:T(8,128)(2,1)}), bf16[5632,2048]{1,0:T(8,128)(2,1)}) %all-gather.25.cloned.1.call-update) | async-done | bytes 23068688 | tf_op jit(solution)/shard_map/all_gather | solution.py:201
  1648.8 35.6 convolution_bitcast_fusion.2
  1711.0 41.4 all-to-all-done
  1773.0 36.6 all-to-all-done.2
  1853.5 108.0 %all-to-all-done.3 = bf16[4,2,72,2048]{3,2,1,0:T(8,128)(2,1)S(1)} async-done(((bf16[4,2,72,2048]{3,2,1,0:T(8,128)(2,1)}), bf16[4,2,72,2048]{3,2,1,0:T(8,128)(2,1)S(1)}, u32[]{:S(2)}, u32[]{:S(2)}) %all-to-all-start.3) | async-done | bytes 2359328 | tf_op jit(solution)/shard_map/all_to_all | solution.py:268
  1976.6 105.8 %all-to-all-done.1 = bf16[4,2,72,2048]{3,2,1,0:T(8,128)(2,1)} async-done(((bf16[4,2,72,2048]{3,2,1,0:T(8,128)(2,1)}), bf16[4,2,72,2048]{3,2,1,0:T(8,128)(2,1)}, u32[]{:S(2)}, u32[]{:S(2)}) %all-to-all-start.1) | async-done | bytes 2359328 | tf_op jit(solution)/shard_map/all_to_all | solution.py:267
  2104.9 22.9 multiply_reduce_fusion.2
  2137.9 44.1 while.31
  2182.8 21.7 fusion.90
  2204.6 1187.7 %reduce-scatter.19.cloned.1.call-done = f32[2,2048,1408]{1,2,0:T(8,128)} async-done(((f32[2,2048,5632]{1,2,0:T(8,128)}), f32[2,2048,1408]{1,2,0:T(8,128)}) %reduce-scatter.19.cloned.1.call-update) | async-done | bytes 23068688 | tf_op jit(solution)/shard_map/reduce_scatter | solution.py:207
  3414.4 23.6 convolution_bitcast_fusion.3
  3442.3 49.6 reduce-scatter.11.cloned.1.call-done
  3507.4 74.9 %reduce-scatter.13.cloned.1.call-done = f32[4,128,4,128]{1,3,2,0:T(8,128)} async-done(((f32[4,1024,4,128]{1,3,2,0:T(8,128)}), f32[4,128,4,128]{1,3,2,0:T(8,128)}) %reduce-scatter.13.cloned.1.call-update) | async-done | bytes 1048592 | tf_op jit(solution)/shard_map/reduce_scatter | solution.py:324
  3583.7 21.6 fusion.121
  3605.7 730.9 %reduce-scatter.23.cloned.1.call-done = f32[1408,2048]{1,0:T(8,128)} async-done(((f32[5632,2048]{1,0:T(8,128)}), f32[1408,2048]{1,0:T(8,128)}) %reduce-scatter.23.cloned.1.call-update) | async-done | bytes 11534352 | tf_op jit(solution)/shard_map/reduce_scatter | solution.py:208
  4353.3 43.2 all-reduce.10
  4401.5 86.8 %reduce-scatter.21.cloned.1.call-done = f32[2,256,1408]{1,2,0:T(8,128)} async-done(((f32[2,2048,1408]{1,2,0:T(8,128)}), f32[2,256,1408]{1,2,0:T(8,128)}) %reduce-scatter.21.cloned.1.call-update) | async-done | bytes 2883600 | tf_op jit(solution)/shard_map/reduce_scatter | solution.py:211
  4491.7 146.6 %reduce-scatter.29.cloned.1.call-done = f32[2,176,2048]{2,1,0:T(8,128)} async-done(((f32[2,1408,2048]{2,1,0:T(8,128)}), f32[2,176,2048]{2,1,0:T(8,128)}) %reduce-scatter.29.cloned.1.call-update) | async-done | bytes 2883600 | tf_op jit(solution)/shard_map/reduce_scatter | solution.py:264
  4638.3 360.3 %reduce-scatter.17.cloned.1.call-done = f32[64,2048]{1,0:T(8,128)} async-done(((f32[2048,2048]{1,0:T(8,128)}), f32[64,2048]{1,0:T(8,128)}) %reduce-scatter.17.cloned.1.call-update) | async-done | bytes 524304 | tf_op jit(solution)/shard_map/reduce_scatter | solution.py:350
  4998.6 269.9 %reduce-scatter.27.cloned.1.call-done = f32[2,256,2816]{2,1,0:T(8,128)} async-done(((f32[2,2048,2816]{2,1,0:T(8,128)}), f32[2,256,2816]{2,1,0:T(8,128)}) %reduce-scatter.27.cloned.1.call-update) | async-done | bytes 5767184 | tf_op jit(solution)/shard_map/reduce_scatter | solution.py:263
  5268.5 439.6 %reduce-scatter.15.cloned.1.call-done = f32[64,6144]{1,0:T(8,128)} async-done(((f32[2048,6144]{1,0:T(8,128)}), f32[64,6144]{1,0:T(8,128)}) %reduce-scatter.15.cloned.1.call-update) | async-done | bytes 1572880 | tf_op jit(solution)/shard_map/reduce_scatter | solution.py:346
  5708.1 90.1 %reduce-scatter.25.cloned.1.call-done = f32[1408,256]{1,0:T(8,128)} async-done(((f32[1408,2048]{1,0:T(8,128)}), f32[1408,256]{1,0:T(8,128)}) %reduce-scatter.25.cloned.1.call-update) | async-done | bytes 1441808 | tf_op jit(solution)/shard_map/reduce_scatter | solution.py:212
  (322 shorter events, 336.8 us)
Async XLA Ops:
  7.2 162.4 %all-gather.11.cloned.1.call-start = ((), (), s32[]{:S(2)}) async-start(), calls=%async_computation.14 | async-start | bytes 25952256 | tf_op jit(solution)/shard_map/all_gather | solution.py:115
  8.0 229.5 %all-gather.19.cloned.1.call-start = ((), (), s32[]{:S(2)}) async-start(), calls=%async_computation.18 | async-start | bytes 12976128 | tf_op jit(solution)/shard_map/all_gather | solution.py:123
  8.7 275.0 %all-gather.23.cloned.1.call-start = ((), (), s32[]{:S(2)}) async-start(), calls=%async_computation.20 | async-start | bytes 6488064 | tf_op jit(solution)/shard_map/all_gather | solution.py:124
  9.4 323.5 %all-gather.13.cloned.1.call-start = ((), (), s32[]{:S(2)}) async-start(), calls=%async_computation.15 | async-start | bytes 4718592 | tf_op jit(solution)/shard_map/all_gather | solution.py:163
  54.0 231.7 %copy-start.39 = (bf16[2048]{0:T(1024)(128)(2,1)}, bf16[2048]{0:T(1024)(128)(2,1)S(1)}, u32[]{:S(2)}) copy-start(bf16[2048]{0:T(1024)(128)(2,1)S(1)} %get-tuple-element.298) | copy-start | bytes 12292
  54.1 126.5 %copy-start.26 = (f32[2048]{0:T(1024)}, f32[2048]{0:T(1024)S(1)}, u32[]{:S(2)}) copy-start(f32[2048]{0:T(1024)S(1)} %convert_element_type.146) | copy-start | bytes 24580
  54.3 126.3 %copy-start.37 = (f32[128]{0:T(128)}, f32[128]{0:T(128)S(1)}, u32[]{:S(2)}) copy-start(f32[128]{0:T(128)S(1)} %add_rsqrt_fusion.1) | copy-start | bytes 1540
  183.6 197.2 %all-gather.15.cloned.1.call-start = ((), (), s32[]{:S(2)}) async-start(), calls=%async_computation.16 | async-start | bytes 4718592 | tf_op jit(solution)/shard_map/all_gather | solution.py:162
  189.2 270.6 %all-gather.17.cloned.1.call-start = ((), (), s32[]{:S(2)}) async-start(), calls=%async_computation.17 | async-start | bytes 8650752 | tf_op jit(solution)/shard_map/all_gather | solution.py:117
  189.8 1038.0 %all-gather.21.cloned.1.call-start = ((), (), s32[]{:S(2)}) async-start(), calls=%async_computation.19 | async-start | bytes 57671680 | tf_op jit(solution)/shard_map/all_gather | solution.py:200
  237.5 1381.2 %all-gather.25.cloned.1.call-start = ((), (), s32[]{:S(2)}) async-start(), calls=%async_computation.21 | async-start | bytes 28835840 | tf_op jit(solution)/shard_map/all_gather | solution.py:201
  283.8 1472.5 %all-gather.27.cloned.1.call-start = ((), (), s32[]{:S(2)}) async-start(), calls=%async_computation.22 | async-start | bytes 25952256 | tf_op jit(solution)/shard_map/all_gather | solution.py:127
  284.5 1525.1 %all-gather.29.cloned.1.call-start = ((), (), s32[]{:S(2)}) async-start(), calls=%async_computation.23 | async-start | bytes 12976128 | tf_op jit(solution)/shard_map/all_gather | solution.py:128
  285.1 3107.1 %reduce-scatter.19.cloned.1.call-start = ((), (), s32[]{:S(2)}) async-start(), calls=%async_computation.28 | async-start | bytes 115343360 | tf_op jit(solution)/shard_map/reduce_scatter | solution.py:207
  285.7 178.9 %copy-start.30 = (f32[2048]{0:T(1024)}, f32[2048]{0:T(1024)S(1)}, u32[]{:S(2)}) copy-start(f32[2048]{0:T(1024)S(1)} %convert_element_type.156) | copy-start | bytes 24580
  464.6 787.1 %copy-start.45 = (f32[128]{0:T(128)}, f32[128]{0:T(128)S(1)}, u32[]{:S(2)}) copy-start(f32[128]{0:T(128)S(1)} %add_rsqrt_fusion) | copy-start | bytes 1540
  465.7 1222.8 %copy-start = (bf16[128,2048]{1,0:T(8,128)(2,1)}, bf16[128,2048]{1,0:T(8,128)(2,1)S(1)}, u32[]{:S(2)}) copy-start(bf16[128,2048]{1,0:T(8,128)(2,1)S(1)} %multiply_convert_fusion.8) | copy-start | bytes 1572868
  465.7 1152.9 %copy-start.16 = (bf16[1,128,2048]{2,1,0:T(8,128)(2,1)S(1)}, bf16[1,128,2048]{2,1,0:T(8,128)(2,1)}, u32[]{:S(2)}) copy-start(bf16[1,128,2048]{2,1,0:T(8,128)(2,1)} %param.21) | copy-start | bytes 1572868
  1693.5 58.9 %all-to-all-start = ((bf16[4,2,72,2048]{3,2,1,0:T(8,128)(2,1)}), bf16[4,2,72,2048]{3,2,1,0:T(8,128)(2,1)}, u32[]{:S(2)}, u32[]{:S(2)}) async-start(bf16[4,2,72,2048]{3,2,1,0:T(8,128)(2,1)} %broadcast_select_fusion), calls=%async_computation | async-start | bytes 4718592 | tf_op jit(solution)/shard_map/all_to_all | solution.py:238
  1752.4 57.2 all-to-all-start.2
  1839.7 121.8 %all-to-all-start.3 = ((bf16[4,2,72,2048]{3,2,1,0:T(8,128)(2,1)}), bf16[4,2,72,2048]{3,2,1,0:T(8,128)(2,1)S(1)}, u32[]{:S(2)}, u32[]{:S(2)}) async-start(bf16[4,2,72,2048]{3,2,1,0:T(8,128)(2,1)} %copy.119), calls=%async_computation.3 | async-start | bytes 4718592 | tf_op jit(solution)/shard_map/all_to_all | solution.py:268
  1853.5 112.6 %copy-start.40 = (bf16[2048]{0:T(1024)(128)(2,1)S(1)}, bf16[2048]{0:T(1024)(128)(2,1)}, u32[]{:S(2)}) copy-start(bf16[2048]{0:T(1024)(128)(2,1)} %copy-done.39) | copy-start | bytes 12292
  1961.5 120.8 %all-to-all-start.1 = ((bf16[4,2,72,2048]{3,2,1,0:T(8,128)(2,1)}), bf16[4,2,72,2048]{3,2,1,0:T(8,128)(2,1)}, u32[]{:S(2)}, u32[]{:S(2)}) async-start(bf16[4,2,72,2048]{3,2,1,0:T(8,128)(2,1)} %copy.115), calls=%async_computation.1 | async-start | bytes 4718592 | tf_op jit(solution)/shard_map/all_to_all | solution.py:267
  1966.1 1525.9 %reduce-scatter.11.cloned.1.call-start = ((), (), s32[]{:S(2)}) async-start(), calls=%async_computation.24 | async-start | bytes 9437184 | tf_op jit(solution)/shard_map/reduce_scatter | solution.py:323
  2182.0 1400.3 %reduce-scatter.13.cloned.1.call-start = ((), (), s32[]{:S(2)}) async-start(), calls=%async_computation.25 | async-start | bytes 9437184 | tf_op jit(solution)/shard_map/reduce_scatter | solution.py:324
  2182.8 2153.8 %reduce-scatter.23.cloned.1.call-start = ((), (), s32[]{:S(2)}) async-start(), calls=%async_computation.30 | async-start | bytes 57671680 | tf_op jit(solution)/shard_map/reduce_scatter | solution.py:208
  2204.5 2283.8 %reduce-scatter.21.cloned.1.call-start = ((), (), s32[]{:S(2)}) async-start(), calls=%async_computation.29 | async-start | bytes 25952256 | tf_op jit(solution)/shard_map/reduce_scatter | solution.py:211
  3392.2 1246.1 %reduce-scatter.29.cloned.1.call-start = ((), (), s32[]{:S(2)}) async-start(), calls=%async_computation.33 | async-start | bytes 25952256 | tf_op jit(solution)/shard_map/reduce_scatter | solution.py:264
  3405.2 1593.4 %reduce-scatter.17.cloned.1.call-start = ((), (), s32[]{:S(2)}) async-start(), calls=%async_computation.27 | async-start | bytes 17301504 | tf_op jit(solution)/shard_map/reduce_scatter | solution.py:350
  3414.3 1854.2 %reduce-scatter.27.cloned.1.call-start = ((), (), s32[]{:S(2)}) async-start(), calls=%async_computation.32 | async-start | bytes 51904512 | tf_op jit(solution)/shard_map/reduce_scatter | solution.py:263
  3438.0 2270.1 %reduce-scatter.15.cloned.1.call-start = ((), (), s32[]{:S(2)}) async-start(), calls=%async_computation.26 | async-start | bytes 51904512 | tf_op jit(solution)/shard_map/reduce_scatter | solution.py:346
  3605.3 2192.9 %reduce-scatter.25.cloned.1.call-start = ((), (), s32[]{:S(2)}) async-start(), calls=%async_computation.31 | async-start | bytes 12976128 | tf_op jit(solution)/shard_map/reduce_scatter | solution.py:212
  (46 other events, 993.3 us)
Sparse Core Ops, SparseCore 0:
  10.9 158.6 all-gather.10
  171.5 65.8 all-gather.18
  239.3 44.3 all-gather.22
  285.8 47.1 all-gather.12
  335.0 45.8 all-gather.14
  383.6 76.1 all-gather.16
  461.4 766.3 all-gather.20
  1229.3 389.2 all-gather.24
  1620.5 114.7 all-gather.26
  1737.1 67.6 all-gather.28
  1807.2 1584.9 reduce-scatter.18
  3394.5 97.3 reduce-scatter.10
  3494.3 87.9 reduce-scatter.12
  3584.7 751.8 reduce-scatter.22
  4340.0 148.2 reduce-scatter.20
  4492.4 145.8 reduce-scatter.28
  4641.0 357.5 reduce-scatter.16
  5002.7 265.7 reduce-scatter.26
  5276.6 431.4 reduce-scatter.14
  5712.4 85.7 reduce-scatter.24
where the time goes:
time: 5810 us
  waiting for transfers between devices  5220 us (90%)
  matrix products  346 us (6%)
  blocking collectives  86.7 us (1%)
  local copies, waits for them, and re-layouts  73.4 us (1%)
    reduce_scatter x1, waiting for transfers between devices, shards(): lax.psum_scatter(up_term, 'expert', scatter_dimension=2, tiled=True)  1190 us
    all_gather x1, waiting for transfers between devices, shards(): lax.all_gather(up_local, 'expert', axis=2, tiled=True)  762 us
    reduce_scatter x1, waiting for transfers between devices, shards(): lax.psum_scatter(down_term, 'expert', scatter_dimension=0, tiled=True)  731 us
    reduce_scatter x1, waiting for transfers between devices, shards(): lax.psum_scatter(qkv_weight_term, ('expert', 'context', 'dp'), scatter_di...  440 us
    all_gather x1, waiting for transfers between devices, shards(): lax.all_gather(down_local, 'expert', axis=0, tiled=True)  367 us
    reduce_scatter x1, waiting for transfers between devices, shards(): lax.psum_scatter(out_weight_term, ('expert', 'context', 'dp'), scatter_di...  360 us
    reduce_scatter x1, waiting for transfers between devices, shards(): lax.psum_scatter(expert_up_term, ('context', 'dp'), scatter_dimension=1,...  270 us
    reduce_scatter x1, waiting for transfers between devices, shards(): lax.psum_scatter(expert_down_term, ('context', 'dp'), scatter_dimension=1...  147 us
  transfers between devices with their start and end apart: 24, of which 22 were waited for; matrix products, arithmetic and copies ran while one was open for 8% of the time, Pallas kernels for 0%

commit v1 on v0

v1 whole, which is shorter than its diff:
```python
import math

import jax
import jax.numpy as jnp
from jax import lax
from jax.sharding import PartitionSpec as P

HEADS = 16
HEAD_DIM = 128


eps_norm = 1e-06
neg_fill = -1e30
rope_base = 1000000.0
group_heads = 4
floats = jnp.float32
halves = jnp.bfloat16
every = ("expert", "context", "dp")
group = ("expert", "context")


def rope_tables(positions, half):
    inverse = jnp.exp(
        jnp.arange(half).astype(jnp.float32) * (-2.0 * math.log(rope_base) / (2 * half))
    )
    angle = positions.astype(jnp.float32)[:, None] * inverse[None, :]
    return (jnp.cos(angle), jnp.sin(angle))


def rotate(values, cosine, sine):
    half = values.shape[-1] // 2
    front = values[..., :half]
    behind = values[..., half:]
    cosine = cosine[:, None, :]
    sine = sine[:, None, :]
    return jnp.concatenate(
        [front * cosine - behind * sine, behind * cosine + front * sine], axis=-1
    )


def rotate_back(grads, cosine, sine):
    half = grads.shape[-1] // 2
    front = grads[..., :half]
    behind = grads[..., half:]
    cosine = cosine[:, None, :]
    sine = sine[:, None, :]
    return jnp.concatenate(
        [front * cosine + behind * sine, behind * cosine - front * sine], axis=-1
    )


def silu_parts(grad_hidden, gate_pre, up_pre):
    sigma = jax.nn.sigmoid(gate_pre)
    gate_grad = grad_hidden * up_pre * sigma * (1.0 + gate_pre * (1.0 - sigma))
    up_grad = grad_hidden * gate_pre * sigma
    return (gate_grad, up_grad)


def dot(left, right):
    return jnp.dot(left, right, preferred_element_type=floats)


def dot_tn(left, right):
    return lax.dot_general(left, right, (((0,), (0,)), ((), ())), preferred_element_type=floats)


def dot_nt(left, right):
    return lax.dot_general(left, right, (((1,), (1,)), ((), ())), preferred_element_type=floats)


def dp_step(value, step):
    count = lax.axis_size("dp")
    return lax.ppermute(value, "dp", [(i, i ^ step) for i in range(count)])


def other_core(value):
    return lax.ppermute(value, "context", [(0, 1), (1, 0)])


def gather_square(first, second):
    first_x, first_y = dp_step(first, 1), dp_step(first, 2)
    second_y, second_x = dp_step(second, 2), dp_step(second, 1)
    first_far, second_far = dp_step(first_x, 2), dp_step(second_y, 1)
    return [first, first_x, first_y, first_far], [second, second_x, second_y, second_far]


def reduce_square(first, second):
    first_far, first_near = dp_step(first[3], 1), dp_step(first[1], 1)
    second_far, second_near = dp_step(second[3], 2), dp_step(second[2], 2)
    first_pass = (first[2].astype(floats) + first_far.astype(floats)).astype(halves)
    second_pass = (second[1].astype(floats) + second_far.astype(floats)).astype(halves)
    first_last, second_last = dp_step(first_pass, 2), dp_step(second_pass, 1)
    first_sum = first[0].astype(floats) + first_near.astype(floats) + first_last.astype(floats)
    second_sum = second[0].astype(floats) + second_near.astype(floats) + second_last.astype(floats)
    return first_sum, second_sum


def gather_weight(kept, given):
    core = lax.axis_index("context")
    place = lax.axis_index("dp")
    taken = other_core(given)
    near, far = gather_square(kept, taken)
    out = jnp.zeros((2, 4) + kept.shape, kept.dtype)
    zeros = (0,) * kept.ndim
    for step in range(4):
        out = lax.dynamic_update_slice(out, near[step][None, None], (core, place ^ step) + zeros)
        out = lax.dynamic_update_slice(out, far[step][None, None], (1 - core, place ^ step) + zeros)
    return out


def line_gather(block):
    count = lax.axis_size("expert")
    if count != 4:
        return lax.all_gather(block, "expert", axis=0)
    here = lax.axis_index("expert")
    lower = lax.ppermute(block, "expert", [(0, 1), (1, 2), (2, 3)])
    upper = lax.ppermute(block, "expert", [(1, 0), (2, 1), (3, 2)])
    second = lax.ppermute(block, "expert", [(0, 2), (1, 3), (2, 0), (3, 1)])
    third = lax.ppermute(second, "expert", [(2, 3), (1, 0)])
    table = (
        (block, upper, second, third),
        (lower, block, upper, second),
        (second, lower, block, upper),
        (third, second, lower, block),
    )
    rows = []
    for slot in range(4):
        pick = table[3][slot]
        for at in (2, 1, 0):
            pick = jnp.where(here == at, table[at][slot], pick)
        rows.append(pick)
    return jnp.stack(rows)


def group_gather(block):
    if lax.axis_size("expert") != 4:
        return lax.all_gather(block, group, axis=0, tiled=True)
    core = lax.axis_index("context")
    mine = line_gather(block)
    other = other_core(mine)
    both = jnp.stack([jnp.where(core == 0, mine, other), jnp.where(core == 0, other, mine)], axis=1)
    return both.reshape((-1,) + block.shape[1:])


def group_reduce(part):
    count = lax.axis_size("expert")
    if count != 4:
        return lax.psum_scatter(part, group, scatter_dimension=0, tiled=True)
    core = lax.axis_index("context")
    here = lax.axis_index("expert")
    width = part.shape[1]
    view = part.reshape(count, 2, -1, width)
    mine = lax.dynamic_index_in_dim(view, core, 1, keepdims=False)
    other = lax.dynamic_index_in_dim(view, 1 - core, 1, keepdims=False).astype(halves)
    rows = (mine + other_core(other).astype(floats)).astype(halves)

    def of(place):
        return lax.dynamic_index_in_dim(rows, jnp.clip(place, 0, 3), 0, keepdims=False)

    corner = lax.ppermute(of(jnp.where(here == 3, 0, 3)), "expert", [(3, 2), (0, 1)])
    lower = lax.ppermute(of(here + 1), "expert", [(0, 1), (1, 2), (2, 3)])
    upper = lax.ppermute(of(here - 1), "expert", [(1, 0), (2, 1), (3, 2)])
    passed = (of(here ^ 2).astype(floats) + corner.astype(floats)).astype(halves)
    second = lax.ppermute(passed, "expert", [(0, 2), (1, 3), (2, 0), (3, 1)])
    return (
        of(here).astype(floats)
        + lower.astype(floats)
        + upper.astype(floats)
        + second.astype(floats)
    )


def spread(values):
    count = lax.axis_size(every)
    padded = jnp.broadcast_to(values.reshape(1, -1, 128), (count, values.shape[0] // 128, 128))
    got = lax.all_to_all(padded, every, split_axis=0, concat_axis=0, tiled=True)
    return got.reshape(count, -1)


def head_weights(qkv_weight, out_weight):
    count = lax.axis_size(group)
    place = lax.axis_index("dp")
    rows, wide = qkv_weight.shape
    width = wide // 3
    piece = width // count
    cut = qkv_weight.reshape(rows, 3, count, piece).transpose(2, 0, 1, 3).reshape(count, rows, 3 * piece)
    cut = lax.all_to_all(cut, group, split_axis=0, concat_axis=0, tiled=True)
    half = count // 2
    first, second = gather_square(cut[:half], cut[half:])
    weight = jnp.zeros((count, 4, rows, 3 * piece), halves)
    half_rows = rows // 2
    first_out, second_out = gather_square(out_weight[:half_rows], out_weight[half_rows:])
    out = jnp.zeros((4, 2, half_rows, width), halves)
    for step in range(4):
        at = place ^ step
        weight = lax.dynamic_update_slice(weight, first[step][:, None], (0, at, 0, 0))
        weight = lax.dynamic_update_slice(weight, second[step][:, None], (half, at, 0, 0))
        out = lax.dynamic_update_slice(out, first_out[step][None, None], (at, 0, 0, 0))
        out = lax.dynamic_update_slice(out, second_out[step][None, None], (at, 1, 0, 0))
    return weight.reshape(width, 3 * piece), out.reshape(piece, width)


def heads_forward(all_tokens, gain, bias, weights, seq_ids):
    weight, out_rows = weights
    count = lax.axis_size(group)
    index = lax.axis_index(group)
    length, width = all_tokens.shape
    piece = width // count
    heads = piece // HEAD_DIM
    scale = 1.0 / math.sqrt(HEAD_DIM)
    tokens = all_tokens.astype(floats)
    stat = lax.rsqrt(jnp.mean(tokens * tokens, axis=-1, keepdims=True) + eps_norm)
    unit = tokens * stat
    normed = (unit * gain).astype(halves)
    own_bias = lax.dynamic_index_in_dim(bias.reshape(3, count, piece), index, 1, keepdims=False)
    projected = dot(normed, weight) + own_bias.reshape(1, 3 * piece)
    positions = jnp.arange(length, dtype=jnp.int32)
    cosine, sine = rope_tables(positions, HEAD_DIM // 2)
    raw = projected.reshape(length, 3, heads, HEAD_DIM)
    query = (rotate(raw[:, 0], cosine, sine) * scale).astype(halves)
    key = rotate(raw[:, 1], cosine, sine).astype(halves)
    value = raw[:, 2].astype(halves)
    visible = (positions[None, :] <= positions[:, None]) & (seq_ids[None, :] == seq_ids[:, None])
    scores = jnp.einsum("qhd,khd->hqk", query, key, preferred_element_type=floats)
    scores = jnp.where(visible[None], scores, neg_fill)
    top = jnp.max(scores, axis=-1, keepdims=True)
    grown = jnp.exp(scores - top)
    probs = grown / jnp.sum(grown, axis=-1, keepdims=True)
    attended = jnp.einsum("hqk,khd->qhd", probs.astype(halves), value, preferred_element_type=floats)
    attended = attended.reshape(length, piece).astype(halves)
    mixed = group_reduce(dot(attended, out_rows))
    return mixed, (normed, query, key, value, probs, attended, cosine, sine)


def heads_backward(all_tokens, gain, weights, saved, mid_low):
    weight, out_rows = weights
    normed, query, key, value, probs, attended, cosine, sine = saved
    count = lax.axis_size(group)
    index = lax.axis_index(group)
    place = lax.axis_index("dp")
    length, width = all_tokens.shape
    piece = width // count
    heads = piece // HEAD_DIM
    scale = 1.0 / math.sqrt(HEAD_DIM)
    all_mid = group_gather(mid_low)
    attended_grad = dot_nt(all_mid, out_rows).astype(halves).reshape(length, heads, HEAD_DIM)
    prob_grad = jnp.einsum("qhd,khd->hqk", attended_grad, value, preferred_element_type=floats)
    delta = jnp.sum(probs * prob_grad, axis=-1, keepdims=True)
    score_grad = (probs * (prob_grad - delta)).astype(halves)
    query_grad = jnp.einsum("hqk,khd->qhd", score_grad, key, preferred_element_type=floats)
    key_grad = jnp.einsum("hqk,qhd->khd", score_grad, query, preferred_element_type=floats)
    value_grad = jnp.einsum(
        "hqk,qhd->khd", probs.astype(halves), attended_grad, preferred_element_type=floats
    )
    proj_grad = jnp.concatenate(
        [
            rotate_back(query_grad * scale, cosine, sine).reshape(length, piece),
            rotate_back(key_grad, cosine, sine).reshape(length, piece),
            value_grad.reshape(length, piece),
        ],
        axis=-1,
    ).astype(halves)
    weight_part = dot_tn(normed, proj_grad).astype(halves)
    in_part = dot_nt(proj_grad, weight)
    tokens = all_tokens.astype(floats)
    stat = lax.rsqrt(jnp.mean(tokens * tokens, axis=-1, keepdims=True) + eps_norm)
    gain_part = jnp.sum(in_part * (tokens * stat), axis=0)
    bias_part = lax.dynamic_update_slice(
        jnp.zeros((3, count, piece), floats),
        jnp.sum(proj_grad.astype(floats), axis=0).reshape(3, 1, piece),
        (0, index, 0),
    ).reshape(-1)
    attn_in_grad = group_reduce(in_part)
    rows = width // (count * 4)
    half = count // 2
    cut = weight_part.reshape(count, 4, rows, 3 * piece)
    picks = [lax.dynamic_index_in_dim(cut, place ^ step, 1, keepdims=False) for step in range(4)]
    first, second = reduce_square([pick[:half] for pick in picks], [pick[half:] for pick in picks])
    total = jnp.concatenate([first, second]).astype(halves)
    total = lax.all_to_all(total, group, split_axis=0, concat_axis=0, tiled=True)
    qkv_out = (
        total.reshape(count, rows, 3, piece).transpose(1, 2, 0, 3).reshape(rows, 3 * width).astype(floats)
    )
    out_part = dot_tn(attended, all_mid).astype(halves).reshape(4, rows, width)
    picks = [lax.dynamic_index_in_dim(out_part, place ^ step, 0, keepdims=False) for step in range(4)]
    first, second = reduce_square(
        [pick[: rows // 2] for pick in picks], [pick[rows // 2 :] for pick in picks]
    )
    return attn_in_grad, gain_part, bias_part, qkv_out, jnp.concatenate([first, second])


def rows_weights(qkv_weight, out_weight):
    return (
        lax.all_gather(qkv_weight, every, axis=0, tiled=True),
        lax.all_gather(out_weight, every, axis=0, tiled=True),
    )


def rows_forward(own_tokens, gain, bias, weights, seq_ids):
    weight, out_weight = weights
    tok_count, width = own_tokens.shape
    seq_len = seq_ids.shape[0]
    head_groups = HEADS // group_heads
    block_place = lax.axis_index(group)
    positions = block_place * tok_count + jnp.arange(tok_count, dtype=jnp.int32)
    cosine, sine = rope_tables(positions, HEAD_DIM // 2)
    scale = 1.0 / math.sqrt(HEAD_DIM)
    tokens = own_tokens.astype(floats)
    stat = lax.rsqrt(jnp.mean(tokens * tokens, axis=-1, keepdims=True) + eps_norm)
    unit = tokens * stat
    normed = (unit * gain).astype(halves)
    projected = dot(normed, weight) + bias
    raw = projected.reshape(tok_count, 3, HEADS, HEAD_DIM)
    query = (rotate(raw[:, 0], cosine, sine) * scale).astype(halves)
    key = rotate(raw[:, 1], cosine, sine).astype(halves)
    value = raw[:, 2].astype(halves)

    def by_group(array):
        return array.reshape(tok_count, head_groups, group_heads, HEAD_DIM).transpose(1, 0, 2, 3)

    query_groups = by_group(query)
    key_all = lax.all_gather(by_group(key), group, axis=1, tiled=True)
    value_all = lax.all_gather(by_group(value), group, axis=1, tiled=True)
    query_ids = lax.dynamic_slice_in_dim(seq_ids, block_place * tok_count, tok_count)
    key_places = jnp.arange(seq_len, dtype=jnp.int32)
    visible = (key_places[None, :] <= positions[:, None]) & (seq_ids[None, :] == query_ids[:, None])

    def attend_group(pieces):
        q_part, k_part, v_part = pieces
        scores = jnp.einsum("qhd,khd->hqk", q_part, k_part, preferred_element_type=floats)
        scores = jnp.where(visible[None], scores, neg_fill)
        top_score = jnp.max(scores, axis=-1, keepdims=True)
        grown = jnp.exp(scores - top_score)
        total = jnp.sum(grown, axis=-1, keepdims=True)
        probs_low = (grown / total).astype(halves)
        mixed = jnp.einsum("hqk,khd->qhd", probs_low, v_part, preferred_element_type=floats)
        return (mixed, top_score + jnp.log(total))

    mixed_groups, log_totals = lax.map(attend_group, (query_groups, key_all, value_all))
    attended = mixed_groups.transpose(1, 0, 2, 3).reshape(tok_count, width).astype(halves)
    saved = (normed, unit, query_groups, key_all, value_all, log_totals, attended, cosine, sine, visible)
    return dot(attended, out_weight), saved


def rows_backward(weights, saved, mid_low):
    weight, out_weight = weights
    normed, unit, query_groups, key_all, value_all, log_totals, attended, cosine, sine, visible = saved
    tok_count, width = mid_low.shape
    head_groups = HEADS // group_heads
    scale = 1.0 / math.sqrt(HEAD_DIM)
    attended_grad = dot_nt(mid_low, out_weight).astype(halves)
    grad_groups = attended_grad.reshape(tok_count, head_groups, group_heads, HEAD_DIM).transpose(
        1, 0, 2, 3
    )

    def attend_back(pieces):
        q_part, k_part, v_part, g_part, log_part = pieces
        scores = jnp.einsum("qhd,khd->hqk", q_part, k_part, preferred_element_type=floats)
        scores = jnp.where(visible[None], scores, neg_fill)
        probs = jnp.exp(scores - log_part)
        prob_grad = jnp.einsum("qhd,khd->hqk", g_part, v_part, preferred_element_type=floats)
        delta = jnp.sum(probs * prob_grad, axis=-1, keepdims=True)
        score_grad = (probs * (prob_grad - delta)).astype(halves)
        q_grad = jnp.einsum("hqk,khd->qhd", score_grad, k_part, preferred_element_type=floats)
        k_grad = jnp.einsum("hqk,qhd->khd", score_grad, q_part, preferred_element_type=floats)
        v_grad = jnp.einsum(
            "hqk,qhd->khd", probs.astype(halves), g_part, preferred_element_type=floats
        )
        return (q_grad, k_grad, v_grad)

    query_grads, key_grads, value_grads = lax.map(
        attend_back, (query_groups, key_all, value_all, grad_groups, log_totals)
    )
    key_grad = lax.psum_scatter(key_grads, group, scatter_dimension=1, tiled=True)
    value_grad = lax.psum_scatter(value_grads, group, scatter_dimension=1, tiled=True)

    def by_head(array):
        return array.transpose(1, 0, 2, 3).reshape(tok_count, HEADS, HEAD_DIM)

    proj_grad = jnp.concatenate(
        [
            rotate_back(by_head(query_grads) * scale, cosine, sine).reshape(tok_count, width),
            rotate_back(by_head(key_grad), cosine, sine).reshape(tok_count, width),
            by_head(value_grad).reshape(tok_count, width),
        ],
        axis=-1,
    ).astype(halves)
    bias_part = jnp.sum(proj_grad.astype(floats), axis=0)
    attn_in_grad = dot_nt(proj_grad, weight)
    gain_part = jnp.sum(attn_in_grad * unit, axis=0)
    qkv_out = lax.psum_scatter(dot_tn(normed, proj_grad), every, scatter_dimension=0, tiled=True)
    out_out = lax.psum_scatter(dot_tn(attended, mid_low), every, scatter_dimension=0, tiled=True)
    return attn_in_grad, gain_part, bias_part, qkv_out, out_out


def shards(
    tokens,
    cotangent,
    segments,
    expert_ids,
    slot_order,
    gate_weights,
    qkv_weight,
    qkv_bias,
    out_weight,
    norm_attn,
    norm_ffn,
    shared_gate_up,
    shared_down,
    shared_gate,
    expert_gate_up,
    expert_down,
):
    count = lax.axis_size(group)
    devices = lax.axis_size(every)
    core = lax.axis_index("context")
    place = lax.axis_index("dp")
    index = lax.axis_index(group)
    tok_count, width = tokens.shape[1:]
    topk = expert_ids.shape[2]
    pairs = tok_count * topk
    experts = expert_gate_up.shape[0] * lax.axis_size("expert")
    capacity = (9 * pairs + 8 * experts - 1) // (8 * experts)
    length = count * tok_count
    by_heads = HEADS % count == 0

    vectors = [norm_attn, norm_ffn, shared_gate, qkv_bias]
    lengths = [vector.shape[0] for vector in vectors]
    routing = [expert_ids[0].reshape(pairs), slot_order[0, 0], gate_weights[0].reshape(pairs)]
    payload = jnp.concatenate([v.astype(floats) for v in vectors + routing])
    payload = jnp.pad(payload, (0, -payload.shape[0] % 128))
    small = spread(payload)
    at = 0
    gathered = []
    for size in lengths:
        gathered.append(small[:, at : at + size].reshape(-1))
        at += size
    gain_attn, gain_ffn, gate_vector, bias = gathered
    small_own = lax.dynamic_index_in_dim(
        small.reshape(count, devices // count, -1), place, 1, keepdims=False
    )
    routes = [small_own[:, at + i * pairs : at + (i + 1) * pairs] for i in range(3)]
    pair_expert, pair_order, pair_gate = [r.reshape(count, tok_count, topk) for r in routes]

    own_tokens = tokens[0]
    resid_in = own_tokens.astype(floats)
    if by_heads:
        weights = head_weights(qkv_weight, out_weight)
        all_tokens = group_gather(own_tokens)
        mixed, saved = heads_forward(all_tokens, gain_attn, bias, weights, segments[0])
    else:
        weights = rows_weights(qkv_weight, out_weight)
        mixed, saved = rows_forward(own_tokens, gain_attn, bias, weights, segments[0])

    def core_half(array, axis, which):
        size = array.shape[axis] // 2
        return lax.dynamic_slice_in_dim(array, which * size, size, axis)

    def expert_of(array, which):
        return lax.dynamic_index_in_dim(array, which, 0, keepdims=False)

    def gate_up_half(which):
        part = core_half(shared_gate_up, 2, which)
        return jnp.concatenate([part[0], part[1]], axis=-1)

    expert_up = gather_weight(expert_of(expert_gate_up, core), expert_of(expert_gate_up, 1 - core))
    expert_up = expert_up.reshape(width, -1)
    expert_dn = gather_weight(expert_of(expert_down, core), expert_of(expert_down, 1 - core))
    expert_dn = expert_dn.reshape(-1, width)
    ff_width = expert_dn.shape[0]
    shared_up = gather_weight(gate_up_half(core), gate_up_half(1 - core)).reshape(width, -1)
    down_turned = shared_down.T
    shared_dn = gather_weight(core_half(down_turned, 1, core), core_half(down_turned, 1, 1 - core))
    shared_dn = shared_dn.reshape(width, -1)
    hidden_units = shared_dn.shape[1]

    resid_mid = resid_in + mixed
    stat_ffn = lax.rsqrt(jnp.mean(resid_mid * resid_mid, axis=-1, keepdims=True) + eps_norm)
    unit_ffn = resid_mid * stat_ffn
    normed_ffn = (unit_ffn * gain_ffn).astype(halves)
    grad_out = cotangent[0].astype(floats)

    all_grads = group_gather(cotangent[0])
    all_normed = group_gather(normed_ffn)

    chosen = pair_expert == index.astype(floats)
    has_pair = jnp.any(chosen, axis=-1)
    order = jnp.sum(jnp.where(chosen, pair_order, 0.0), axis=-1)
    gate = jnp.sum(jnp.where(chosen, pair_gate, 0.0), axis=-1)
    earlier = has_pair[:, None, :] & (order[:, None, :] < order[:, :, None])
    rank = jnp.sum(earlier.astype(jnp.int32), axis=-1)
    kept = has_pair & (rank < capacity)
    gate = jnp.where(kept, gate, 0.0)
    slots = jnp.arange(capacity, dtype=jnp.int32)
    select = (rank[:, None, :] == slots[None, :, None]) & kept[:, None, :]
    slot_gate = jnp.sum(jnp.where(select, gate[:, None, :], 0.0), axis=-1).reshape(-1, 1)
    select = select.astype(halves)

    def to_slots(rows):
        got = jnp.einsum(
            "brt,btd->brd",
            select,
            rows.reshape(count, tok_count, width),
            preferred_element_type=floats,
        )
        return got.reshape(count * capacity, width)

    def from_slots(rows):
        got = jnp.einsum(
            "brt,brd->btd",
            select,
            rows.reshape(count, capacity, width),
            preferred_element_type=floats,
        )
        return got.reshape(length, width)

    slot_in = to_slots(all_normed).astype(halves)
    slot_grad = (to_slots(all_grads) * slot_gate).astype(halves)
    expert_pre = dot(slot_in, expert_up)
    expert_g, expert_u = expert_pre[:, :ff_width], expert_pre[:, ff_width:]
    expert_hidden = (jax.nn.silu(expert_g) * expert_u).astype(halves)
    hidden_grad = dot_nt(slot_grad, expert_dn)
    expert_pre_grad = jnp.concatenate(
        silu_parts(hidden_grad, expert_g, expert_u), axis=-1
    ).astype(halves)
    expert_out = dot(expert_hidden, expert_dn).astype(halves)
    slot_in_grad = dot_nt(expert_pre_grad, expert_up).astype(halves)

    shared_pre = dot(all_normed, shared_up)
    shared_g, shared_u = shared_pre[:, :hidden_units], shared_pre[:, hidden_units:]
    shared_hidden = (jax.nn.silu(shared_g) * shared_u).astype(halves)
    gate_shared = jax.nn.sigmoid(
        jnp.sum(all_normed.astype(floats) * gate_vector, axis=-1, keepdims=True)
    )
    shared_grad = (gate_shared * all_grads.astype(floats)).astype(halves)
    hidden_grad = dot(shared_grad, shared_dn)
    shared_pre_grad = jnp.concatenate(
        silu_parts(hidden_grad, shared_g, shared_u), axis=-1
    ).astype(halves)
    shared_part = dot_nt(shared_hidden, shared_dn)
    logit_part = jnp.sum(all_grads.astype(floats) * shared_part, axis=-1)

    ffn_part = dot_nt(shared_pre_grad, shared_up) + from_slots(slot_in_grad)
    out_part = gate_shared * shared_part + gate.reshape(length, 1) * from_slots(expert_out)

    logit_sums = lax.all_to_all(
        logit_part.reshape(count, 1, tok_count), group, split_axis=0, concat_axis=0, tiled=True
    )
    own_gate = jax.nn.sigmoid(
        jnp.sum(normed_ffn.astype(floats) * gate_vector, axis=-1, keepdims=True)
    )
    logit_grad = jnp.sum(logit_sums, axis=0).reshape(tok_count, 1) * own_gate * (1.0 - own_gate)
    ffn_grad = group_reduce(ffn_part) + logit_grad * gate_vector
    unit_grad = ffn_grad * gain_ffn
    gain_ffn_part = jnp.sum(ffn_grad * unit_ffn, axis=0)
    gate_vector_part = jnp.sum(logit_grad * normed_ffn.astype(floats), axis=0)
    mid_grad = grad_out + stat_ffn * (
        unit_grad - unit_ffn * jnp.mean(unit_grad * unit_ffn, axis=-1, keepdims=True)
    )
    mid_low = mid_grad.astype(halves)
    layer_sum = resid_mid + group_reduce(out_part)

    def block_of(array, crel, step):
        size = width // 8
        blk = (core ^ crel) * 4 + (place ^ step)
        return lax.dynamic_slice_in_dim(array, blk * size, size, 1)

    def reduce_blocks(block):
        near, far = reduce_square(
            [block(0, step) for step in range(4)], [block(1, step) for step in range(4)]
        )
        return near, other_core(far)

    def in_order(near, far, axis):
        return (
            jnp.where(core == 0, near, far),
            jnp.where(core == 0, far, near),
        )

    expert_down_term = dot_tn(expert_hidden, slot_grad).astype(halves)
    expert_down_term = expert_down_term.reshape(8, -1, width)
    expert_down_out = jnp.stack(
        in_order(
            *reduce_blocks(
                lambda crel, step: lax.dynamic_index_in_dim(
                    expert_down_term, (core ^ crel) * 4 + (place ^ step), 0, keepdims=False
                )
            ),
            0,
        )
    )
    expert_up_out = jnp.stack(
        in_order(
            *reduce_blocks(
                lambda crel, step: dot_tn(block_of(slot_in, crel, step), expert_pre_grad).astype(halves)
            ),
            0,
        )
    )
    lower, upper = in_order(
        *reduce_blocks(
            lambda crel, step: dot_tn(block_of(all_normed, crel, step), shared_pre_grad).astype(halves)
        ),
        0,
    )
    shared_up_out = jnp.concatenate(
        [array.reshape(width // 8, 2, hidden_units).transpose(1, 0, 2) for array in (lower, upper)],
        axis=-1,
    )
    lower, upper = in_order(
        *reduce_blocks(
            lambda crel, step: dot_tn(block_of(shared_grad, crel, step), shared_hidden).astype(halves)
        ),
        0,
    )
    shared_down_out = jnp.concatenate([lower, upper], axis=-1).T

    if by_heads:
        attn_in_grad, gain_attn_part, bias_part, qkv_out, out_weight_out = heads_backward(
            all_tokens, gain_attn, weights, saved, mid_low
        )
    else:
        attn_in_grad, gain_attn_part, bias_part, qkv_out, out_weight_out = rows_backward(
            weights, saved, mid_low
        )
    stat_attn = lax.rsqrt(jnp.mean(resid_in * resid_in, axis=-1, keepdims=True) + eps_norm)
    unit_attn = resid_in * stat_attn
    unit_grad = attn_in_grad * gain_attn
    input_grad = mid_grad + stat_attn * (
        unit_grad - unit_attn * jnp.mean(unit_grad * unit_attn, axis=-1, keepdims=True)
    )

    parts = [gain_attn_part, gain_ffn_part, gate_vector_part, bias_part]
    packed = jnp.concatenate([part.reshape(devices, -1) for part in parts], axis=1)
    total = packed.shape[1]
    packed = jnp.pad(packed, ((0, 0), (0, -total % 128)))
    packed = lax.all_to_all(
        packed.reshape(devices, -1, 128), every, split_axis=0, concat_axis=0, tiled=True
    )
    sums = jnp.sum(packed, axis=0).reshape(-1)
    at = 0
    small_out = []
    for size in lengths:
        small_out.append(sums[at : at + size])
        at += size
    gain_attn_out, gain_ffn_out, gate_vector_out, bias_out = small_out
    return (
        layer_sum.astype(halves)[None],
        input_grad[None],
        qkv_out,
        bias_out,
        out_weight_out,
        gain_attn_out,
        gain_ffn_out,
        shared_up_out,
        shared_down_out,
        gate_vector_out,
        expert_up_out,
        expert_down_out,
    )


def solution(mesh):
    placed = (
        P("dp", ("expert", "context"), None),
        P("dp", ("expert", "context"), None),
        P("dp", None),
        P("dp", ("expert", "context"), None),
        P("dp", ("expert", "context"), None),
        P("dp", ("expert", "context"), None),
        P(("expert", "context", "dp"), None),
        P(("expert", "context", "dp")),
        P(("expert", "context", "dp"), None),
        P(("expert", "context", "dp")),
        P(("expert", "context", "dp")),
        P(None, ("context", "dp"), "expert"),
        P("expert", ("context", "dp")),
        P(("expert", "context", "dp")),
        P("expert", ("context", "dp"), None),
        P("expert", ("context", "dp"), None),
    )
    return jax.shard_map(
        shards,
        mesh=mesh,
        in_specs=placed,
        out_specs=(
            P("dp", ("expert", "context"), None),
            P("dp", ("expert", "context"), None),
            P(("expert", "context", "dp"), None),
            P(("expert", "context", "dp")),
            P(("expert", "context", "dp"), None),
            P(("expert", "context", "dp")),
            P(("expert", "context", "dp")),
            P(None, ("context", "dp"), "expert"),
            P("expert", ("context", "dp")),
            P(("expert", "context", "dp")),
            P("expert", ("context", "dp"), None),
            P("expert", ("context", "dp"), None),
        ),
        check_vma=False,
    )
```

time: 5810 us -> 1250 us (0.22)
  waiting for transfers between devices: 5220 us -> 439 us
  local copies, waits for them, and re-layouts: 73.4 us -> 295 us
  starting transfers between devices: 18.5 us -> 191 us
  matrix products: 346 us -> 191 us
  blocking collectives: 86.7 us -> 0 us
  other arithmetic: 43.6 us -> 107 us
    reduce_scatter x10 -> x0, waiting for transfers between devices: 3440 us -> none  [the longest x1 1190 us: shards(): lax.psum_scatter(up_term, 'expert', scatter_dimension=2, tiled=True)]
    all_gather x10 -> x0, waiting for transfers between devices: 1490 us -> none  [the longest x1 762 us: shards(): lax.all_gather(up_local, 'expert', axis=2, tiled=True)]
    ppermute x0 -> x120, waiting for transfers between devices: none -> 439 us  [the longest x72 259 us: dp_step(): return lax.ppermute(value, 'dp', [(i, i ^ step) for i in range(count)])]
    all_to_all x4 -> x5, waiting for transfers between devices: 292 us -> 0.01 us  [the longest x1 0.01 us: spread(): got = lax.all_to_all(padded, every, split_axis=0, concat_axis=0, tiled=True)]
    ppermute x0 -> x120, starting transfers between devices: none -> 164 us  [the longest x72 75.2 us: dp_step(): return lax.ppermute(value, 'dp', [(i, i ^ step) for i in range(count)])]
    dynamic_update_slice x0 -> x48, local copies, waits for them, and re-layouts: none -> 161 us  [the longest x16 78.4 us: gather_weight(): lax.dynamic_update_slice(out, far[step][None, None], (1 - core, place ^ s...]
    dot_general x48 -> x49, matrix products: 346 us -> 191 us  [the longest x27 73 us: dot_tn(): lax.dot_general(left, right, (((0,), (0,)), ((), ())), preferred_element_...]
    unnamed x2 -> x0, blocking collectives: 86.7 us -> none
  transfers between devices with their start and end apart: 24 -> 125, of which waited for: 22 -> 52; matrix products, arithmetic and copies ran while one was open for 8% -> 37% of each run, Pallas kernels for 0% -> 0%
where the time goes in v1:
time: 1250 us; the launch traced here: 1230 us
  waiting for transfers between devices  439 us (35%)
  local copies, waits for them, and re-layouts  295 us (24%)
  starting transfers between devices  191 us (15%)
  matrix products  191 us (15%)
  other arithmetic  107 us (9%)
    ppermute x72, waiting for transfers between devices, dp_step(): return lax.ppermute(value, 'dp', [(i, i ^ step) for i in range(count)])  259 us
    ppermute x4, waiting for transfers between devices, group_reduce(): second = lax.ppermute(passed, 'expert', [(0, 2), (1, 3), (2, 0), (3, 1)])  78.9 us
    dynamic_update_slice x16, local copies, waits for them, and re-layouts, gather_weight(): lax.dynamic_update_slice(out, far[step][None, None], (1 - core, place ^ s...  78.4 us
    ppermute x72, starting transfers between devices, dp_step(): return lax.ppermute(value, 'dp', [(i, i ^ step) for i in range(count)])  75.2 us
    dot_general x27, matrix products, dot_tn(): lax.dot_general(left, right, (((0,), (0,)), ((), ())), preferred_element_...  73 us
    dynamic_update_slice x15, local copies, waits for them, and re-layouts, gather_weight(): lax.dynamic_update_slice(out, near[step][None, None], (core, place ^ step...  71 us
    dot_general x6, matrix products, dot_nt(): lax.dot_general(left, right, (((1,), (1,)), ((), ())), preferred_element_...  56.6 us
    dot_general x6, matrix products, dot(): return jnp.dot(left, right, preferred_element_type=floats)  41.7 us
  transfers between devices with their start and end apart: 125, of which 52 were waited for; matrix products, arithmetic and copies ran while one was open for 37% of the time, Pallas kernels for 0%

profile of v1, /device:TPU:0, one launch (start us, length us, event | category | flops | bytes accessed | tf_op | source)
XLA Modules:
  0.0 1226.6 jit_solution(8145354692978902813)
XLA Ops:
  50.1 13.3 %dynamic_update_slice.171 = bf16[2,4,256,704]{2,1,0,3:T(4,128)(2,1)S(1)} dynamic-update-slice(bf16[2,4,256,704]{2,1,0,3:T(4,128)(2,1)S(1)} %broadcast_in_dim.273, bf16[1,1,256,704]{2,1,0,3:T(2,128)(2,1)} %copy.453, s32[]{:T(128)S(6)} %select_n.564, s32[]{:T(128)S(6)} %select_n.558, s32[]{:T(128)} %constant.179.clone.1, s32[]{:T(128)} %constant.179.clone.1) | dynamic-update-slice | bytes 720900 | tf_op jit(solution)/shard_map/dynamic_update_slice | solution.py:106
  97.7 13.3 %dynamic_update_slice.172 = bf16[2,4,256,704]{2,1,0,3:T(4,128)(2,1)S(1)} dynamic-update-slice(bf16[2,4,256,704]{2,1,0,3:T(4,128)(2,1)S(1)} %dynamic_update_slice.171, bf16[1,1,256,704]{2,1,0,3:T(2,128)(2,1)} %copy.454, s32[]{:T(128)S(6)} %select_n.565, s32[]{:T(128)S(6)} %select_n.558, s32[]{:T(128)} %constant.179.clone.1, s32[]{:T(128)} %constant.179.clone.1) | dynamic-update-slice | bytes 720900 | tf_op jit(solution)/shard_map/dynamic_update_slice | solution.py:107
  111.0 13.3 %dynamic_update_slice.173 = bf16[2,4,256,704]{2,1,0,3:T(4,128)(2,1)S(1)} dynamic-update-slice(bf16[2,4,256,704]{2,1,0,3:T(4,128)(2,1)S(1)} %dynamic_update_slice.172, bf16[1,1,256,704]{2,1,0,3:T(2,128)(2,1)} %copy.455, s32[]{:T(128)S(6)} %select_n.564, s32[]{:T(128)S(6)} %select_n.559, s32[]{:T(128)} %constant.179.clone.1, s32[]{:T(128)} %constant.179.clone.1) | dynamic-update-slice | bytes 720900 | tf_op jit(solution)/shard_map/dynamic_update_slice | solution.py:106
  174.4 13.3 %dynamic_update_slice.174 = bf16[2,4,256,704]{2,1,0,3:T(4,128)(2,1)S(1)} dynamic-update-slice(bf16[2,4,256,704]{2,1,0,3:T(4,128)(2,1)S(1)} %dynamic_update_slice.173, bf16[1,1,256,704]{2,1,0,3:T(2,128)(2,1)} %copy.456, s32[]{:T(128)S(6)} %select_n.565, s32[]{:T(128)S(6)} %select_n.559, s32[]{:T(128)} %constant.179.clone.1, s32[]{:T(128)} %constant.179.clone.1) | dynamic-update-slice | bytes 720900 | tf_op jit(solution)/shard_map/dynamic_update_slice | solution.py:107
  187.8 13.3 %dynamic_update_slice.175 = bf16[2,4,256,704]{2,1,0,3:T(4,128)(2,1)S(1)} dynamic-update-slice(bf16[2,4,256,704]{2,1,0,3:T(4,128)(2,1)S(1)} %dynamic_update_slice.174, bf16[1,1,256,704]{2,1,0,3:T(2,128)(2,1)} %copy.457, s32[]{:T(128)S(6)} %select_n.564, s32[]{:T(128)S(6)} %select_n.560, s32[]{:T(128)} %constant.179.clone.1, s32[]{:T(128)} %constant.179.clone.1) | dynamic-update-slice | bytes 720900 | tf_op jit(solution)/shard_map/dynamic_update_slice | solution.py:106
  201.1 13.3 %dynamic_update_slice.176 = bf16[2,4,256,704]{2,1,0,3:T(4,128)(2,1)S(1)} dynamic-update-slice(bf16[2,4,256,704]{2,1,0,3:T(4,128)(2,1)S(1)} %dynamic_update_slice.175, bf16[1,1,256,704]{2,1,0,3:T(2,128)(2,1)} %copy.458, s32[]{:T(128)S(6)} %select_n.565, s32[]{:T(128)S(6)} %select_n.560, s32[]{:T(128)} %constant.179.clone.1, s32[]{:T(128)} %constant.179.clone.1) | dynamic-update-slice | bytes 720900 | tf_op jit(solution)/shard_map/dynamic_update_slice | solution.py:107
  214.5 13.3 %dynamic_update_slice.177 = bf16[2,4,256,704]{2,1,0,3:T(4,128)(2,1)S(1)} dynamic-update-slice(bf16[2,4,256,704]{2,1,0,3:T(4,128)(2,1)S(1)} %dynamic_update_slice.176, bf16[1,1,256,704]{2,1,0,3:T(2,128)(2,1)} %copy.459, s32[]{:T(128)S(6)} %select_n.564, s32[]{:T(128)S(6)} %select_n.561, s32[]{:T(128)} %constant.179.clone.1, s32[]{:T(128)} %constant.179.clone.1) | dynamic-update-slice | bytes 720900 | tf_op jit(solution)/shard_map/dynamic_update_slice | solution.py:106
  274.0 13.7 %dynamic_update_slice.178 = bf16[2,4,256,704]{2,1,0,3:T(4,128)(2,1)S(1)} dynamic-update-slice(bf16[2,4,256,704]{2,1,0,3:T(4,128)(2,1)S(1)} %dynamic_update_slice.177, bf16[1,1,256,704]{2,1,0,3:T(2,128)(2,1)} %copy.460, s32[]{:T(128)S(6)} %select_n.565, s32[]{:T(128)S(6)} %select_n.561, s32[]{:T(128)} %constant.179.clone.1, s32[]{:T(128)} %constant.179.clone.1) | dynamic-update-slice | bytes 720900 | tf_op jit(solution)/shard_map/dynamic_update_slice | solution.py:107
  301.8 22.9 %collective-permute-done.29 = bf16[256,1408]{1,0:T(8,128)(2,1)S(1)} collective-permute-done((bf16[256,1408]{1,0:T(8,128)(2,1)}, bf16[256,1408]{1,0:T(8,128)(2,1)S(1)}, u32[]{:S(2)}, u32[]{:S(2)}) %collective-permute-start.29) | collective-permute-done | bytes 720928 | tf_op jit(solution)/shard_map/ppermute | solution.py:73
  329.7 14.4 %collective-permute-done.31 = bf16[256,1408]{1,0:T(8,128)(2,1)} collective-permute-done((bf16[256,1408]{1,0:T(8,128)(2,1)}, bf16[256,1408]{1,0:T(8,128)(2,1)}, u32[]{:S(2)}, u32[]{:S(2)}) %collective-permute-start.31) | collective-permute-done | bytes 720928 | tf_op jit(solution)/shard_map/ppermute | solution.py:73
  346.9 12.5 %collective-permute-done.32 = bf16[256,1408]{1,0:T(8,128)(2,1)S(1)} collective-permute-done((bf16[256,1408]{1,0:T(8,128)(2,1)}, bf16[256,1408]{1,0:T(8,128)(2,1)S(1)}, u32[]{:S(2)}, u32[]{:S(2)}) %collective-permute-start.32) | collective-permute-done | bytes 720928 | tf_op jit(solution)/shard_map/ppermute | solution.py:73
  364.6 10.4 collective-permute-done.52
  377.8 12.5 %collective-permute-done.53 = bf16[176,2048]{1,0:T(8,128)(2,1)S(1)} collective-permute-done((bf16[176,2048]{1,0:T(8,128)(2,1)}, bf16[176,2048]{1,0:T(8,128)(2,1)S(1)}, u32[]{:S(2)}, u32[]{:S(2)}) %collective-permute-start.53) | collective-permute-done | bytes 720928 | tf_op jit(solution)/shard_map/ppermute | solution.py:73
  392.6 9.8 collective-permute-done.6
  415.2 27.3 %collective-permute-done.10 = bf16[4,64,768]{2,1,0:T(8,128)(2,1)S(1)} collective-permute-done((bf16[4,64,768]{2,1,0:T(8,128)(2,1)S(1)}, bf16[4,64,768]{2,1,0:T(8,128)(2,1)S(1)}, u32[]{:S(2)}, u32[]{:S(2)}) %collective-permute-start.10) | collective-permute-done | bytes 393248 | tf_op jit(solution)/shard_map/ppermute | solution.py:73
  527.3 23.0 %collective-permute-done.21 = bf16[128,2048]{1,0:T(8,128)(2,1)S(1)} collective-permute-done((bf16[128,2048]{1,0:T(8,128)(2,1)S(1)}, bf16[128,2048]{1,0:T(8,128)(2,1)S(1)}, u32[]{:S(2)}, u32[]{:S(2)}) %collective-permute-start.21) | collective-permute-done | bytes 524320 | tf_op jit(solution)/shard_map/ppermute | solution.py:164
  557.0 16.9 %collective-permute-done.23 = bf16[128,2048]{1,0:T(8,128)(2,1)} collective-permute-done((bf16[128,2048]{1,0:T(8,128)(2,1)S(1)}, bf16[128,2048]{1,0:T(8,128)(2,1)}, u32[]{:S(2)}, u32[]{:S(2)}) %collective-permute-start.23) | collective-permute-done | bytes 524320 | tf_op jit(solution)/shard_map/ppermute | solution.py:118
  610.2 13.5 %fusion.184 = f32[576,2816]{1,0:T(8,128)} fusion(bf16[576,2048]{1,0:T(8,128)(2,1)S(1)} %bitcast.604, bf16[2048,2816]{1,0:T(8,128)(2,1)} %bitcast.99), kind=kOutput, calls=%fused_computation.443 | convolution fusion | flops 6643777536 | bytes 20381696 | tf_op jit(solution)/shard_map/dot_general | solution.py:60
  623.7 10.0 multiply_convert_fusion.6
  649.8 10.4 fusion.183
  667.7 10.6 fusion.2
  709.3 10.9 convolution_convert_fusion.10
  737.0 9.6 bitcast_add_fusion
  784.9 39.4 %collective-permute-done.93 = bf16[256,1408]{1,0:T(8,128)(2,1)S(1)} collective-permute-done((bf16[256,1408]{1,0:T(8,128)(2,1)S(1)}, bf16[256,1408]{1,0:T(8,128)(2,1)S(1)}, u32[]{:S(2)}, u32[]{:S(2)}) %collective-permute-start.93) | collective-permute-done | bytes 720928 | tf_op jit(solution)/shard_map/ppermute | solution.py:73
  874.0 21.0 %collective-permute-done.118 = bf16[176,2048]{1,0:T(8,128)(2,1)S(1)} collective-permute-done((bf16[176,2048]{1,0:T(8,128)(2,1)S(1)}, bf16[176,2048]{1,0:T(8,128)(2,1)S(1)}, u32[]{:S(2)}, u32[]{:S(2)}) %collective-permute-start.118) | collective-permute-done | bytes 720928 | tf_op jit(solution)/shard_map/ppermute | solution.py:73
  933.6 22.2 %collective-permute-done.69 = bf16[128,2048]{1,0:T(8,128)(2,1)S(1)} collective-permute-done((bf16[128,2048]{1,0:T(8,128)(2,1)S(1)}, bf16[128,2048]{1,0:T(8,128)(2,1)S(1)}, u32[]{:S(2)}, u32[]{:S(2)}) %collective-permute-start.69) | collective-permute-done | bytes 524320 | tf_op jit(solution)/shard_map/ppermute | solution.py:164
  967.1 9.0 collective-permute-done.115
  1048.6 10.9 multiply_reduce_fusion
  1150.9 11.2 collective-permute-done.76
  1162.1 15.2 %collective-permute-start.59 = (bf16[128,2048]{1,0:T(8,128)(2,1)}, bf16[128,2048]{1,0:T(8,128)(2,1)}, u32[]{:S(2)}, u32[]{:S(2)}) collective-permute-start(bf16[128,2048]{1,0:T(8,128)(2,1)} %fusion.65), channel_id=1, source_target_pairs={{0,16},{8,24},{16,0},{24,8},{1,17},{9,25},{17,1},{25,9},{2,18},{10... | collective-permute-start | bytes 1572872 | tf_op jit(solution)/shard_map/ppermute | solution.py:164
  1185.8 24.9 %collective-permute-done.79 = bf16[128,2048]{1,0:T(8,128)(2,1)} collective-permute-done((bf16[128,2048]{1,0:T(8,128)(2,1)}, bf16[128,2048]{1,0:T(8,128)(2,1)}, u32[]{:S(2)}, u32[]{:S(2)}) %collective-permute-start.79) | collective-permute-done | bytes 524320 | tf_op jit(solution)/shard_map/ppermute | solution.py:164
  1212.6 8.9 collective-permute-done.59
  (795 shorter events, 738.7 us)
Async XLA Ops:
  2.4 66.0 %collective-permute-start.11 = (bf16[32,2048]{1,0:T(8,128)(2,1)}, bf16[32,2048]{1,0:T(8,128)(2,1)}, u32[]{:S(2)}, u32[]{:S(2)}) collective-permute-start(bf16[32,2048]{1,0:T(8,128)(2,1)} %get-tuple-element.223), channel_id=1, source_target_pairs={{0,1},{1,0},{2,3},{3,2},{4,5},{5,4},{6,7},{7,6},{8,9},{9,8},{10,11... | collective-permute-start | bytes 393224 | tf_op jit(solution)/shard_map/ppermute | solution.py:73
  5.4 70.3 %collective-permute-start.13 = (bf16[32,2048]{1,0:T(8,128)(2,1)}, bf16[32,2048]{1,0:T(8,128)(2,1)}, u32[]{:S(2)}, u32[]{:S(2)}) collective-permute-start(bf16[32,2048]{1,0:T(8,128)(2,1)} %get-tuple-element.223), channel_id=1, source_target_pairs={{0,2},{1,3},{2,0},{3,1},{4,6},{5,7},{6,4},{7,5},{8,10},{9,11},{10,... | collective-permute-start | bytes 393224 | tf_op jit(solution)/shard_map/ppermute | solution.py:73
  6.9 64.8 %collective-permute-start.12 = (bf16[32,2048]{1,0:T(8,128)(2,1)}, bf16[32,2048]{1,0:T(8,128)(2,1)}, u32[]{:S(2)}, u32[]{:S(2)}) collective-permute-start(bf16[32,2048]{1,0:T(8,128)(2,1)} %get-tuple-element.222), channel_id=1, source_target_pairs={{0,1},{1,0},{2,3},{3,2},{4,5},{5,4},{6,7},{7,6},{8,9},{9,8},{10,11... | collective-permute-start | bytes 393224 | tf_op jit(solution)/shard_map/ppermute | solution.py:73
  7.4 69.8 %collective-permute-start.14 = (bf16[32,2048]{1,0:T(8,128)(2,1)}, bf16[32,2048]{1,0:T(8,128)(2,1)}, u32[]{:S(2)}, u32[]{:S(2)}) collective-permute-start(bf16[32,2048]{1,0:T(8,128)(2,1)} %get-tuple-element.222), channel_id=1, source_target_pairs={{0,2},{1,3},{2,0},{3,1},{4,6},{5,7},{6,4},{7,5},{8,10},{9,11},{10,... | collective-permute-start | bytes 393224 | tf_op jit(solution)/shard_map/ppermute | solution.py:73
  13.4 111.0 %all-to-all-start = ((f32[32,15,128]{2,1,0:T(8,128)}), f32[32,15,128]{2,1,0:T(8,128)}, u32[]{:S(2)}, u32[]{:S(2)}) async-start(f32[32,15,128]{2,1,0:T(8,128)} %broadcast_in_dim.243), calls=%async_computation | async-start | bytes 524288 | tf_op jit(solution)/shard_map/all_to_all | solution.py:176
  21.9 70.4 %collective-permute-start.35 = (bf16[256,704]{0,1:T(8,128)(2,1)}, bf16[256,704]{0,1:T(8,128)(2,1)}, u32[]{:S(2)}, u32[]{:S(2)}) collective-permute-start(bf16[256,704]{0,1:T(8,128)(2,1)} %get-tuple-element.218), channel_id=1, source_target_pairs={{0,1},{1,0},{2,3},{3,2},{4,5},{5,4},{6,7},{7,6},{8,9},{9,8},{10,11... | collective-permute-start | bytes 1081352 | tf_op jit(solution)/shard_map/ppermute | solution.py:73
  71.7 76.8 %collective-permute-start.1 = (bf16[128,2048]{1,0:T(8,128)(2,1)S(1)}, bf16[128,2048]{1,0:T(8,128)(2,1)}, u32[]{:S(2)}, u32[]{:S(2)}) collective-permute-start(bf16[128,2048]{1,0:T(8,128)(2,1)S(1)} %bitcast.568), channel_id=1, source_target_pairs={{0,16},{8,24},{16,0},{24,8},{1,17},{9,25},{17,1},{25,9},{2,18},{10... | collective-permute-start | bytes 1572872 | tf_op jit(solution)/shard_map/ppermute | solution.py:118
  75.6 73.5 %collective-permute-start.48 = (bf16[176,2048]{1,0:T(8,128)(2,1)}, bf16[176,2048]{1,0:T(8,128)(2,1)}, u32[]{:S(2)}, u32[]{:S(2)}) collective-permute-start(bf16[176,2048]{1,0:T(8,128)(2,1)} %get-tuple-element.203), channel_id=1, source_target_pairs={{0,4},{4,0},{1,5},{5,1},{2,6},{6,2},{3,7},{7,3},{8,12},{12,8},{9,1... | collective-permute-start | bytes 2162696 | tf_op jit(solution)/shard_map/ppermute | solution.py:77
  90.3 62.2 %collective-permute-start.49 = (bf16[176,2048]{1,0:T(8,128)(2,1)}, bf16[176,2048]{1,0:T(8,128)(2,1)}, u32[]{:S(2)}, u32[]{:S(2)}) collective-permute-start(bf16[176,2048]{1,0:T(8,128)(2,1)} %get-tuple-element.202), channel_id=1, source_target_pairs={{0,1},{1,0},{2,3},{3,2},{4,5},{5,4},{6,7},{7,6},{8,9},{9,8},{10,11... | collective-permute-start | bytes 2162696 | tf_op jit(solution)/shard_map/ppermute | solution.py:73
  94.8 133.0 %collective-permute-start.28 = (bf16[256,1408]{1,0:T(8,128)(2,1)}, bf16[256,1408]{1,0:T(8,128)(2,1)}, u32[]{:S(2)}, u32[]{:S(2)}) collective-permute-start(bf16[256,1408]{1,0:T(8,128)(2,1)} %get-tuple-element.106), channel_id=1, source_target_pairs={{0,1},{1,0},{2,3},{3,2},{4,5},{5,4},{6,7},{7,6},{8,9},{9,8},{10,11... | collective-permute-start | bytes 2162696 | tf_op jit(solution)/shard_map/ppermute | solution.py:73
  124.4 166.6 %all-to-all-start.1 = ((bf16[8,64,768]{2,1,0:T(8,128)(2,1)}), bf16[8,64,768]{2,1,0:T(8,128)(2,1)}, u32[]{:S(2)}, u32[]{:S(2)}) async-start(bf16[8,64,768]{2,1,0:T(8,128)(2,1)} %reshape.557), calls=%async_computation.1 | async-start | bytes 1572864 | tf_op jit(solution)/shard_map/all_to_all | solution.py:187
  152.5 78.9 %collective-permute-start = (bf16[128,2048]{1,0:T(8,128)(2,1)S(1)}, bf16[128,2048]{1,0:T(8,128)(2,1)}, u32[]{:S(2)}, u32[]{:S(2)}) collective-permute-start(bf16[128,2048]{1,0:T(8,128)(2,1)S(1)} %bitcast.569), channel_id=1, source_target_pairs={{0,8},{8,16},{16,24},{1,9},{9,17},{17,25},{2,10},{10,18},{18,26},{... | collective-permute-start | bytes 1572872 | tf_op jit(solution)/shard_map/ppermute | solution.py:116
  157.2 75.0 %collective-permute-start.3 = (bf16[128,2048]{1,0:T(8,128)(2,1)S(1)}, bf16[128,2048]{1,0:T(8,128)(2,1)}, u32[]{:S(2)}, u32[]{:S(2)}) collective-permute-start(bf16[128,2048]{1,0:T(8,128)(2,1)S(1)} %bitcast.570), channel_id=1, source_target_pairs={{8,0},{16,8},{24,16},{9,1},{17,9},{25,17},{10,2},{18,10},{26,18},{... | collective-permute-start | bytes 1572872 | tf_op jit(solution)/shard_map/ppermute | solution.py:117
  159.9 77.6 %collective-permute-start.61 = (bf16[128,2048]{1,0:T(8,128)(2,1)}, bf16[128,2048]{1,0:T(8,128)(2,1)}, u32[]{:S(2)}, u32[]{:S(2)}) collective-permute-start(bf16[128,2048]{1,0:T(8,128)(2,1)} %bitcast.122), channel_id=1, source_target_pairs={{0,16},{8,24},{16,0},{24,8},{1,17},{9,25},{17,1},{25,9},{2,18},{10... | collective-permute-start | bytes 1572872 | tf_op jit(solution)/shard_map/ppermute | solution.py:118
  166.9 72.0 %collective-permute-start.2 = (bf16[128,2048]{1,0:T(8,128)(2,1)}, bf16[128,2048]{1,0:T(8,128)(2,1)}, u32[]{:S(2)}, u32[]{:S(2)}) collective-permute-start(bf16[128,2048]{1,0:T(8,128)(2,1)} %collective-permute-done.1), channel_id=1, source_target_pairs={{16,24},{8,0},{17,25},{9,1},{18,26},{10,2},{19,27},{11,3},{20,28},... | collective-permute-start | bytes 1572872 | tf_op jit(solution)/shard_map/ppermute | solution.py:119
  227.9 70.0 %collective-permute-start.42 = (bf16[256,2816]{1,0:T(8,128)(2,1)}, bf16[256,2816]{1,0:T(8,128)(2,1)}, u32[]{:S(2)}, u32[]{:S(2)}) collective-permute-start(bf16[256,2816]{1,0:T(8,128)(2,1)} %get-tuple-element.150), channel_id=1, source_target_pairs={{0,1},{1,0},{2,3},{3,2},{4,5},{5,4},{6,7},{7,6},{8,9},{9,8},{10,11... | collective-permute-start | bytes 4325384 | tf_op jit(solution)/shard_map/ppermute | solution.py:73
  231.4 260.2 %collective-permute-start.44 = (bf16[256,2816]{1,0:T(8,128)(2,1)}, bf16[256,2816]{1,0:T(8,128)(2,1)}, u32[]{:S(2)}, u32[]{:S(2)}) collective-permute-start(bf16[256,2816]{1,0:T(8,128)(2,1)} %get-tuple-element.150), channel_id=1, source_target_pairs={{0,2},{1,3},{2,0},{3,1},{4,6},{5,7},{6,4},{7,5},{8,10},{9,11},{10,... | collective-permute-start | bytes 4325384 | tf_op jit(solution)/shard_map/ppermute | solution.py:73
  247.8 114.3 %collective-permute-start.51 = (bf16[176,2048]{1,0:T(8,128)(2,1)}, bf16[176,2048]{1,0:T(8,128)(2,1)}, u32[]{:S(2)}, u32[]{:S(2)}) collective-permute-start(bf16[176,2048]{1,0:T(8,128)(2,1)} %get-tuple-element.202), channel_id=1, source_target_pairs={{0,2},{1,3},{2,0},{3,1},{4,6},{5,7},{6,4},{7,5},{8,10},{9,11},{10,... | collective-permute-start | bytes 2162696 | tf_op jit(solution)/shard_map/ppermute | solution.py:73
  294.6 66.6 %collective-permute-start.50 = (bf16[176,2048]{1,0:T(8,128)(2,1)}, bf16[176,2048]{1,0:T(8,128)(2,1)S(1)}, u32[]{:S(2)}, u32[]{:S(2)}) collective-permute-start(bf16[176,2048]{1,0:T(8,128)(2,1)} %collective-permute-done.48), channel_id=1, source_target_pairs={{0,1},{1,0},{2,3},{3,2},{4,5},{5,4},{6,7},{7,6},{8,9},{9,8},{10,11... | collective-permute-start | bytes 2162696 | tf_op jit(solution)/shard_map/ppermute | solution.py:73
  361.2 82.0 %collective-permute-start.4 = (bf16[4,128,2048]{2,1,0:T(8,128)(2,1)S(1)}, bf16[4,128,2048]{2,1,0:T(8,128)(2,1)S(1)}, u32[]{:S(2)}, u32[]{:S(2)}) collective-permute-start(bf16[4,128,2048]{2,1,0:T(8,128)(2,1)S(1)} %copy-done.70), channel_id=1, source_target_pairs={{0,4},{4,0},{1,5},{5,1},{2,6},{6,2},{3,7},{7,3},{8,12},{12,8},{9,1... | collective-permute-start | bytes 6291464 | tf_op jit(solution)/shard_map/ppermute | solution.py:77
  402.5 85.2 %collective-permute-start.43 = (bf16[256,2816]{1,0:T(8,128)(2,1)}, bf16[256,2816]{1,0:T(8,128)(2,1)}, u32[]{:S(2)}, u32[]{:S(2)}) collective-permute-start(bf16[256,2816]{1,0:T(8,128)(2,1)} %collective-permute-done.41), channel_id=1, source_target_pairs={{0,1},{1,0},{2,3},{3,2},{4,5},{5,4},{6,7},{7,6},{8,9},{9,8},{10,11... | collective-permute-start | bytes 4325384 | tf_op jit(solution)/shard_map/ppermute | solution.py:73
  414.8 73.7 %collective-permute-start.45 = (bf16[256,2816]{1,0:T(8,128)(2,1)}, bf16[256,2816]{1,0:T(8,128)(2,1)}, u32[]{:S(2)}, u32[]{:S(2)}) collective-permute-start(bf16[256,2816]{1,0:T(8,128)(2,1)} %collective-permute-done.41), channel_id=1, source_target_pairs={{0,2},{1,3},{2,0},{3,1},{4,6},{5,7},{6,4},{7,5},{8,10},{9,11},{10,... | collective-permute-start | bytes 4325384 | tf_op jit(solution)/shard_map/ppermute | solution.py:73
  485.3 67.7 %collective-permute-start.64 = (bf16[4,128,2048]{2,1,0:T(8,128)(2,1)S(1)}, bf16[4,128,2048]{2,1,0:T(8,128)(2,1)S(1)}, u32[]{:S(2)}, u32[]{:S(2)}) collective-permute-start(bf16[4,128,2048]{2,1,0:T(8,128)(2,1)S(1)} %copy-done.69), channel_id=1, source_target_pairs={{0,4},{4,0},{1,5},{5,1},{2,6},{6,2},{3,7},{7,3},{8,12},{12,8},{9,1... | collective-permute-start | bytes 6291464 | tf_op jit(solution)/shard_map/ppermute | solution.py:77
  488.5 111.9 %collective-permute-start.47 = (bf16[256,2816]{1,0:T(8,128)(2,1)}, bf16[256,2816]{1,0:T(8,128)(2,1)}, u32[]{:S(2)}, u32[]{:S(2)}) collective-permute-start(bf16[256,2816]{1,0:T(8,128)(2,1)} %collective-permute-done.45), channel_id=1, source_target_pairs={{0,1},{1,0},{2,3},{3,2},{4,5},{5,4},{6,7},{7,6},{8,9},{9,8},{10,11... | collective-permute-start | bytes 4325384 | tf_op jit(solution)/shard_map/ppermute | solution.py:73
  768.1 62.2 %collective-permute-start.107 = (bf16[256,2816]{1,0:T(8,128)(2,1)}, bf16[256,2816]{1,0:T(8,128)(2,1)S(1)}, u32[]{:S(2)}, u32[]{:S(2)}) collective-permute-start(bf16[256,2816]{1,0:T(8,128)(2,1)} %convolution_convert_fusion.5), channel_id=1, source_target_pairs={{0,1},{1,0},{2,3},{3,2},{4,5},{5,4},{6,7},{7,6},{8,9},{9,8},{10,11... | collective-permute-start | bytes 4325384 | tf_op jit(solution)/shard_map/ppermute | solution.py:73
  770.7 73.8 %collective-permute-start.110 = (bf16[256,2816]{1,0:T(8,128)(2,1)S(1)}, bf16[256,2816]{1,0:T(8,128)(2,1)S(1)}, u32[]{:S(2)}, u32[]{:S(2)}) collective-permute-start(bf16[256,2816]{1,0:T(8,128)(2,1)S(1)} %copy-done.115), channel_id=1, source_target_pairs={{0,2},{1,3},{2,0},{3,1},{4,6},{5,7},{6,4},{7,5},{8,10},{9,11},{10,... | collective-permute-start | bytes 4325384 | tf_op jit(solution)/shard_map/ppermute | solution.py:73
  860.3 97.0 %collective-permute-start.92 = (bf16[256,1408]{1,0:T(8,128)(2,1)}, bf16[256,1408]{1,0:T(8,128)(2,1)S(1)}, u32[]{:S(2)}, u32[]{:S(2)}) collective-permute-start(bf16[256,1408]{1,0:T(8,128)(2,1)} %convolution_convert_fusion.19), channel_id=1, source_target_pairs={{0,1},{1,0},{2,3},{3,2},{4,5},{5,4},{6,7},{7,6},{8,9},{9,8},{10,11... | collective-permute-start | bytes 2162696 | tf_op jit(solution)/shard_map/ppermute | solution.py:73
  958.2 63.5 %collective-permute-start.112 = (f32[256,2816]{1,0:T(8,128)}, f32[256,2816]{1,0:T(8,128)}, u32[]{:S(2)}, u32[]{:S(2)}) collective-permute-start(f32[256,2816]{1,0:T(8,128)} %convert_add_fusion), channel_id=1, source_target_pairs={{0,4},{4,0},{1,5},{5,1},{2,6},{6,2},{3,7},{7,3},{8,12},{12,8},{9,1... | collective-permute-start | bytes 8650760 | tf_op jit(solution)/shard_map/ppermute | solution.py:77
  994.2 218.4 %collective-permute-start.56 = (bf16[128,2048]{1,0:T(8,128)(2,1)}, bf16[128,2048]{1,0:T(8,128)(2,1)}, u32[]{:S(2)}, u32[]{:S(2)}) collective-permute-start(bf16[128,2048]{1,0:T(8,128)(2,1)} %get-tuple-element.168), channel_id=1, source_target_pairs={{0,8},{8,16},{16,24},{1,9},{9,17},{17,25},{2,10},{10,18},{18,26},{... | collective-permute-start | bytes 1572872 | tf_op jit(solution)/shard_map/ppermute | solution.py:161
  1133.0 79.5 %collective-permute-start.57 = (bf16[128,2048]{1,0:T(8,128)(2,1)}, bf16[128,2048]{1,0:T(8,128)(2,1)}, u32[]{:S(2)}, u32[]{:S(2)}) collective-permute-start(bf16[128,2048]{1,0:T(8,128)(2,1)} %get-tuple-element.170), channel_id=1, source_target_pairs={{8,0},{16,8},{24,16},{9,1},{17,9},{25,17},{10,2},{18,10},{26,18},{... | collective-permute-start | bytes 1572872 | tf_op jit(solution)/shard_map/ppermute | solution.py:162
  1146.9 63.8 %collective-permute-start.79 = (bf16[128,2048]{1,0:T(8,128)(2,1)}, bf16[128,2048]{1,0:T(8,128)(2,1)}, u32[]{:S(2)}, u32[]{:S(2)}) collective-permute-start(bf16[128,2048]{1,0:T(8,128)(2,1)} %fusion.57), channel_id=1, source_target_pairs={{0,16},{8,24},{16,0},{24,8},{1,17},{9,25},{17,1},{25,9},{2,18},{10... | collective-permute-start | bytes 1572872 | tf_op jit(solution)/shard_map/ppermute | solution.py:164
  1162.1 59.4 %collective-permute-start.59 = (bf16[128,2048]{1,0:T(8,128)(2,1)}, bf16[128,2048]{1,0:T(8,128)(2,1)}, u32[]{:S(2)}, u32[]{:S(2)}) collective-permute-start(bf16[128,2048]{1,0:T(8,128)(2,1)} %fusion.65), channel_id=1, source_target_pairs={{0,16},{8,24},{16,0},{24,8},{1,17},{9,25},{17,1},{25,9},{2,18},{10... | collective-permute-start | bytes 1572872 | tf_op jit(solution)/shard_map/ppermute | solution.py:164
  (241 other events, 5173.0 us)

commit v2 on v1

--- a/solution.py
+++ b/solution.py
@@ -3,6 +3,8 @@
 import jax
 import jax.numpy as jnp
 from jax import lax
+from jax.experimental import pallas as pl
+from jax.experimental.pallas import tpu as pltpu
 from jax.sharding import PartitionSpec as P
 
 HEADS = 16
@@ -77,97 +79,105 @@
     return lax.ppermute(value, "context", [(0, 1), (1, 0)])
 
 
-def gather_square(first, second):
-    first_x, first_y = dp_step(first, 1), dp_step(first, 2)
-    second_y, second_x = dp_step(second, 2), dp_step(second, 1)
-    first_far, second_far = dp_step(first_x, 2), dp_step(second_y, 1)
-    return [first, first_x, first_y, first_far], [second, second_x, second_y, second_far]
-
-
-def reduce_square(first, second):
-    first_far, first_near = dp_step(first[3], 1), dp_step(first[1], 1)
-    second_far, second_near = dp_step(second[3], 2), dp_step(second[2], 2)
-    first_pass = (first[2].astype(floats) + first_far.astype(floats)).astype(halves)
-    second_pass = (second[1].astype(floats) + second_far.astype(floats)).astype(halves)
-    first_last, second_last = dp_step(first_pass, 2), dp_step(second_pass, 1)
-    first_sum = first[0].astype(floats) + first_near.astype(floats) + first_last.astype(floats)
-    second_sum = second[0].astype(floats) + second_near.astype(floats) + second_last.astype(floats)
-    return first_sum, second_sum
-
-
-def gather_weight(kept, given):
+def after(value, *others):
+    return lax.optimization_barrier((value,) + others)[0]
+
+
+def near_blocks(block):
+    return dp_step(block, 1), dp_step(block, 2)
+
+
+def place_blocks(pieces, places, out_shape, views):
+    count = len(pieces)
+
+    def kernel(place_ref, *refs):
+        blocks, out, held = refs[:count], refs[count], refs[count + 1 : 2 * count + 1]
+        in_sems, out_sems = refs[2 * count + 1 :]
+        loads = [
+            pltpu.make_async_copy(blocks[i], held[i], in_sems.at[i]) for i in range(count)
+        ]
+        stores = [
+            pltpu.make_async_copy(held[i], views[i](out, place_ref[i]), out_sems.at[i])
+            for i in range(count)
+        ]
+        for load in loads:
+            load.start()
+        for load, store in zip(loads, stores):
+            load.wait()
+            store.start()
+        for store in stores:
+            store.wait()
+
+    return pl.pallas_call(
+        kernel,
+        out_shape=jax.ShapeDtypeStruct(out_shape, pieces[0].dtype),
+        in_specs=[pl.BlockSpec(memory_space=pltpu.SMEM)]
+        + [pl.BlockSpec(memory_space=pl.ANY)] * len(pieces),
+        out_specs=pl.BlockSpec(memory_space=pl.ANY),
+        scratch_shapes=[pltpu.VMEM(piece.shape, piece.dtype) for piece in pieces]
+        + [
+            pltpu.SemaphoreType.DMA((count,)),
+            pltpu.SemaphoreType.DMA((count,)),
+        ],
+        compiler_params=pltpu.CompilerParams(vmem_limit_bytes=32 * 1024 * 1024),
+        cost_estimate=pl.CostEstimate(
+            flops=0, bytes_accessed=2 * sum(p.size * 2 for p in pieces), transcendentals=0
+        ),
+    )(jnp.stack(places).astype(jnp.int32), *pieces)
+
+
+def sum_weight(part):
+    rows, wide = part.shape
+    return lax.psum_scatter(
+        part.reshape(2, rows // 2, wide), "dp", scatter_dimension=1, tiled=True
+    )
+
+
+def both_cores(kept, given):
     core = lax.axis_index("context")
-    place = lax.axis_index("dp")
     taken = other_core(given)
-    near, far = gather_square(kept, taken)
-    out = jnp.zeros((2, 4) + kept.shape, kept.dtype)
-    zeros = (0,) * kept.ndim
-    for step in range(4):
-        out = lax.dynamic_update_slice(out, near[step][None, None], (core, place ^ step) + zeros)
-        out = lax.dynamic_update_slice(out, far[step][None, None], (1 - core, place ^ step) + zeros)
-    return out
-
-
-def line_gather(block):
-    count = lax.axis_size("expert")
-    if count != 4:
-        return lax.all_gather(block, "expert", axis=0)
-    here = lax.axis_index("expert")
-    lower = lax.ppermute(block, "expert", [(0, 1), (1, 2), (2, 3)])
-    upper = lax.ppermute(block, "expert", [(1, 0), (2, 1), (3, 2)])
-    second = lax.ppermute(block, "expert", [(0, 2), (1, 3), (2, 0), (3, 1)])
-    third = lax.ppermute(second, "expert", [(2, 3), (1, 0)])
-    table = (
-        (block, upper, second, third),
-        (lower, block, upper, second),
-        (second, lower, block, upper),
-        (third, second, lower, block),
-    )
-    rows = []
-    for slot in range(4):
-        pick = table[3][slot]
-        for at in (2, 1, 0):
-            pick = jnp.where(here == at, table[at][slot], pick)
-        rows.append(pick)
-    return jnp.stack(rows)
-
-
-def group_gather(block):
-    if lax.axis_size("expert") != 4:
-        return lax.all_gather(block, group, axis=0, tiled=True)
+    return jnp.stack([jnp.where(core == 0, kept, taken), jnp.where(core == 0, taken, kept)])
+
+
+def gather_rows(both):
+    out = lax.all_gather(both, "dp", axis=1, tiled=True)
+    return out.reshape(-1, both.shape[2])
+
+
+def cores_in_order(blocks):
     core = lax.axis_index("context")
-    mine = line_gather(block)
+    mine = jnp.where(core == 0, blocks[0], blocks[1])
+    other = other_core(jnp.where(core == 0, blocks[1], blocks[0]))
+    return jnp.where(core == 0, mine, other), jnp.where(core == 0, other, mine)
+
+
+def along_expert(blocks):
+    return lax.all_to_all(blocks, "expert", split_axis=0, concat_axis=0, tiled=True)
+
+
+def gather_line(block):
+    return along_expert(jnp.broadcast_to(block[None], (lax.axis_size("expert"),) + block.shape))
+
+
+def gather_cores(mine):
+    core = lax.axis_index("context")
     other = other_core(mine)
     both = jnp.stack([jnp.where(core == 0, mine, other), jnp.where(core == 0, other, mine)], axis=1)
-    return both.reshape((-1,) + block.shape[1:])
+    return both.reshape((-1,) + mine.shape[2:])
+
+
+def group_gather(block):
+    return gather_cores(gather_line(block))
 
 
 def group_reduce(part):
     count = lax.axis_size("expert")
-    if count != 4:
-        return lax.psum_scatter(part, group, scatter_dimension=0, tiled=True)
     core = lax.axis_index("context")
-    here = lax.axis_index("expert")
-    width = part.shape[1]
-    view = part.reshape(count, 2, -1, width)
+    view = part.reshape(count, 2, -1, part.shape[1])
     mine = lax.dynamic_index_in_dim(view, core, 1, keepdims=False)
     other = lax.dynamic_index_in_dim(view, 1 - core, 1, keepdims=False).astype(halves)
     rows = (mine + other_core(other).astype(floats)).astype(halves)
-
-    def of(place):
-        return lax.dynamic_index_in_dim(rows, jnp.clip(place, 0, 3), 0, keepdims=False)
-
-    corner = lax.ppermute(of(jnp.where(here == 3, 0, 3)), "expert", [(3, 2), (0, 1)])
-    lower = lax.ppermute(of(here + 1), "expert", [(0, 1), (1, 2), (2, 3)])
-    upper = lax.ppermute(of(here - 1), "expert", [(1, 0), (2, 1), (3, 2)])
-    passed = (of(here ^ 2).astype(floats) + corner.astype(floats)).astype(halves)
-    second = lax.ppermute(passed, "expert", [(0, 2), (1, 3), (2, 0), (3, 1)])
-    return (
-        of(here).astype(floats)
-        + lower.astype(floats)
-        + upper.astype(floats)
-        + second.astype(floats)
-    )
+    return jnp.sum(along_expert(rows).astype(floats), axis=0), rows
 
 
 def spread(values):
@@ -177,30 +187,42 @@
     return got.reshape(count, -1)
 
 
-def head_weights(qkv_weight, out_weight):
+def head_cut(qkv_weight, out_weight, vectors):
     count = lax.axis_size(group)
+    rows, wide = qkv_weight.shape
+    piece = wide // (3 * count)
+    cut = qkv_weight.reshape(rows, 3, count, piece).transpose(2, 0, 1, 3).reshape(count, rows, 3 * piece)
+    columns = jnp.concatenate([vector.reshape(-1, rows) for vector in vectors]).T
+    columns = jnp.pad(columns, ((0, 0), (0, 128 - columns.shape[1])))
+    columns = jnp.broadcast_to(columns[None], (count,) + columns.shape)
+    cut = jnp.concatenate([cut, columns], axis=-1)
+    cut = lax.all_to_all(cut, group, split_axis=0, concat_axis=0, tiled=True)
+    out = out_weight.reshape(rows, count, piece).transpose(1, 0, 2)
+    return jnp.concatenate([cut, out], axis=-1)
+
+
+def head_weights(own, x_block, y_block, pins):
+    count, rows, wide = own.shape
     place = lax.axis_index("dp")
-    rows, wide = qkv_weight.shape
-    width = wide // 3
-    piece = width // count
-    cut = qkv_weight.reshape(rows, 3, count, piece).transpose(2, 0, 1, 3).reshape(count, rows, 3 * piece)
-    cut = lax.all_to_all(cut, group, split_axis=0, concat_axis=0, tiled=True)
     half = count // 2
-    first, second = gather_square(cut[:half], cut[half:])
-    weight = jnp.zeros((count, 4, rows, 3 * piece), halves)
-    half_rows = rows // 2
-    first_out, second_out = gather_square(out_weight[:half_rows], out_weight[half_rows:])
-    out = jnp.zeros((4, 2, half_rows, width), halves)
-    for step in range(4):
-        at = place ^ step
-        weight = lax.dynamic_update_slice(weight, first[step][:, None], (0, at, 0, 0))
-        weight = lax.dynamic_update_slice(weight, second[step][:, None], (half, at, 0, 0))
-        out = lax.dynamic_update_slice(out, first_out[step][None, None], (at, 0, 0, 0))
-        out = lax.dynamic_update_slice(out, second_out[step][None, None], (at, 1, 0, 0))
-    return weight.reshape(width, 3 * piece), out.reshape(piece, width)
-
-
-def heads_forward(all_tokens, gain, bias, weights, seq_ids):
+    far_low = dp_step(after(x_block[:half], *pins), 2)
+    far_high = dp_step(after(y_block[half:], *pins), 1)
+    pieces = [own, x_block, y_block, far_low, far_high]
+    places = [place, place ^ 1, place ^ 2, place ^ 3, place ^ 3]
+    whole = lambda out, at: out.at[:, at]
+    low = lambda out, at: out.at[pl.ds(0, half), at]
+    high = lambda out, at: out.at[pl.ds(half, half), at]
+    packed = place_blocks(pieces, places, (count, 4, rows, wide), [whole] * 3 + [low, high])
+    piece = (wide - 128) // 4
+    weight = packed[..., : 3 * piece].reshape(count * 4 * rows, 3 * piece)
+    out = packed[..., 3 * piece + 128 :].transpose(1, 2, 0, 3).reshape(4 * rows, count * piece)
+    columns = packed[..., 3 * piece : 3 * piece + 6].astype(floats)
+    vectors = [columns[..., at].reshape(-1) for at in range(3)]
+    vectors.append(columns[..., 3:].transpose(0, 1, 3, 2).reshape(-1))
+    return (weight, out), vectors, (far_low, far_high)
+
+
+def heads_forward(all_tokens, gain, bias, weights, seq_ids, pin):
     weight, out_rows = weights
     count = lax.axis_size(group)
     index = lax.axis_index(group)
@@ -228,11 +250,11 @@
     probs = grown / jnp.sum(grown, axis=-1, keepdims=True)
     attended = jnp.einsum("hqk,khd->qhd", probs.astype(halves), value, preferred_element_type=floats)
     attended = attended.reshape(length, piece).astype(halves)
-    mixed = group_reduce(dot(attended, out_rows))
-    return mixed, (normed, query, key, value, probs, attended, cosine, sine)
-
-
-def heads_backward(all_tokens, gain, weights, saved, mid_low):
+    mixed, rows = group_reduce(after(dot(attended, out_rows), *pin))
+    return mixed, (normed, query, key, value, probs, attended, cosine, sine), (attended, rows)
+
+
+def heads_backward(all_tokens, gain, weights, saved, mid_low, pins):
     weight, out_rows = weights
     normed, query, key, value, probs, attended, cosine, sine = saved
     count = lax.axis_size(group)
@@ -242,7 +264,7 @@
     piece = width // count
     heads = piece // HEAD_DIM
     scale = 1.0 / math.sqrt(HEAD_DIM)
-    all_mid = group_gather(mid_low)
+    all_mid = gather_cores(after(gather_line(mid_low), pins[0]))
     attended_grad = dot_nt(all_mid, out_rows).astype(halves).reshape(length, heads, HEAD_DIM)
     prob_grad = jnp.einsum("qhd,khd->hqk", attended_grad, value, preferred_element_type=floats)
     delta = jnp.sum(probs * prob_grad, axis=-1, keepdims=True)
@@ -261,7 +283,8 @@
         axis=-1,
     ).astype(halves)
     weight_part = dot_tn(normed, proj_grad).astype(halves)
-    in_part = dot_nt(proj_grad, weight)
+    in_part = dot_nt(after(proj_grad, pins[1], pins[2]), weight)
+    layer_sum, _ = group_reduce(after(pins[3], all_mid))
     tokens = all_tokens.astype(floats)
     stat = lax.rsqrt(jnp.mean(tokens * tokens, axis=-1, keepdims=True) + eps_norm)
     gain_part = jnp.sum(in_part * (tokens * stat), axis=0)
@@ -270,23 +293,19 @@
         jnp.sum(proj_grad.astype(floats), axis=0).reshape(3, 1, piece),
         (0, index, 0),
     ).reshape(-1)
-    attn_in_grad = group_reduce(in_part)
+    attn_in_grad, rows_low = group_reduce(after(in_part, layer_sum))
     rows = width // (count * 4)
-    half = count // 2
-    cut = weight_part.reshape(count, 4, rows, 3 * piece)
-    picks = [lax.dynamic_index_in_dim(cut, place ^ step, 1, keepdims=False) for step in range(4)]
-    first, second = reduce_square([pick[:half] for pick in picks], [pick[half:] for pick in picks])
-    total = jnp.concatenate([first, second]).astype(halves)
+    cut = weight_part.reshape(count, 4, rows, 3 * piece).transpose(1, 0, 2, 3)
+    total = lax.psum_scatter(
+        cut.reshape(width, 3 * piece), "dp", scatter_dimension=0, tiled=True
+    ).reshape(count, rows, 3 * piece)
     total = lax.all_to_all(total, group, split_axis=0, concat_axis=0, tiled=True)
     qkv_out = (
         total.reshape(count, rows, 3, piece).transpose(1, 2, 0, 3).reshape(rows, 3 * width).astype(floats)
     )
-    out_part = dot_tn(attended, all_mid).astype(halves).reshape(4, rows, width)
-    picks = [lax.dynamic_index_in_dim(out_part, place ^ step, 0, keepdims=False) for step in range(4)]
-    first, second = reduce_square(
-        [pick[: rows // 2] for pick in picks], [pick[rows // 2 :] for pick in picks]
-    )
-    return attn_in_grad, gain_part, bias_part, qkv_out, jnp.concatenate([first, second])
+    out_part = dot_tn(attended, all_mid).astype(halves)
+    out_out = lax.psum_scatter(out_part, "dp", scatter_dimension=0, tiled=True).astype(floats)
+    return attn_in_grad, gain_part, bias_part, qkv_out, out_out, layer_sum, (all_mid, rows_low)
 
 
 def rows_weights(qkv_weight, out_weight):
@@ -426,31 +445,6 @@
 
     vectors = [norm_attn, norm_ffn, shared_gate, qkv_bias]
     lengths = [vector.shape[0] for vector in vectors]
-    routing = [expert_ids[0].reshape(pairs), slot_order[0, 0], gate_weights[0].reshape(pairs)]
-    payload = jnp.concatenate([v.astype(floats) for v in vectors + routing])
-    payload = jnp.pad(payload, (0, -payload.shape[0] % 128))
-    small = spread(payload)
-    at = 0
-    gathered = []
-    for size in lengths:
-        gathered.append(small[:, at : at + size].reshape(-1))
-        at += size
-    gain_attn, gain_ffn, gate_vector, bias = gathered
-    small_own = lax.dynamic_index_in_dim(
-        small.reshape(count, devices // count, -1), place, 1, keepdims=False
-    )
-    routes = [small_own[:, at + i * pairs : at + (i + 1) * pairs] for i in range(3)]
-    pair_expert, pair_order, pair_gate = [r.reshape(count, tok_count, topk) for r in routes]
-
-    own_tokens = tokens[0]
-    resid_in = own_tokens.astype(floats)
-    if by_heads:
-        weights = head_weights(qkv_weight, out_weight)
-        all_tokens = group_gather(own_tokens)
-        mixed, saved = heads_forward(all_tokens, gain_attn, bias, weights, segments[0])
-    else:
-        weights = rows_weights(qkv_weight, out_weight)
-        mixed, saved = rows_forward(own_tokens, gain_attn, bias, weights, segments[0])
 
     def core_half(array, axis, which):
         size = array.shape[axis] // 2
@@ -463,16 +457,74 @@
         part = core_half(shared_gate_up, 2, which)
         return jnp.concatenate([part[0], part[1]], axis=-1)
 
-    expert_up = gather_weight(expert_of(expert_gate_up, core), expert_of(expert_gate_up, 1 - core))
-    expert_up = expert_up.reshape(width, -1)
-    expert_dn = gather_weight(expert_of(expert_down, core), expert_of(expert_down, 1 - core))
-    expert_dn = expert_dn.reshape(-1, width)
+    down_turned = shared_down.T
+
+    own_tokens = tokens[0]
+    resid_in = own_tokens.astype(floats)
+    ed_first = expert_of(expert_down, core)
+    ed_first = lax.all_gather(ed_first, "dp", axis=0)
+    ed_second = other_core(expert_of(expert_down, 1 - core))
+    su_both = both_cores(gate_up_half(core), gate_up_half(1 - core))
+    sd_both = both_cores(core_half(down_turned, 1, core), core_half(down_turned, 1, 1 - core))
+    eu_both = both_cores(expert_of(expert_gate_up, core), expert_of(expert_gate_up, 1 - core))
+
+    if by_heads:
+        cut = head_cut(qkv_weight, out_weight, vectors)
+        marks = (cut,)
+        all_tokens = lax.all_gather(after(own_tokens, cut), group, axis=0, tiled=True)
+        cut_x, cut_y = near_blocks(cut)
+        weights, gathered, previous = head_weights(
+            cut, cut_x, cut_y, (ed_second, su_both, sd_both, eu_both)
+        )
+    else:
+        weights = rows_weights(qkv_weight, out_weight)
+        payload = jnp.concatenate([vector.astype(floats) for vector in vectors])
+        payload = jnp.pad(payload, (0, -payload.shape[0] % 128))
+        small = spread(payload)
+        gathered = []
+        for at, size in enumerate(lengths):
+            first = sum(lengths[:at])
+            gathered.append(small[:, first : first + size].reshape(-1))
+        previous = marks = weights
+    gain_attn, gain_ffn, gate_vector, bias = gathered
+
+    routing = [expert_ids[0].reshape(pairs), slot_order[0, 0], gate_weights[0].reshape(pairs)]
+    routing = jnp.concatenate([v.astype(floats) for v in routing]).reshape(1, -1, 128)
+    routing = jnp.broadcast_to(routing, (count,) + routing.shape[1:])
+    routing = lax.all_to_all(after(routing, *marks), group, split_axis=0, concat_axis=0, tiled=True)
+    routing = routing.reshape(count, 3, tok_count, topk)
+    pair_expert, pair_order, pair_gate = routing[:, 0], routing[:, 1], routing[:, 2]
+
+    ed_second_x, ed_second_y = near_blocks(after(ed_second, *previous))
+    ed_split = ed_second.shape[0] // 32 * 16
+    ed_far = dp_step(ed_second_x[:ed_split], 2), dp_step(ed_second_y[ed_split:], 1)
+    ed_pin = (ed_second_x, ed_second_y) + ed_far
+    expert_up = gather_rows(eu_both)
+    if by_heads:
+        grads_line = gather_line(after(cotangent[0], all_tokens))
+        mixed, saved, marks = heads_forward(
+            all_tokens, gain_attn, bias, weights, segments[0], (grads_line,) + ed_pin
+        )
+        all_grads = gather_cores(after(grads_line, mixed))
+    else:
+        mixed, saved = rows_forward(own_tokens, gain_attn, bias, weights, segments[0])
+        all_grads = group_gather(cotangent[0])
+        marks = (mixed, mixed)
+    shared_up = gather_rows(after(su_both, marks[0]))
+    shared_dn = gather_rows(after(sd_both, marks[1]))
+    hidden_units = shared_dn.shape[1]
+    own_at = lambda out, at: out.at[at]
+    firsts = lambda out, at: out.at[pl.ds(at, 4)]
+    far_low = lambda out, at: out.at[at, pl.ds(0, ed_split)]
+    far_high = lambda out, at: out.at[at, pl.ds(ed_split, ed_second.shape[0] - ed_split)]
+    other_at = 4 - 4 * core
+    expert_dn = place_blocks(
+        [ed_first, ed_second, ed_second_x, ed_second_y, *ed_far],
+        [4 * core] + [other_at + (place ^ step) for step in (0, 1, 2, 3, 3)],
+        (8,) + ed_second.shape,
+        [firsts, own_at, own_at, own_at, far_low, far_high],
+    ).reshape(-1, width)
     ff_width = expert_dn.shape[0]
-    shared_up = gather_weight(gate_up_half(core), gate_up_half(1 - core)).reshape(width, -1)
-    down_turned = shared_down.T
-    shared_dn = gather_weight(core_half(down_turned, 1, core), core_half(down_turned, 1, 1 - core))
-    shared_dn = shared_dn.reshape(width, -1)
-    hidden_units = shared_dn.shape[1]
 
     resid_mid = resid_in + mixed
     stat_ffn = lax.rsqrt(jnp.mean(resid_mid * resid_mid, axis=-1, keepdims=True) + eps_norm)
@@ -480,9 +532,7 @@
     normed_ffn = (unit_ffn * gain_ffn).astype(halves)
     grad_out = cotangent[0].astype(floats)
 
-    all_grads = group_gather(cotangent[0])
     all_normed = group_gather(normed_ffn)
-
     chosen = pair_expert == index.astype(floats)
     has_pair = jnp.any(chosen, axis=-1)
     order = jnp.sum(jnp.where(chosen, pair_order, 0.0), axis=-1)
@@ -525,8 +575,10 @@
     ).astype(halves)
     expert_out = dot(expert_hidden, expert_dn).astype(halves)
     slot_in_grad = dot_nt(expert_pre_grad, expert_up).astype(halves)
-
-    shared_pre = dot(all_normed, shared_up)
+    eu_term = dot_tn(slot_in, expert_pre_grad).astype(halves)
+    ed_term = dot_tn(expert_hidden, slot_grad).astype(halves)
+
+    shared_pre = dot(after(all_normed, eu_term, ed_term), shared_up)
     shared_g, shared_u = shared_pre[:, :hidden_units], shared_pre[:, hidden_units:]
     shared_hidden = (jax.nn.silu(shared_g) * shared_u).astype(halves)
     gate_shared = jax.nn.sigmoid(
@@ -539,6 +591,8 @@
     ).astype(halves)
     shared_part = dot_nt(shared_hidden, shared_dn)
     logit_part = jnp.sum(all_grads.astype(floats) * shared_part, axis=-1)
+    su_term = dot_tn(all_normed, shared_pre_grad).astype(halves)
+    sd_term = dot_tn(shared_grad, shared_hidden).astype(halves)
 
     ffn_part = dot_nt(shared_pre_grad, shared_up) + from_slots(slot_in_grad)
     out_part = gate_shared * shared_part + gate.reshape(length, 1) * from_slots(expert_out)
@@ -550,79 +604,43 @@
         jnp.sum(normed_ffn.astype(floats) * gate_vector, axis=-1, keepdims=True)
     )
     logit_grad = jnp.sum(logit_sums, axis=0).reshape(tok_count, 1) * own_gate * (1.0 - own_gate)
-    ffn_grad = group_reduce(ffn_part) + logit_grad * gate_vector
+    ffn_grad = group_reduce(ffn_part)[0] + logit_grad * gate_vector
     unit_grad = ffn_grad * gain_ffn
     gain_ffn_part = jnp.sum(ffn_grad * unit_ffn, axis=0)
     gate_vector_part = jnp.sum(logit_grad * normed_ffn.astype(floats), axis=0)
     mid_grad = grad_out + stat_ffn * (
         unit_grad - unit_ffn * jnp.mean(unit_grad * unit_ffn, axis=-1, keepdims=True)
     )
-    mid_low = mid_grad.astype(halves)
-    layer_sum = resid_mid + group_reduce(out_part)
-
-    def block_of(array, crel, step):
-        size = width // 8
-        blk = (core ^ crel) * 4 + (place ^ step)
-        return lax.dynamic_slice_in_dim(array, blk * size, size, 1)
-
-    def reduce_blocks(block):
-        near, far = reduce_square(
-            [block(0, step) for step in range(4)], [block(1, step) for step in range(4)]
-        )
-        return near, other_core(far)
-
-    def in_order(near, far, axis):
-        return (
-            jnp.where(core == 0, near, far),
-            jnp.where(core == 0, far, near),
-        )
-
-    expert_down_term = dot_tn(expert_hidden, slot_grad).astype(halves)
-    expert_down_term = expert_down_term.reshape(8, -1, width)
-    expert_down_out = jnp.stack(
-        in_order(
-            *reduce_blocks(
-                lambda crel, step: lax.dynamic_index_in_dim(
-                    expert_down_term, (core ^ crel) * 4 + (place ^ step), 0, keepdims=False
-                )
-            ),
-            0,
-        )
-    )
-    expert_up_out = jnp.stack(
-        in_order(
-            *reduce_blocks(
-                lambda crel, step: dot_tn(block_of(slot_in, crel, step), expert_pre_grad).astype(halves)
-            ),
-            0,
-        )
-    )
-    lower, upper = in_order(
-        *reduce_blocks(
-            lambda crel, step: dot_tn(block_of(all_normed, crel, step), shared_pre_grad).astype(halves)
-        ),
-        0,
-    )
-    shared_up_out = jnp.concatenate(
-        [array.reshape(width // 8, 2, hidden_units).transpose(1, 0, 2) for array in (lower, upper)],
-        axis=-1,
-    )
-    lower, upper = in_order(
-        *reduce_blocks(
-            lambda crel, step: dot_tn(block_of(shared_grad, crel, step), shared_hidden).astype(halves)
-        ),
-        0,
-    )
-    shared_down_out = jnp.concatenate([lower, upper], axis=-1).T
+    mid_low = after(mid_grad.astype(halves), su_term, sd_term)
+
+    su_sum, sd_sum, eu_sum = sum_weight(su_term), sum_weight(sd_term), sum_weight(eu_term)
 
     if by_heads:
-        attn_in_grad, gain_attn_part, bias_part, qkv_out, out_weight_out = heads_backward(
-            all_tokens, gain_attn, weights, saved, mid_low
+        attn_in_grad, gain_attn_part, bias_part, qkv_out, out_weight_out, layer_sum, marks = heads_backward(
+            all_tokens, gain_attn, weights, saved, mid_low, (eu_sum, su_sum, sd_sum, out_part)
         )
     else:
         attn_in_grad, gain_attn_part, bias_part, qkv_out, out_weight_out = rows_backward(
             weights, saved, mid_low
         )
+        marks = (mid_low, attn_in_grad)
+        layer_sum = group_reduce(out_part)[0]
+    layer_sum = resid_mid + layer_sum
+    mark_end = marks[1]
+
+    ed_sum = sum_weight(after(ed_term, mark_end))
+    su_sum, sd_sum, eu_sum = (after(total, mark_end) for total in (su_sum, sd_sum, eu_sum))
+    shared_up_out = jnp.concatenate(
+        [
+            array.reshape(width // 8, 2, hidden_units).transpose(1, 0, 2)
+            for array in cores_in_order(su_sum)
+        ],
+        axis=-1,
+    ).astype(floats)
+    shared_down_out = jnp.concatenate(cores_in_order(sd_sum), axis=-1).T.astype(floats)
+    expert_up_out = jnp.stack(cores_in_order(eu_sum)).astype(floats)
+    expert_down_out = jnp.stack(cores_in_order(ed_sum)).astype(floats)
+
     stat_attn = lax.rsqrt(jnp.mean(resid_in * resid_in, axis=-1, keepdims=True) + eps_norm)
     unit_attn = resid_in * stat_attn
     unit_grad = attn_in_grad * gain_attn
@@ -633,7 +651,7 @@
     parts = [gain_attn_part, gain_ffn_part, gate_vector_part, bias_part]
     packed = jnp.concatenate([part.reshape(devices, -1) for part in parts], axis=1)
     total = packed.shape[1]
-    packed = jnp.pad(packed, ((0, 0), (0, -total % 128)))
+    packed = jnp.pad(after(packed, mark_end), ((0, 0), (0, -total % 128)))
     packed = lax.all_to_all(
         packed.reshape(devices, -1, 128), every, split_axis=0, concat_axis=0, tiled=True
     )

time: 1250 us -> 828 us (0.66); the launches traced: 1230 us -> 822 us
  local copies, waits for them, and re-layouts: 295 us -> 95.3 us
  starting transfers between devices: 191 us -> 67.4 us
  waiting for transfers between devices: 439 us -> 339 us
    all_to_all x2 -> x9, waiting for transfers between devices: 0.01 us -> 258 us  [the longest x7 233 us: along_expert(): lax.all_to_all(blocks, 'expert', split_axis=0, concat_axis=0, tiled=True)]
    ppermute x72 -> x8, waiting for transfers between devices: 259 us -> 42.7 us  [dp_step(): return lax.ppermute(value, 'dp', [(i, i ^ step) for i in range(count)])]
    ppermute x32 -> x0, waiting for transfers between devices: 179 us -> none  [the longest x4 78.9 us: group_reduce(): second = lax.ppermute(passed, 'expert', [(0, 2), (1, 3), (2, 0), (3, 1)])]
    dynamic_update_slice x47 -> x0, local copies, waits for them, and re-layouts: 161 us -> none  [the longest x16 78.4 us: gather_weight(): lax.dynamic_update_slice(out, far[step][None, None], (1 - core, place ^ s...]
    ppermute x32 -> x0, starting transfers between devices: 86.8 us -> none  [the longest x4 24.3 us: group_reduce(): second = lax.ppermute(passed, 'expert', [(0, 2), (1, 3), (2, 0), (3, 1)])]
    ppermute x72 -> x8, starting transfers between devices: 75.2 us -> 11.3 us  [dp_step(): return lax.ppermute(value, 'dp', [(i, i ^ step) for i in range(count)])]
    all_to_all x2 -> x9, starting transfers between devices: 10.9 us -> 42.2 us  [the longest x7 32.6 us: along_expert(): lax.all_to_all(blocks, 'expert', split_axis=0, concat_axis=0, tiled=True)]
    dot_general x27 -> x6, matrix products: 73 us -> 42.3 us  [dot_tn(): lax.dot_general(left, right, (((0,), (0,)), ((), ())), preferred_element_...]
  transfers between devices with their start and end apart: 125 -> 46, of which waited for: 52 -> 20; matrix products, arithmetic and copies ran while one was open for 37% -> 45% of each run, Pallas kernels for 0% -> 1%
where the time goes in v2:
time: 828 us; the launch traced here: 822 us
  waiting for transfers between devices  339 us (41%)
  matrix products  180 us (22%)
  other arithmetic  119 us (14%)
  local copies, waits for them, and re-layouts  95.3 us (12%)
  starting transfers between devices  67.4 us (8%)
  between operations  15.7 us (2%)
    all_to_all x7, waiting for transfers between devices, along_expert(): lax.all_to_all(blocks, 'expert', split_axis=0, concat_axis=0, tiled=True)  233 us
    dot_general x6, matrix products, dot(): return jnp.dot(left, right, preferred_element_type=floats)  55 us
    dot_general x6, matrix products, dot_nt(): lax.dot_general(left, right, (((1,), (1,)), ((), ())), preferred_element_...  50 us
    ppermute x8, waiting for transfers between devices, dp_step(): return lax.ppermute(value, 'dp', [(i, i ^ step) for i in range(count)])  42.7 us
    dot_general x6, matrix products, dot_tn(): lax.dot_general(left, right, (((0,), (0,)), ((), ())), preferred_element_...  42.3 us
    all_to_all x7, starting transfers between devices, along_expert(): lax.all_to_all(blocks, 'expert', split_axis=0, concat_axis=0, tiled=True)  32.6 us
    unnamed x208, local copies, waits for them, and re-layouts  24.6 us
    all_to_all x1, waiting for transfers between devices, head_cut(): cut = lax.all_to_all(cut, group, split_axis=0, concat_axis=0, tiled=True)  22.1 us
  transfers between devices with their start and end apart: 46, of which 20 were waited for; matrix products, arithmetic and copies ran while one was open for 45% of the time, Pallas kernels for 1%

profile of v2, /device:TPU:0, one launch (start us, length us, event | category | flops | bytes accessed | tf_op | source)
XLA Modules:
  0.0 822.3 jit_solution(15684709301223767507)
XLA Ops:
  12.5 6.3 all-to-all-start
  20.5 22.1 %all-to-all-done = bf16[8,64,896]{2,1,0:T(8,128)(2,1)S(1)} async-done(((bf16[8,64,896]{2,1,0:T(8,128)(2,1)}), bf16[8,64,896]{2,1,0:T(8,128)(2,1)S(1)}, u32[]{:S(2)}, u32[]{:S(2)}) %all-to-all-start) | async-done | bytes 917536 | tf_op jit(solution)/shard_map/all_to_all | solution.py:199
  66.9 19.9 %collective-permute-done.1.refs_2_ = bf16[8,64,1152]{2,1,0:T(8,128)(2,1)S(1)} collective-permute-done((bf16[8,64,1152]{2,1,0:T(8,128)(2,1)S(1)}, bf16[8,64,1152]{2,1,0:T(8,128)(2,1)S(1)}, u32[]{:S(2)}, u32[]{:S(2)}) %collective-permute-start.1) | collective-permute-done | bytes 1179680 | tf_op jit(solution)/shard_map/ppermute | solution.py:75
  94.6 10.4 %collective-permute-done.6.refs_3_ = bf16[4,64,1152]{2,1,0:T(8,128)(2,1)S(1)} collective-permute-done((bf16[4,64,1152]{2,1,0:T(8,128)(2,1)S(1)}, bf16[4,64,1152]{2,1,0:T(8,128)(2,1)S(1)}, u32[]{:S(2)}, u32[]{:S(2)}) %collective-permute-start.6) | collective-permute-done | bytes 589856 | tf_op jit(solution)/shard_map/ppermute | solution.py:75
  122.3 8.6 %collective-permute-done.9.refs_3_ = bf16[176,2048]{1,0:T(8,128)(2,1)} collective-permute-done((bf16[176,2048]{1,0:T(8,128)(2,1)}, bf16[176,2048]{1,0:T(8,128)(2,1)}, u32[]{:S(2)}, u32[]{:S(2)}) %collective-permute-start.9) | collective-permute-done | bytes 720928 | tf_op jit(solution)/shard_map/ppermute | solution.py:75
  146.9 5.7 convolution_add_fusion
  159.8 5.2 fusion.83
  165.0 13.1 %fusion.97 = (f32[2,1024]{1,0:T(2,128)S(1)}, f32[2,1024,1024]{1,2,0:T(8,128)}) fusion(f32[2,1024,1024]{1,2,0:T(8,128)} %fusion.83, pred[1024,1024]{0,1:T(8,128)(4,1)S(1)} %copy-done.47), kind=kOutput, calls=%fused_computation.248 | output fusion | flops 8389631 | bytes 17833984 | tf_op jit(solution)/shard_map/sub | solution.py:249
  182.7 14.3 %fusion.98 = f32[1024,2048]{1,0:T(8,128)} fusion(bf16[1024,256]{0,1:T(8,128)(2,1)S(1)} %bitcast.388, bf16[256,2048]{1,0:T(8,128)(2,1)S(1)} %bitcast.357), kind=kOutput, calls=%fused_computation.249 | convolution fusion | flops 1073741824 | bytes 9961472 | tf_op jit(solution)/shard_map/dot_general | solution.py:62
  215.0 46.7 %all-to-all-done.2 = bf16[4,128,2048]{2,1,0:T(8,128)(2,1)S(1)} async-done(((bf16[4,128,2048]{2,1,0:T(8,128)(2,1)}), bf16[4,128,2048]{2,1,0:T(8,128)(2,1)S(1)}, u32[]{:S(2)}, u32[]{:S(2)}) %all-to-all-start.2) | async-done | bytes 2097184 | tf_op jit(solution)/shard_map/all_to_all | solution.py:155
  281.4 43.1 %all-to-all-done.3 = bf16[4,128,2048]{2,1,0:T(8,128)(2,1)S(1)} async-done(((bf16[4,128,2048]{2,1,0:T(8,128)(2,1)}), bf16[4,128,2048]{2,1,0:T(8,128)(2,1)S(1)}, u32[]{:S(2)}, u32[]{:S(2)}) %all-to-all-start.3) | async-done | bytes 2097184 | tf_op jit(solution)/shard_map/all_to_all | solution.py:155
  351.9 11.2 %fusion.99 = f32[576,2816]{1,0:T(8,128)S(1)} fusion(bf16[576,2048]{1,0:T(8,128)(2,1)} %bitcast.375, bf16[2048,2816]{1,0:T(8,128)(2,1)} %bitcast.401), kind=kOutput, calls=%fused_computation.250 | convolution fusion | flops 6643777536 | bytes 20381696 | tf_op jit(solution)/shard_map/dot_general | solution.py:62
  363.2 6.3 multiply_convert_fusion.5
  369.5 12.2 %convolution_convert_fusion = bf16[2048,2816]{1,0:T(8,128)(2,1)} fusion(bf16[576,2048]{1,0:T(8,128)(2,1)S(1)} %bitcast.376, bf16[576,1408]{1,0:T(8,128)(2,1)S(1)} %get-tuple-element.153, bf16[576,1408]{1,0:T(8,128)(2,1)S(1)} %get-tuple-element.152), kind=kOutput, calls=%fused_computation.1 | convolution fusion | flops 6656032768 | bytes 17137664 | tf_op jit(solution)/shard_map/dot_general | solution.py:66
  384.2 9.7 %copy.320 = f32[4,2,128,2048]{3,2,1,0:T(8,128)} copy(f32[4,2,128,2048]{3,2,0,1:T(8,128)} %get-tuple-element.167) | data formatting | bytes 16777216 | tf_op jit(solution)/shard_map/convert_element_type | solution.py:587
  402.1 6.5 convolution_convert_fusion.2
  408.6 8.7 %convolution_convert_fusion.5 = bf16[576,2048]{1,0:T(8,128)(2,1)S(1)} fusion(bf16[2048,2816]{1,0:T(8,128)(2,1)S(1)} %bitcast.404, bf16[576,1408]{1,0:T(8,128)(2,1)} %copy-done.84, bf16[576,1408]{1,0:T(8,128)(2,1)S(1)} %copy-done.83), kind=kOutput, calls=%fused_computation.64 | convolution fusion | flops 6651445248 | bytes 17137664 | tf_op jit(solution)/shard_map/dot_general | solution.py:70
  422.0 12.0 %fusion.100 = f32[1024,1408]{1,0:T(8,128)} fusion(bf16[1024,2048]{1,0:T(8,128)(2,1)} %bitcast.333, bf16[2048,1408]{1,0:T(8,128)(2,1)} %bitcast.405), kind=kOutput, calls=%fused_computation.251 | convolution fusion | flops 5905580032 | bytes 15728640 | tf_op jit(solution)/shard_map/dot_general | solution.py:62
  434.1 7.6 multiply_convert_fusion.7
  441.7 11.9 %bitcast_add_fusion = f32[1024,2048]{1,0:T(8,128)} fusion(f32[8,128,2048]{2,1,0:T(8,128)S(1)} %bitcast.345, bf16[2048,1408]{1,0:T(8,128)(2,1)} %bitcast.406, bf16[1024,704]{1,0:T(8,128)(2,1)S(1)} %get-tuple-element.155, bf16[1024,704]{1,0:T(8,128)(2,1)S(1)} %get-tuple-element.154), kind=kOutput, calls=%fused_computation.13 | convolution fusion | flops 5913444352 | bytes 25427968 | tf_op jit(solution)/shard_map/dot_general | solution.py:70
  462.2 10.3 %fusion.7 = (bf16[1024,2048]{1,0:T(8,128)(2,1)}, f32[1024]{0:T(1024)}, f32[1024,2048]{1,0:T(8,128)}) fusion(f32[4,2,128,2048]{3,2,1,0:T(8,128)S(1)} %bitcast.325, f32[1024]{0:T(1024)S(1)} %bitcast.392, f32[8,128,2048]{2,1,0:T(8,128)S(1)} %fusion.65, f32[1024]{0:T(1024)S(1)} %copy-done.59, bf16[1024,704]{1,0:T(8,128)(2,1)} %get-tuple-element.160, ...), kind=kOutput, calls=%fused_computation.12 | convolution fusion | flops 2967469056 | bytes 33697792 | tf_op jit(solution)/shard_map/dot_general | solution.py:70
  475.9 6.2 convolution_convert_fusion.4
  489.1 5.5 all-to-all-start.5
  494.9 10.8 %convolution_convert_fusion.1 = bf16[2048,1408]{1,0:T(8,128)(2,1)} fusion(bf16[1024,2048]{1,0:T(8,128)(2,1)} %bitcast.334, bf16[1024,704]{1,0:T(8,128)(2,1)} %copy-done.81, bf16[1024,704]{1,0:T(8,128)(2,1)S(1)} %copy-done.80), kind=kOutput, calls=%fused_computation.21 | convolution fusion | flops 5914230784 | bytes 12845056 | tf_op jit(solution)/shard_map/dot_general | solution.py:66
  505.7 37.4 %all-to-all-done.5 = bf16[4,128,2048]{2,1,0:T(8,128)(2,1)} async-done(((bf16[4,128,2048]{2,1,0:T(8,128)(2,1)}), bf16[4,128,2048]{2,1,0:T(8,128)(2,1)}, u32[]{:S(2)}, u32[]{:S(2)}) %all-to-all-start.5) | async-done | bytes 2097184 | tf_op jit(solution)/shard_map/all_to_all | solution.py:155
  553.6 47.0 %all-to-all-done.7 = bf16[4,128,2048]{2,1,0:T(8,128)(2,1)} async-done(((bf16[4,128,2048]{2,1,0:T(8,128)(2,1)}), bf16[4,128,2048]{2,1,0:T(8,128)(2,1)}, u32[]{:S(2)}, u32[]{:S(2)}) %all-to-all-start.7) | async-done | bytes 2097184 | tf_op jit(solution)/shard_map/all_to_all | solution.py:155
  608.4 5.8 fusion.22
  648.2 11.5 %fusion.4 = (f32[2048]{0:T(1024)S(1)}, f32[1024,2048]{1,0:T(8,128)}) fusion(bf16[1024,2048]{1,0:T(8,128)(2,1)} %all-gather.6.cloned.1.call-done, f32[1024]{0:T(1024)S(1)} %copy-done.69, bf16[1024,768]{0,1:T(8,128)(2,1)} %copy-done.44, bf16[2048,768]{1,0:T(8,128)(2,1)} %bitcast.366), kind=kOutput, calls=%fused_computation.7 | convolution fusion | flops 3229612032 | bytes 17313792 | tf_op jit(solution)/shard_map/dot_general | solution.py:70
  659.7 37.5 %all-to-all-done.8 = bf16[4,128,2048]{2,1,0:T(8,128)(2,1)} async-done(((bf16[4,128,2048]{2,1,0:T(8,128)(2,1)}), bf16[4,128,2048]{2,1,0:T(8,128)(2,1)}, u32[]{:S(2)}, u32[]{:S(2)}) %all-to-all-start.8) | async-done | bytes 2097184 | tf_op jit(solution)/shard_map/all_to_all | solution.py:155
  720.1 7.5 all-to-all-done.11
  739.7 12.3 %all-to-all-done.10 = bf16[8,64,768]{2,1,0:T(8,128)(2,1)S(1)} async-done(((bf16[8,64,768]{2,1,0:T(8,128)(2,1)}), bf16[8,64,768]{2,1,0:T(8,128)(2,1)S(1)}, u32[]{:S(2)}, u32[]{:S(2)}) %all-to-all-start.10) | async-done | bytes 786464 | tf_op jit(solution)/shard_map/all_to_all | solution.py:302
  784.1 20.9 %all-to-all-done.9 = bf16[4,128,2048]{2,1,0:T(8,128)(2,1)} async-done(((bf16[4,128,2048]{2,1,0:T(8,128)(2,1)}), bf16[4,128,2048]{2,1,0:T(8,128)(2,1)}, u32[]{:S(2)}, u32[]{:S(2)}) %all-to-all-start.9) | async-done | bytes 2097184 | tf_op jit(solution)/shard_map/all_to_all | solution.py:155
  (464 shorter events, 312.4 us)
Async XLA Ops:
  12.5 30.1 %all-to-all-start = ((bf16[8,64,896]{2,1,0:T(8,128)(2,1)}), bf16[8,64,896]{2,1,0:T(8,128)(2,1)S(1)}, u32[]{:S(2)}, u32[]{:S(2)}) async-start(bf16[8,64,896]{2,1,0:T(8,128)(2,1)} %pad_maximum_fusion.13), calls=%async_computation | async-start | bytes 1835008 | tf_op jit(solution)/shard_map/all_to_all | solution.py:199
  18.8 118.3 %all-gather.6.cloned.1.call-start = ((), (), s32[]{:S(2)}) async-start(), calls=%async_computation.18 | async-start | bytes 4718592 | tf_op jit(solution)/shard_map/all_gather | solution.py:474
  43.7 281.7 %all-gather.8.cloned.1.call-start = ((), (), s32[]{:S(2)}) async-start(), calls=%async_computation.19 | async-start | bytes 3604480 | tf_op jit(solution)/shard_map/all_gather | solution.py:465
  45.0 307.0 %all-gather.10.cloned.1.call-start = ((), (), s32[]{:S(2)}) async-start(), calls=%async_computation.20 | async-start | bytes 14417920 | tf_op jit(solution)/shard_map/all_gather | solution.py:143
  58.3 28.6 %collective-permute-start.2 = (bf16[176,2048]{1,0:T(8,128)(2,1)}, bf16[176,2048]{1,0:T(8,128)(2,1)}, u32[]{:S(2)}, u32[]{:S(2)}) collective-permute-start(bf16[176,2048]{1,0:T(8,128)(2,1)} %get-tuple-element.192), channel_id=1, source_target_pairs={{0,4},{4,0},{1,5},{5,1},{2,6},{6,2},{3,7},{7,3},{8,12},{12,8},{9,1... | collective-permute-start | bytes 2162696 | tf_op jit(solution)/shard_map/ppermute | solution.py:79
  58.8 28.0 %collective-permute-start.1 = (bf16[8,64,1152]{2,1,0:T(8,128)(2,1)S(1)}, bf16[8,64,1152]{2,1,0:T(8,128)(2,1)S(1)}, u32[]{:S(2)}, u32[]{:S(2)}) collective-permute-start(bf16[8,64,1152]{2,1,0:T(8,128)(2,1)S(1)} %pad_maximum_fusion.12.refs_0_), channel_id=1, source_target_pairs={{0,2},{1,3},{2,0},{3,1},{4,6},{5,7},{6,4},{7,5},{8,10},{9,11},{10,... | collective-permute-start | bytes 3538952 | tf_op jit(solution)/shard_map/ppermute | solution.py:75
  60.2 27.7 %collective-permute-start = (bf16[8,64,1152]{2,1,0:T(8,128)(2,1)S(1)}, bf16[8,64,1152]{2,1,0:T(8,128)(2,1)S(1)}, u32[]{:S(2)}, u32[]{:S(2)}) collective-permute-start(bf16[8,64,1152]{2,1,0:T(8,128)(2,1)S(1)} %pad_maximum_fusion.12.refs_0_), channel_id=1, source_target_pairs={{0,1},{1,0},{2,3},{3,2},{4,5},{5,4},{6,7},{7,6},{8,9},{9,8},{10,11... | collective-permute-start | bytes 3538952 | tf_op jit(solution)/shard_map/ppermute | solution.py:75
  107.8 23.1 %collective-permute-start.9 = (bf16[176,2048]{1,0:T(8,128)(2,1)}, bf16[176,2048]{1,0:T(8,128)(2,1)}, u32[]{:S(2)}, u32[]{:S(2)}) collective-permute-start(bf16[176,2048]{1,0:T(8,128)(2,1)} %collective-permute-done.2.refs_1_), channel_id=1, source_target_pairs={{0,2},{1,3},{2,0},{3,1},{4,6},{5,7},{6,4},{7,5},{8,10},{9,11},{10,... | collective-permute-start | bytes 2162696 | tf_op jit(solution)/shard_map/ppermute | solution.py:75
  108.9 25.6 %collective-permute-start.8 = (bf16[176,2048]{1,0:T(8,128)(2,1)}, bf16[176,2048]{1,0:T(8,128)(2,1)}, u32[]{:S(2)}, u32[]{:S(2)}) collective-permute-start(bf16[176,2048]{1,0:T(8,128)(2,1)} %collective-permute-done.2.refs_1_), channel_id=1, source_target_pairs={{0,1},{1,0},{2,3},{3,2},{4,5},{5,4},{6,7},{7,6},{8,9},{9,8},{10,11... | collective-permute-start | bytes 2162696 | tf_op jit(solution)/shard_map/ppermute | solution.py:75
  132.6 64.4 %collective-permute-start.11 = (bf16[96,2048]{1,0:T(8,128)(2,1)}, bf16[96,2048]{1,0:T(8,128)(2,1)S(1)}, u32[]{:S(2)}, u32[]{:S(2)}) collective-permute-start(bf16[96,2048]{1,0:T(8,128)(2,1)} %slice.204), channel_id=1, source_target_pairs={{0,1},{1,0},{2,3},{3,2},{4,5},{5,4},{6,7},{7,6},{8,9},{9,8},{10,11... | collective-permute-start | bytes 1179656 | tf_op jit(solution)/shard_map/ppermute | solution.py:75
  136.2 60.8 %collective-permute-start.10 = (bf16[80,2048]{1,0:T(8,128)(2,1)}, bf16[80,2048]{1,0:T(8,128)(2,1)S(1)}, u32[]{:S(2)}, u32[]{:S(2)}) collective-permute-start(bf16[80,2048]{1,0:T(8,128)(2,1)} %slice.203), channel_id=1, source_target_pairs={{0,2},{1,3},{2,0},{3,1},{4,6},{5,7},{6,4},{7,5},{8,10},{9,11},{10,... | collective-permute-start | bytes 983048 | tf_op jit(solution)/shard_map/ppermute | solution.py:75
  138.8 58.3 %all-to-all-start.1 = ((bf16[4,128,2048]{2,1,0:T(8,128)(2,1)}), bf16[4,128,2048]{2,1,0:T(8,128)(2,1)}, u32[]{:S(2)}, u32[]{:S(2)}) async-start(bf16[4,128,2048]{2,1,0:T(8,128)(2,1)} %broadcast_in_dim.46), calls=%async_computation.1 | async-start | bytes 4194304 | tf_op jit(solution)/shard_map/all_to_all | solution.py:155
  208.1 53.6 %all-to-all-start.2 = ((bf16[4,128,2048]{2,1,0:T(8,128)(2,1)}), bf16[4,128,2048]{2,1,0:T(8,128)(2,1)S(1)}, u32[]{:S(2)}, u32[]{:S(2)}) async-start(bf16[4,128,2048]{2,1,0:T(8,128)(2,1)} %fusion.16), calls=%async_computation.2 | async-start | bytes 4194304 | tf_op jit(solution)/shard_map/all_to_all | solution.py:155
  213.3 168.6 %all-gather.14.cloned.1.call-start = ((), (), s32[]{:S(2)}) async-start(), calls=%async_computation.22 | async-start | bytes 3604480 | tf_op jit(solution)/shard_map/all_gather | solution.py:143
  272.6 51.9 %all-to-all-start.3 = ((bf16[4,128,2048]{2,1,0:T(8,128)(2,1)}), bf16[4,128,2048]{2,1,0:T(8,128)(2,1)S(1)}, u32[]{:S(2)}, u32[]{:S(2)}) async-start(bf16[4,128,2048]{2,1,0:T(8,128)(2,1)} %broadcast_in_dim.48), calls=%async_computation.3 | async-start | bytes 4194304 | tf_op jit(solution)/shard_map/all_to_all | solution.py:155
  276.2 145.8 %all-gather.12.cloned.1.call-start = ((), (), s32[]{:S(2)}) async-start(), calls=%async_computation.21 | async-start | bytes 7208960 | tf_op jit(solution)/shard_map/all_gather | solution.py:143
  276.3 54.1 %collective-permute-start.14 = (bf16[4,128,2048]{2,1,0:T(8,128)(2,1)}, bf16[4,128,2048]{2,1,0:T(8,128)(2,1)}, u32[]{:S(2)}, u32[]{:S(2)}) collective-permute-start(bf16[4,128,2048]{2,1,0:T(8,128)(2,1)} %all-to-all-done.1), channel_id=1, source_target_pairs={{0,4},{4,0},{1,5},{5,1},{2,6},{6,2},{3,7},{7,3},{8,12},{12,8},{9,1... | collective-permute-start | bytes 6291464 | tf_op jit(solution)/shard_map/ppermute | solution.py:79
  276.8 323.8 %reduce-scatter.7.cloned.1.call-start = ((), (), s32[]{:S(2)}) async-start(), calls=%async_computation.23 | async-start | bytes 14417920 | tf_op jit(solution)/shard_map/reduce_scatter | solution.py:131
  456.2 27.8 %collective-permute-start.15 = (bf16[4,128,2048]{2,1,0:T(8,128)(2,1)S(1)}, bf16[4,128,2048]{2,1,0:T(8,128)(2,1)}, u32[]{:S(2)}, u32[]{:S(2)}) collective-permute-start(bf16[4,128,2048]{2,1,0:T(8,128)(2,1)S(1)} %fusion.21), channel_id=1, source_target_pairs={{0,4},{4,0},{1,5},{5,1},{2,6},{6,2},{3,7},{7,3},{8,12},{12,8},{9,1... | collective-permute-start | bytes 6291464 | tf_op jit(solution)/shard_map/ppermute | solution.py:79
  475.8 172.3 %reduce-scatter.11.cloned.1.call-start = ((), (), s32[]{:S(2)}) async-start(), calls=%async_computation.25 | async-start | bytes 3604480 | tf_op jit(solution)/shard_map/reduce_scatter | solution.py:131
  489.1 54.0 %all-to-all-start.5 = ((bf16[4,128,2048]{2,1,0:T(8,128)(2,1)}), bf16[4,128,2048]{2,1,0:T(8,128)(2,1)}, u32[]{:S(2)}, u32[]{:S(2)}) async-start(bf16[4,128,2048]{2,1,0:T(8,128)(2,1)} %fusion.15), calls=%async_computation.5 | async-start | bytes 4194304 | tf_op jit(solution)/shard_map/all_to_all | solution.py:155
  548.3 52.3 %all-to-all-start.7 = ((bf16[4,128,2048]{2,1,0:T(8,128)(2,1)}), bf16[4,128,2048]{2,1,0:T(8,128)(2,1)}, u32[]{:S(2)}, u32[]{:S(2)}) async-start(bf16[4,128,2048]{2,1,0:T(8,128)(2,1)} %broadcast_in_dim.58), calls=%async_computation.7 | async-start | bytes 4194304 | tf_op jit(solution)/shard_map/all_to_all | solution.py:155
  552.8 95.4 %reduce-scatter.9.cloned.1.call-start = ((), (), s32[]{:S(2)}) async-start(), calls=%async_computation.24 | async-start | bytes 7208960 | tf_op jit(solution)/shard_map/reduce_scatter | solution.py:131
  553.5 166.6 %reduce-scatter.13.cloned.1.call-start = ((), (), s32[]{:S(2)}) async-start(), calls=%async_computation.26 | async-start | bytes 3932160 | tf_op jit(solution)/shard_map/reduce_scatter | solution.py:299
  614.3 24.3 %collective-permute-start.17 = (bf16[4,128,2048]{2,1,0:T(8,128)(2,1)}, bf16[4,128,2048]{2,1,0:T(8,128)(2,1)}, u32[]{:S(2)}, u32[]{:S(2)}) collective-permute-start(bf16[4,128,2048]{2,1,0:T(8,128)(2,1)} %fusion.22), channel_id=1, source_target_pairs={{0,4},{4,0},{1,5},{5,1},{2,6},{6,2},{3,7},{7,3},{8,12},{12,8},{9,1... | collective-permute-start | bytes 6291464 | tf_op jit(solution)/shard_map/ppermute | solution.py:79
  643.5 53.7 %all-to-all-start.8 = ((bf16[4,128,2048]{2,1,0:T(8,128)(2,1)}), bf16[4,128,2048]{2,1,0:T(8,128)(2,1)}, u32[]{:S(2)}, u32[]{:S(2)}) async-start(bf16[4,128,2048]{2,1,0:T(8,128)(2,1)} %fusion.14), calls=%async_computation.9 | async-start | bytes 4194304 | tf_op jit(solution)/shard_map/all_to_all | solution.py:155
  647.9 86.7 %reduce-scatter.15.cloned.1.call-start = ((), (), s32[]{:S(2)}) async-start(), calls=%async_computation.27 | async-start | bytes 1310720 | tf_op jit(solution)/shard_map/reduce_scatter | solution.py:307
  706.5 101.9 %reduce-scatter.17.cloned.1.call-start = ((), (), s32[]{:S(2)}) async-start(), calls=%async_computation.28 | async-start | bytes 7208960 | tf_op jit(solution)/shard_map/reduce_scatter | solution.py:131
  727.6 24.5 %all-to-all-start.10 = ((bf16[8,64,768]{2,1,0:T(8,128)(2,1)}), bf16[8,64,768]{2,1,0:T(8,128)(2,1)S(1)}, u32[]{:S(2)}, u32[]{:S(2)}) async-start(bf16[8,64,768]{2,1,0:T(8,128)(2,1)} %bitcast.387), calls=%async_computation.14 | async-start | bytes 1572864 | tf_op jit(solution)/shard_map/all_to_all | solution.py:302
  738.3 29.1 %collective-permute-start.20 = (bf16[256,704]{0,1:T(8,128)(2,1)}, bf16[256,704]{0,1:T(8,128)(2,1)}, u32[]{:S(2)}, u32[]{:S(2)}) collective-permute-start(bf16[256,704]{0,1:T(8,128)(2,1)} %select_bitcast_fusion.11), channel_id=1, source_target_pairs={{0,4},{4,0},{1,5},{5,1},{2,6},{6,2},{3,7},{7,3},{8,12},{12,8},{9,1... | collective-permute-start | bytes 1081352 | tf_op jit(solution)/shard_map/ppermute | solution.py:79
  739.2 30.4 %collective-permute-start.19 = (bf16[256,1408]{1,0:T(8,128)(2,1)}, bf16[256,1408]{1,0:T(8,128)(2,1)}, u32[]{:S(2)}, u32[]{:S(2)}) collective-permute-start(bf16[256,1408]{1,0:T(8,128)(2,1)} %select_bitcast_fusion.8), channel_id=1, source_target_pairs={{0,4},{4,0},{1,5},{5,1},{2,6},{6,2},{3,7},{7,3},{8,12},{12,8},{9,1... | collective-permute-start | bytes 2162696 | tf_op jit(solution)/shard_map/ppermute | solution.py:79
  752.0 53.0 %all-to-all-start.9 = ((bf16[4,128,2048]{2,1,0:T(8,128)(2,1)}), bf16[4,128,2048]{2,1,0:T(8,128)(2,1)}, u32[]{:S(2)}, u32[]{:S(2)}) async-start(bf16[4,128,2048]{2,1,0:T(8,128)(2,1)} %fusion.13), calls=%async_computation.12 | async-start | bytes 4194304 | tf_op jit(solution)/shard_map/all_to_all | solution.py:155
  (114 other events, 1230.3 us)
Sparse Core Ops, SparseCore 0:
  43.8 46.0 all-gather.5
  91.7 57.8 all-gather.7
  152.0 112.9 all-gather.9
  266.7 41.6 all-gather.13
  310.7 65.7 all-gather.11
  381.8 111.2 reduce-scatter.6
  496.8 41.6 reduce-scatter.10
  557.2 68.0 reduce-scatter.8
  638.7 43.8 reduce-scatter.12
  706.7 27.9 reduce-scatter.14
  737.9 65.8 reduce-scatter.16

commit v3 on v2

v3 whole, which is shorter than its diff:
```python
import math

import jax
import jax.numpy as jnp
from jax import lax
from jax.experimental import pallas as pl
from jax.experimental.pallas import tpu as pltpu
from jax.sharding import PartitionSpec as P

HEADS = 16
HEAD_DIM = 128


eps_norm = 1e-06
neg_fill = -1e30
rope_base = 1000000.0
group_heads = 4
floats = jnp.float32
halves = jnp.bfloat16
every = ("expert", "context", "dp")
group = ("expert", "context")
cost_scale = 0.0


def rope_tables(positions, half):
    inverse = jnp.exp(
        jnp.arange(half).astype(jnp.float32) * (-2.0 * math.log(rope_base) / (2 * half))
    )
    angle = positions.astype(jnp.float32)[:, None] * inverse[None, :]
    return (jnp.cos(angle), jnp.sin(angle))


def rotate(values, cosine, sine):
    half = values.shape[-1] // 2
    front = values[..., :half]
    behind = values[..., half:]
    cosine = cosine[:, None, :]
    sine = sine[:, None, :]
    return jnp.concatenate(
        [front * cosine - behind * sine, behind * cosine + front * sine], axis=-1
    )


def rotate_back(grads, cosine, sine):
    half = grads.shape[-1] // 2
    front = grads[..., :half]
    behind = grads[..., half:]
    cosine = cosine[:, None, :]
    sine = sine[:, None, :]
    return jnp.concatenate(
        [front * cosine + behind * sine, behind * cosine - front * sine], axis=-1
    )


def silu_parts(grad_hidden, gate_pre, up_pre):
    sigma = jax.nn.sigmoid(gate_pre)
    gate_grad = grad_hidden * up_pre * sigma * (1.0 + gate_pre * (1.0 - sigma))
    up_grad = grad_hidden * gate_pre * sigma
    return (gate_grad, up_grad)


def dot(left, right):
    return jnp.dot(left, right, preferred_element_type=floats)


def dot_tn(left, right):
    return lax.dot_general(left, right, (((0,), (0,)), ((), ())), preferred_element_type=floats)


def dot_nt(left, right):
    return lax.dot_general(left, right, (((1,), (1,)), ((), ())), preferred_element_type=floats)


def dp_step(value, step):
    count = lax.axis_size("dp")
    return lax.ppermute(value, "dp", [(i, i ^ step) for i in range(count)])


def other_core(value):
    return lax.ppermute(value, "context", [(0, 1), (1, 0)])


def after(value, *others):
    return lax.optimization_barrier((value,) + others)[0]


def near_blocks(block):
    return dp_step(block, 1), dp_step(block, 2)


def place_blocks(pieces, places, out_shape, views, window):
    at, size = window

    count = len(pieces)

    def kernel(place_ref, *refs):
        blocks, out, held = refs[:count], refs[count], refs[count + 1 : 2 * count + 1]
        in_sems, out_sems = refs[2 * count + 1 :]
        loads = [
            pltpu.make_async_copy(blocks[i].at[..., pl.ds(at, size)], held[i], in_sems.at[i])
            for i in range(count)
        ]
        stores = [
            pltpu.make_async_copy(held[i], views[i](out, place_ref[i]), out_sems.at[i])
            for i in range(count)
        ]
        for load in loads:
            load.start()
        for load, store in zip(loads, stores):
            load.wait()
            store.start()
        for store in stores:
            store.wait()

    return pl.pallas_call(
        kernel,
        out_shape=jax.ShapeDtypeStruct(out_shape, pieces[0].dtype),
        in_specs=[pl.BlockSpec(memory_space=pltpu.SMEM)]
        + [pl.BlockSpec(memory_space=pl.ANY)] * len(pieces),
        out_specs=pl.BlockSpec(memory_space=pl.ANY),
        scratch_shapes=[pltpu.VMEM(piece.shape[:-1] + (size,), piece.dtype) for piece in pieces]
        + [
            pltpu.SemaphoreType.DMA((count,)),
            pltpu.SemaphoreType.DMA((count,)),
        ],
        compiler_params=pltpu.CompilerParams(vmem_limit_bytes=32 * 1024 * 1024),
        cost_estimate=pl.CostEstimate(
            flops=0, bytes_accessed=1024, transcendentals=0
        ),
    )(jnp.stack(places).astype(jnp.int32), *pieces)


def sum_weight(part):
    rows, wide = part.shape
    return lax.psum_scatter(
        part.reshape(2, rows // 2, wide), "dp", scatter_dimension=1, tiled=True
    )


def both_cores(kept, given):
    core = lax.axis_index("context")
    taken = other_core(given)
    return jnp.stack([jnp.where(core == 0, kept, taken), jnp.where(core == 0, taken, kept)])


def gather_rows(both):
    out = lax.all_gather(both, "dp", axis=1, tiled=True)
    return out.reshape(-1, both.shape[2])


def cores_in_order(blocks):
    core = lax.axis_index("context")
    mine = jnp.where(core == 0, blocks[0], blocks[1])
    other = other_core(jnp.where(core == 0, blocks[1], blocks[0]))
    return jnp.where(core == 0, mine, other), jnp.where(core == 0, other, mine)


def along_expert(blocks):
    return lax.all_to_all(blocks, "expert", split_axis=0, concat_axis=0, tiled=True)


def gather_line(block):
    return along_expert(jnp.broadcast_to(block[None], (lax.axis_size("expert"),) + block.shape))


def gather_cores(mine):
    core = lax.axis_index("context")
    other = other_core(mine)
    both = jnp.stack([jnp.where(core == 0, mine, other), jnp.where(core == 0, other, mine)], axis=1)
    return both.reshape((-1,) + mine.shape[2:])


def group_sum(mine, other):
    rows = (mine.astype(floats) + other_core(other).astype(floats)).astype(halves)
    return jnp.sum(along_expert(rows).astype(floats), axis=0)


up_line = [(0, 1), (1, 2), (2, 3)]
down_line = [(1, 0), (2, 1), (3, 2)]
cross_line = [(0, 2), (1, 3), (2, 0), (3, 1)]


def line_gather(block, *pins):
    here = lax.axis_index("expert")
    second = lax.ppermute(block, "expert", cross_line)
    lower = lax.ppermute(block, "expert", up_line)
    upper = lax.ppermute(block, "expert", down_line)
    third = lax.ppermute(second, "expert", [(2, 3), (1, 0)])
    third = after(third, *pins) if pins else third
    mine = jnp.stack(
        [block, jnp.where(here == 3, third, upper), second, jnp.where(here == 0, third, lower)]
    )
    return mine


def line_sum(mine, other, *pins):
    here = lax.axis_index("expert")
    rows = [
        (mine[k].astype(floats) + other[k].astype(floats)).astype(halves) for k in range(4)
    ]
    corner = lax.ppermute(jnp.where(here == 3, rows[1], rows[3]), "expert", [(3, 2), (0, 1)])
    lower = lax.ppermute(rows[1], "expert", up_line)
    upper = lax.ppermute(rows[3], "expert", down_line)
    passed = (rows[2].astype(floats) + corner.astype(floats)).astype(halves)
    second = lax.ppermute(passed, "expert", cross_line)
    second = after(second, *pins) if pins else second
    return (
        rows[0].astype(floats) + lower.astype(floats) + upper.astype(floats) + second.astype(floats)
    )


def further_on(array, back=False):
    here = lax.axis_index("expert")
    count = array.shape[0]
    array = jnp.where(lax.axis_index("context") == 0, array, array[:, ::-1])
    start = lax.rem(count - here, count) if back else here
    return lax.dynamic_slice_in_dim(jnp.concatenate([array, array]), start, count, 0)


def spread(values):
    count = lax.axis_size(every)
    padded = jnp.broadcast_to(values.reshape(1, -1, 128), (count, values.shape[0] // 128, 128))
    got = lax.all_to_all(padded, every, split_axis=0, concat_axis=0, tiled=True)
    return got.reshape(count, -1)


def kernel_call(kernel, out_shapes, in_specs, out_specs, flops, grid=None, scratch=(), aliases=None):
    extra = {} if grid is None else {"grid": grid}
    return pl.pallas_call(
        kernel,
        out_shape=out_shapes,
        in_specs=in_specs,
        out_specs=out_specs,
        scratch_shapes=list(scratch),
        input_output_aliases=aliases or {},
        compiler_params=pltpu.CompilerParams(vmem_limit_bytes=56 * 1024 * 1024),
        cost_estimate=pl.CostEstimate(
            flops=int(flops * cost_scale), bytes_accessed=1024, transcendentals=0
        ),
        **extra,
    )


def kdot(left, right, dims):
    return lax.dot_general(left, right, (dims, ((), ())), preferred_element_type=floats)


nn = ((1,), (0,))
nt = ((1,), (1,))
tn = ((0,), (0,))


def ordered(core, first, second):
    return jnp.where(core == 0, first, second), jnp.where(core == 0, second, first)


def pack_shared(core, gate_up, down):
    rows, both = gate_up.shape[1:]
    units = both // 2
    full = units + -units % 128

    def kernel(core_ref, up_ref, down_ref, out):
        keep = lax.broadcasted_iota(jnp.int32, (rows, full), 1) < units
        fill = jnp.zeros((rows, full - units), floats)
        for at in range(3):
            if at < 2:
                part = up_ref[at].astype(floats)
                low = part[:, :full]
                high = pltpu.roll(part, units, 1)[:, :full]
            else:
                low = jnp.concatenate([down_ref[:units, :].astype(floats).T, fill], axis=1)
                high = jnp.concatenate([down_ref[units:, :].astype(floats).T, fill], axis=1)
            low, high = jnp.where(keep, low, 0.0), jnp.where(keep, high, 0.0)
            mine, other = ordered(core_ref[0], low, high)
            columns = slice(at * full, (at + 1) * full)
            out[0, :, columns] = mine.astype(halves)
            out[1, :, columns] = other.astype(halves)

    vmem = pl.BlockSpec(memory_space=pltpu.VMEM)
    return kernel_call(
        kernel,
        jax.ShapeDtypeStruct((2, rows, 3 * full), halves),
        [pl.BlockSpec(memory_space=pltpu.SMEM), vmem, vmem],
        vmem,
        0,
    )(core, gate_up, down)


def unpack_shared(core, sums, got, units):
    rows, wide = got.shape
    full = wide // 3

    def kernel(core_ref, sums_ref, got_ref, up_out, down_out):
        low, high = ordered(core_ref[0], sums_ref[core_ref[0]], got_ref[...])
        fill = jnp.zeros((rows, 2 * units - full), floats)
        for at in range(2):
            columns = slice(at * full, (at + 1) * full)
            first = jnp.concatenate([low[:, columns].astype(floats), fill], axis=1)
            second = jnp.concatenate([high[:, columns].astype(floats), fill], axis=1)
            up_out[at] = first + pltpu.roll(second, units, 1)
        down_out[:units, :] = low[:, 2 * full :].astype(floats).T[:units]
        down_out[units:, :] = high[:, 2 * full :].astype(floats).T[:units]

    vmem = pl.BlockSpec(memory_space=pltpu.VMEM)
    shape = jax.ShapeDtypeStruct
    return kernel_call(
        kernel,
        (shape((2, rows, 2 * units), floats), shape((2 * units, rows), floats)),
        [pl.BlockSpec(memory_space=pltpu.SMEM), vmem, vmem],
        (vmem, vmem),
        0,
    )(core, sums, got)


def attention_forward(core, places, tokens, gain, blocks, bias, cosine, sine, seg_col, seg_row):
    length, width = tokens.shape
    count, rows_each, wide = blocks[0].shape
    piece = (wide - 128) // 4
    half = count // 2
    spans = [(0, count)] * 3 + [(0, half), (half, count)]
    heads = piece // HEAD_DIM
    scale = 1.0 / math.sqrt(HEAD_DIM)
    tile = 256

    def kernel(
        core_ref, place_ref, tok, gain_ref, bias_ref, cos_ref, sin_ref, segc, segr, *refs
    ):
        pieces, refs = refs[:5], refs[5:]
        w, wout, normed, query, key, value, lse, attended, mine, other, sems = refs
        copies = []
        for i, (first, last) in enumerate(spans):
            for g in range(first, last):
                row = pl.multiple_of((g * 4 + place_ref[i]) * rows_each, rows_each)
                copies.append(
                    pltpu.make_async_copy(
                        pieces[i].at[g - first, :, pl.ds(0, 3 * piece)],
                        w.at[pl.ds(row, rows_each)],
                        sems.at[len(copies)],
                    )
                )
                row = pl.multiple_of(place_ref[i] * rows_each, rows_each)
                copies.append(
                    pltpu.make_async_copy(
                        pieces[i].at[g - first, :, pl.ds(3 * piece + 128, piece)],
                        wout.at[pl.ds(row, rows_each), pl.ds(g * piece, piece)],
                        sems.at[len(copies)],
                    )
                )
        for copy in copies:
            copy.start()
        for copy in copies:
            copy.wait()
        for t in range(length // tile):
            rows = pl.ds(t * tile, tile)
            x = tok[rows, :].astype(floats)
            stat = lax.rsqrt(jnp.mean(x * x, axis=-1, keepdims=True) + eps_norm)
            low = (x * stat * gain_ref[...]).astype(halves)
            normed[rows, :] = low
            proj = kdot(low, w[...], nn) + bias_ref[...]
            c, s = cos_ref[rows, :], sin_ref[rows, :]
            for h in range(heads):
                at = slice(h * HEAD_DIM, (h + 1) * HEAD_DIM)
                q = proj[:, at]
                query[rows, at] = ((q * c + pltpu.roll(q, 64, 1) * s) * scale).astype(halves)
                k = proj[:, piece + h * HEAD_DIM : piece + (h + 1) * HEAD_DIM]
                key[rows, at] = (k * c + pltpu.roll(k, 64, 1) * s).astype(halves)
            value[rows, :] = proj[:, 2 * piece :].astype(halves)
        for t in range(length // tile):
            rows = pl.ds(t * tile, tile)
            seen = (t + 1) * tile
            place = lax.broadcasted_iota(jnp.int32, (tile, seen), 0) + t * tile
            visible = (lax.broadcasted_iota(jnp.int32, (tile, seen), 1) <= place) & (
                segc[rows, :] == segr[:, :seen]
            )
            for h in range(heads):
                at = slice(h * HEAD_DIM, (h + 1) * HEAD_DIM)
                scores = kdot(query[rows, at], key[:seen, at], nt)
                scores = jnp.where(visible, scores, neg_fill)
                top = jnp.max(scores, axis=-1, keepdims=True)
                grown = jnp.exp(scores - top)
                total = jnp.sum(grown, axis=-1, keepdims=True)
                probs = (grown / total).astype(halves)
                attended[rows, at] = kdot(probs, value[:seen, at], nn).astype(halves)
                lse[rows, h : h + 1] = top + jnp.log(total)
            mixed = kdot(attended[rows, :], wout[...], nn).astype(halves)
            k = lax.rem(t + 4 - core_ref[1], 4)
            mine[k], other[k] = ordered(core_ref[0], mixed[: tile // 2], mixed[tile // 2 :])

    vmem = pl.BlockSpec(memory_space=pltpu.VMEM)
    shape = jax.ShapeDtypeStruct
    return kernel_call(
        kernel,
        (
            shape((width, 3 * piece), halves),
            shape((piece, width), halves),
            shape((length, width), halves),
            shape((length, piece), halves),
            shape((length, piece), halves),
            shape((length, piece), halves),
            shape((length, heads), floats),
            shape((length, piece), halves),
            shape((length // tile, tile // 2, width), halves),
            shape((length // tile, tile // 2, width), halves),
        ),
        [pl.BlockSpec(memory_space=pltpu.SMEM)] * 2
        + [vmem] * 7
        + [pl.BlockSpec(memory_space=pl.ANY)] * 5,
        (vmem,) * 10,
        2 * length * width * 4 * piece + 2 * length * length * 2 * piece,
        scratch=[pltpu.SemaphoreType.DMA((8 * count,))],
    )(core, places, tokens, gain, bias, cosine, sine, seg_col, seg_row, *blocks)


def attention_backward(
    core, mid_mine, mid_other, tokens, weight, cosine, sine, seg_col, seg_row, out_rows,
    query, key, value, lse, attended,
):
    length, width = tokens.shape
    piece = out_rows.shape[0]
    heads = piece // HEAD_DIM
    scale = 1.0 / math.sqrt(HEAD_DIM)
    tile = 256

    def kernel(
        core_ref, mid_m, mid_o, tok, w, cos_ref, sin_ref, segc, segr, wout, q_ref, k_ref, v_ref, lse_ref,
        att_ref, proj_grad, mine, other, gain_part, bias_part, out_part, key_grad, value_grad, out_grad,
    ):
        out_grad[...] = jnp.zeros_like(out_grad)
        key_grad[...] = jnp.zeros_like(key_grad)
        value_grad[...] = jnp.zeros_like(value_grad)
        for t in range(length // tile):
            rows = pl.ds(t * tile, tile)
            seen = (t + 1) * tile
            place = lax.broadcasted_iota(jnp.int32, (tile, seen), 0) + t * tile
            visible = (lax.broadcasted_iota(jnp.int32, (tile, seen), 1) <= place) & (
                segc[rows, :] == segr[:, :seen]
            )
            k = lax.rem(t + 4 - core_ref[1], 4)
            mid = jnp.concatenate(ordered(core_ref[0], mid_m[k], mid_o[k]))
            grad = kdot(mid, wout[...], nt).astype(halves)
            out_grad[...] += kdot(att_ref[rows, :], mid, tn)
            c, s = cos_ref[rows, :], sin_ref[rows, :]
            for h in range(heads):
                at = slice(h * HEAD_DIM, (h + 1) * HEAD_DIM)
                query = q_ref[rows, at]
                scores = kdot(query, k_ref[:seen, at], nt)
                probs = jnp.where(visible, jnp.exp(scores - lse_ref[rows, h : h + 1]), 0.0)
                prob_grad = kdot(grad[:, at], v_ref[:seen, at], nt)
                delta = jnp.sum(probs * prob_grad, axis=-1, keepdims=True)
                score_grad = (probs * (prob_grad - delta)).astype(halves)
                q_grad = kdot(score_grad, k_ref[:seen, at], nn) * scale
                proj_grad[rows, at] = (q_grad * c - pltpu.roll(q_grad, 64, 1) * s).astype(halves)
                key_grad[:seen, at] += kdot(score_grad, query, tn)
                value_grad[:seen, at] += kdot(probs.astype(halves), grad[:, at], tn)
        gains = jnp.zeros((1, width), floats)
        biases = jnp.zeros((1, 3 * piece), floats)
        for t in range(length // tile):
            rows = pl.ds(t * tile, tile)
            c, s = cos_ref[rows, :], sin_ref[rows, :]
            for h in range(heads):
                at = slice(h * HEAD_DIM, (h + 1) * HEAD_DIM)
                k_grad = key_grad[rows, at]
                proj_grad[rows, piece + h * HEAD_DIM : piece + (h + 1) * HEAD_DIM] = (
                    k_grad * c - pltpu.roll(k_grad, 64, 1) * s
                ).astype(halves)
            proj_grad[rows, 2 * piece :] = value_grad[rows, :].astype(halves)
            grads = proj_grad[rows, :]
            biases = biases + jnp.sum(grads.astype(floats), axis=0, keepdims=True)
            part = kdot(grads, w[...], nt)
            x = tok[rows, :].astype(floats)
            stat = lax.rsqrt(jnp.mean(x * x, axis=-1, keepdims=True) + eps_norm)
            gains = gains + jnp.sum(part * (x * stat), axis=0, keepdims=True)
            k = lax.rem(t + 4 - core_ref[1], 4)
            part = part.astype(halves)
            mine[k], other[k] = ordered(core_ref[0], part[: tile // 2], part[tile // 2 :])
        out_part[...] = out_grad[...].astype(halves)
        gain_part[...] = gains
        bias_part[...] = biases

    vmem = pl.BlockSpec(memory_space=pltpu.VMEM)
    shape = jax.ShapeDtypeStruct
    return kernel_call(
        kernel,
        (
            shape((length, 3 * piece), halves),
            shape((length // tile, tile // 2, width), halves),
            shape((length // tile, tile // 2, width), halves),
            shape((1, width), floats),
            shape((1, 3 * piece), floats),
            shape((piece, width), halves),
        ),
        [pl.BlockSpec(memory_space=pltpu.SMEM)] + [vmem] * 14,
        (vmem,) * 6,
        2 * length * width * 5 * piece + 2 * length * length * 5 * piece,
        scratch=[
            pltpu.VMEM((length, piece), floats),
            pltpu.VMEM((length, piece), floats),
            pltpu.VMEM((piece, width), floats),
        ],
    )(
        core, mid_mine, mid_other, tokens, weight, cosine, sine, seg_col, seg_row, out_rows,
        query, key, value, lse, attended,
    )


def expert_pass(slot_row, gate_row, rows_in, grads_in, up, downs, places, capacity):
    pairs, half, width = rows_in[0].shape
    rows_each = downs[0].shape[0]
    ff = rows_each * len(downs)
    pair = 2 * half
    count = pairs * capacity
    wide = 2 * ff

    def kernel(
        place_ref, slot_ref, gate_ref, x_mine, x_other, g_mine, g_other, up_hbm, *refs
    ):
        downs_hbm, refs = refs[: len(downs)], refs[len(downs) :]
        slot_in, slot_grad, hidden, pre_grad, out, in_grad, w_up, w_down, pre, up_sems, down_sems = refs
        chunk = 256
        chunks = wide // chunk
        loads = [
            pltpu.make_async_copy(
                up_hbm.at[:, pl.ds(j * chunk, chunk)], w_up.at[:, pl.ds(j * chunk, chunk)], up_sems.at[j]
            )
            for j in range(chunks)
        ]
        down_loads = [
            pltpu.make_async_copy(
                block,
                w_down.at[pl.ds(pl.multiple_of(place_ref[i] * rows_each, 16), rows_each)],
                down_sems.at[i],
            )
            for i, block in enumerate(downs_hbm)
        ]
        for load in loads + down_loads:
            load.start()
        for p in range(pairs):
            slots = pl.ds(p * capacity, capacity)
            picks = lax.broadcasted_iota(jnp.int32, (capacity, pair), 0) == slot_ref[p]
            pick = jnp.where(picks, 1.0, 0.0).astype(halves)
            gates = jnp.sum(jnp.where(picks, gate_ref[p], 0.0), axis=-1, keepdims=True)
            x = jnp.concatenate([x_mine[p], x_other[p]])
            slot_in[slots, :] = kdot(pick, x, nn).astype(halves)
            g = jnp.concatenate([g_mine[p], g_other[p]])
            slot_grad[slots, :] = (kdot(pick, g, nn) * gates).astype(halves)
        for j in range(chunks):
            loads[j].wait()
            at = pl.ds(j * chunk, chunk)
            pre[:, at] = kdot(slot_in[...], w_up[:, at], nn)
        for load in down_loads:
            load.wait()
        start = 0
        while start < ff:
            size = min(256, ff - start)
            at = slice(start, start + size)
            up_at = slice(ff + start, ff + start + size)
            grad = kdot(slot_grad[...], w_down[at, :], nt)
            gate_pre, up_pre = pre[:, at], pre[:, up_at]
            sigma = jax.nn.sigmoid(gate_pre)
            act = gate_pre * sigma
            hidden[:, at] = (act * up_pre).astype(halves)
            pre_grad[:, at] = (grad * up_pre * sigma * (1.0 + gate_pre * (1.0 - sigma))).astype(halves)
            pre_grad[:, up_at] = (grad * act).astype(halves)
            start += size
        for j in range(width // 512):
            at = pl.ds(j * 512, 512)
            out[:, at] = kdot(hidden[...], w_down[:, at], nn).astype(halves)
            in_grad[:, at] = kdot(pre_grad[...], w_up[at, :], nt).astype(halves)

    vmem = pl.BlockSpec(memory_space=pltpu.VMEM)
    hbm = pl.BlockSpec(memory_space=pl.ANY)
    shape = jax.ShapeDtypeStruct
    return kernel_call(
        kernel,
        (
            shape((count, width), halves),
            shape((count, width), halves),
            shape((count, ff), halves),
            shape((count, wide), halves),
            shape((count, width), halves),
            shape((count, width), halves),
        ),
        [pl.BlockSpec(memory_space=pltpu.SMEM)] + [vmem] * 6 + [hbm] * (1 + len(downs)),
        (vmem,) * 6,
        2 * count * width * ff * 6,
        scratch=[
            pltpu.VMEM(up.shape, halves),
            pltpu.VMEM((ff, width), halves),
            pltpu.VMEM((count, wide), floats),
            pltpu.SemaphoreType.DMA((wide // 256,)),
            pltpu.SemaphoreType.DMA((len(downs),)),
        ],
    )(places, slot_row, gate_row, *rows_in, *grads_in, up, *downs)


def shared_pass(slot_col, gate_col, rows_in, grads_in, weights, vector, expert_out, expert_grad):
    pairs, half, width = rows_in[0].shape
    tile = 2 * half
    length = pairs * tile
    units = weights.shape[1] // 3
    capacity = expert_out.shape[0] * tile // length

    def kernel(
        slot_ref, gate_ref, x_mine, x_other, g_mine, g_other, up_ref, down_ref, vec_ref, eout_ref, egrad_ref,
        ffn_mine, ffn_other, out_mine, out_other, pre_grad, hidden, shared_grad, logit,
    ):
        x = jnp.concatenate([x_mine[0], x_other[0]])
        pre = kdot(x, up_ref[...], nn)
        gate_shared = jax.nn.sigmoid(
            jnp.sum(x.astype(floats) * vec_ref[...], axis=-1, keepdims=True)
        )
        grads = jnp.concatenate([g_mine[0], g_other[0]]).astype(floats)
        low_grad = (gate_shared * grads).astype(halves)
        shared_grad[...] = low_grad
        grad = kdot(low_grad, down_ref[...], nn)
        gate_pre, up_pre = pre[:, :units], pre[:, units:]
        sigma = jax.nn.sigmoid(gate_pre)
        act = gate_pre * sigma
        hid = (act * up_pre).astype(halves)
        hidden[...] = hid
        pre_grad[:, :units] = (grad * up_pre * sigma * (1.0 + gate_pre * (1.0 - sigma))).astype(halves)
        pre_grad[:, units:] = (grad * act).astype(halves)
        picks = lax.broadcasted_iota(jnp.int32, (tile, capacity), 1) == slot_ref[...]
        pick = jnp.where(picks, 1.0, 0.0).astype(halves)
        ffn = kdot(pre_grad[...], up_ref[...], nt) + kdot(pick, egrad_ref[...], nn)
        ffn_mine[0], ffn_other[0] = ffn[:half].astype(halves), ffn[half:].astype(halves)
        shared_out = kdot(hid, down_ref[...], nt)
        logit[...] = jnp.sum(grads * shared_out, axis=-1, keepdims=True)
        out = gate_shared * shared_out + gate_ref[...] * kdot(pick, eout_ref[...], nn)
        out_mine[0], out_other[0] = out[:half].astype(halves), out[half:].astype(halves)

    shape = jax.ShapeDtypeStruct
    rows = lambda n: pl.BlockSpec((tile, n), lambda i: (i, 0))
    whole = lambda a: pl.BlockSpec(a.shape, lambda i: (0,) * a.ndim)
    slots = pl.BlockSpec((capacity, width), lambda i: (i, 0))
    halfs = pl.BlockSpec((1, half, width), lambda i: (i, 0, 0))
    half_shape = shape((pairs, half, width), halves)
    return kernel_call(
        kernel,
        (half_shape,) * 4
        + (
            shape((length, 2 * units), halves),
            shape((length, units), halves),
            shape((length, width), halves),
            shape((length, 1), floats),
        ),
        [
            rows(1), rows(1), halfs, halfs, halfs, halfs,
            pl.BlockSpec((width, 2 * units), lambda i: (0, 0)),
            pl.BlockSpec((width, units), lambda i: (0, 2)),
            whole(vector), slots, slots,
        ],
        (halfs,) * 4 + (rows(2 * units), rows(units), rows(width), rows(1)),
        2 * length * width * units * 6,
        grid=(pairs,),
    )(slot_col, gate_col, *rows_in, *grads_in, weights, weights, vector, expert_out, expert_grad)


def weight_grad(lefts, right, into=None, at=0, wide=None):
    rows = lefts[0].shape[-1]
    depth, each = right.shape[0], lefts[0].shape[-2]
    tile = 256
    first = at // tile
    wide = right.shape[1] if wide is None else wide

    def kernel(*refs):
        left_refs, right_ref = refs[: len(lefts)], refs[len(lefts)]
        out, turned = refs[-2:]

        @pl.when(pl.program_id(0) == 0)
        def _():
            if len(lefts) == 1:
                turned[...] = left_refs[0][...].T
            else:
                for block in range(depth // each):
                    rows_low = left_refs[block % 2][block // 2]
                    turned[:, block * each : (block + 1) * each] = rows_low.T

        out[...] = kdot(turned[...], right_ref[...], nn).astype(halves)

    more = [] if into is None else [into]
    return kernel_call(
        kernel,
        jax.ShapeDtypeStruct((rows, wide), halves),
        [pl.BlockSpec(left.shape, lambda j, n=left.ndim: (0,) * n) for left in lefts]
        + [pl.BlockSpec((depth, tile), lambda j: (0, j))]
        + [pl.BlockSpec(memory_space=pl.ANY)] * len(more),
        pl.BlockSpec((rows, tile), lambda j: (0, first + j)),
        2 * depth * rows * right.shape[1],
        grid=(right.shape[1] // tile,),
        scratch=[pltpu.VMEM((rows, depth), halves)],
        aliases={len(lefts) + 1: 0} if more else {},
    )(*lefts, right, *more)


def head_cut(qkv_weight, out_weight, vectors):
    count = lax.axis_size(group)
    rows, wide = qkv_weight.shape
    piece = wide // (3 * count)
    cut = qkv_weight.reshape(rows, 3, count, piece).transpose(2, 0, 1, 3).reshape(count, rows, 3 * piece)
    columns = jnp.concatenate([vector.reshape(-1, rows) for vector in vectors]).T
    columns = jnp.pad(columns, ((0, 0), (0, 128 - columns.shape[1])))
    columns = jnp.broadcast_to(columns[None], (count,) + columns.shape)
    cut = jnp.concatenate([cut, columns], axis=-1)
    cut = lax.all_to_all(cut, group, split_axis=0, concat_axis=0, tiled=True)
    out = out_weight.reshape(rows, count, piece).transpose(1, 0, 2)
    return jnp.concatenate([cut, out], axis=-1)


def head_vectors(blocks, places):
    count, rows, wide = blocks[0].shape
    piece = (wide - 128) // 4
    half = count // 2
    whole = lambda out, at: out.at[:, at]
    low = lambda out, at: out.at[pl.ds(0, half), at]
    high = lambda out, at: out.at[pl.ds(half, half), at]
    packed = place_blocks(
        blocks, places, (count, 4, rows, 128), [whole] * 3 + [low, high], (3 * piece, 128)
    )
    columns = packed[..., :6].astype(floats)
    vectors = [columns[..., at].reshape(-1) for at in range(3)]
    vectors.append(columns[..., 3:].transpose(0, 1, 3, 2).reshape(-1))
    return vectors


def rows_weights(qkv_weight, out_weight):
    return (
        lax.all_gather(qkv_weight, every, axis=0, tiled=True),
        lax.all_gather(out_weight, every, axis=0, tiled=True),
    )


def rows_forward(own_tokens, gain, bias, weights, seq_ids):
    weight, out_weight = weights
    tok_count, width = own_tokens.shape
    seq_len = seq_ids.shape[0]
    head_groups = HEADS // group_heads
    block_place = lax.axis_index(group)
    positions = block_place * tok_count + jnp.arange(tok_count, dtype=jnp.int32)
    cosine, sine = rope_tables(positions, HEAD_DIM // 2)
    scale = 1.0 / math.sqrt(HEAD_DIM)
    tokens = own_tokens.astype(floats)
    stat = lax.rsqrt(jnp.mean(tokens * tokens, axis=-1, keepdims=True) + eps_norm)
    unit = tokens * stat
    normed = (unit * gain).astype(halves)
    projected = dot(normed, weight) + bias
    raw = projected.reshape(tok_count, 3, HEADS, HEAD_DIM)
    query = (rotate(raw[:, 0], cosine, sine) * scale).astype(halves)
    key = rotate(raw[:, 1], cosine, sine).astype(halves)
    value = raw[:, 2].astype(halves)

    def by_group(array):
        return array.reshape(tok_count, head_groups, group_heads, HEAD_DIM).transpose(1, 0, 2, 3)

    query_groups = by_group(query)
    key_all = lax.all_gather(by_group(key), group, axis=1, tiled=True)
    value_all = lax.all_gather(by_group(value), group, axis=1, tiled=True)
    query_ids = lax.dynamic_slice_in_dim(seq_ids, block_place * tok_count, tok_count)
    key_places = jnp.arange(seq_len, dtype=jnp.int32)
    visible = (key_places[None, :] <= positions[:, None]) & (seq_ids[None, :] == query_ids[:, None])

    def attend_group(pieces):
        q_part, k_part, v_part = pieces
        scores = jnp.einsum("qhd,khd->hqk", q_part, k_part, preferred_element_type=floats)
        scores = jnp.where(visible[None], scores, neg_fill)
        top_score = jnp.max(scores, axis=-1, keepdims=True)
        grown = jnp.exp(scores - top_score)
        total = jnp.sum(grown, axis=-1, keepdims=True)
        probs_low = (grown / total).astype(halves)
        mixed = jnp.einsum("hqk,khd->qhd", probs_low, v_part, preferred_element_type=floats)
        return (mixed, top_score + jnp.log(total))

    mixed_groups, log_totals = lax.map(attend_group, (query_groups, key_all, value_all))
    attended = mixed_groups.transpose(1, 0, 2, 3).reshape(tok_count, width).astype(halves)
    saved = (normed, unit, query_groups, key_all, value_all, log_totals, attended, cosine, sine, visible)
    return dot(attended, out_weight), saved


def rows_backward(weights, saved, mid_low):
    weight, out_weight = weights
    normed, unit, query_groups, key_all, value_all, log_totals, attended, cosine, sine, visible = saved
    tok_count, width = mid_low.shape
    head_groups = HEADS // group_heads
    scale = 1.0 / math.sqrt(HEAD_DIM)
    attended_grad = dot_nt(mid_low, out_weight).astype(halves)
    grad_groups = attended_grad.reshape(tok_count, head_groups, group_heads, HEAD_DIM).transpose(
        1, 0, 2, 3
    )

    def attend_back(pieces):
        q_part, k_part, v_part, g_part, log_part = pieces
        scores = jnp.einsum("qhd,khd->hqk", q_part, k_part, preferred_element_type=floats)
        scores = jnp.where(visible[None], scores, neg_fill)
        probs = jnp.exp(scores - log_part)
        prob_grad = jnp.einsum("qhd,khd->hqk", g_part, v_part, preferred_element_type=floats)
        delta = jnp.sum(probs * prob_grad, axis=-1, keepdims=True)
        score_grad = (probs * (prob_grad - delta)).astype(halves)
        q_grad = jnp.einsum("hqk,khd->qhd", score_grad, k_part, preferred_element_type=floats)
        k_grad = jnp.einsum("hqk,qhd->khd", score_grad, q_part, preferred_element_type=floats)
        v_grad = jnp.einsum(
            "hqk,qhd->khd", probs.astype(halves), g_part, preferred_element_type=floats
        )
        return (q_grad, k_grad, v_grad)

    query_grads, key_grads, value_grads = lax.map(
        attend_back, (query_groups, key_all, value_all, grad_groups, log_totals)
    )
    key_grad = lax.psum_scatter(key_grads, group, scatter_dimension=1, tiled=True)
    value_grad = lax.psum_scatter(value_grads, group, scatter_dimension=1, tiled=True)

    def by_head(array):
        return array.transpose(1, 0, 2, 3).reshape(tok_count, HEADS, HEAD_DIM)

    proj_grad = jnp.concatenate(
        [
            rotate_back(by_head(query_grads) * scale, cosine, sine).reshape(tok_count, width),
            rotate_back(by_head(key_grad), cosine, sine).reshape(tok_count, width),
            by_head(value_grad).reshape(tok_count, width),
        ],
        axis=-1,
    ).astype(halves)
    bias_part = jnp.sum(proj_grad.astype(floats), axis=0)
    attn_in_grad = dot_nt(proj_grad, weight)
    gain_part = jnp.sum(attn_in_grad * unit, axis=0)
    qkv_out = lax.psum_scatter(dot_tn(normed, proj_grad), every, scatter_dimension=0, tiled=True)
    out_out = lax.psum_scatter(dot_tn(attended, mid_low), every, scatter_dimension=0, tiled=True)
    return attn_in_grad, gain_part, bias_part, qkv_out, out_out


def routing_of(expert_ids, slot_order, gate_weights, count, mark):
    tok_count, topk = expert_ids.shape[1:]
    routing = [expert_ids[0].reshape(-1), slot_order[0, 0], gate_weights[0].reshape(-1)]
    routing = jnp.concatenate([v.astype(floats) for v in routing]).reshape(1, -1, 128)
    routing = jnp.broadcast_to(routing, (count,) + routing.shape[1:])
    routing = lax.all_to_all(after(routing, mark), group, split_axis=0, concat_axis=0, tiled=True)
    routing = routing.reshape(count, 3, tok_count, topk)
    return routing[:, 0], routing[:, 1], routing[:, 2]


def slots_of(routes, index, capacity):
    pair_expert, pair_order, pair_gate = routes
    chosen = pair_expert == index.astype(floats)
    has_pair = jnp.any(chosen, axis=-1)
    order = jnp.sum(jnp.where(chosen, pair_order, 0.0), axis=-1)
    gate = jnp.sum(jnp.where(chosen, pair_gate, 0.0), axis=-1)
    earlier = has_pair[:, None, :] & (order[:, None, :] < order[:, :, None])
    rank = jnp.sum(earlier.astype(jnp.int32), axis=-1)
    kept = has_pair & (rank < capacity)
    return rank, kept, jnp.where(kept, gate, 0.0)


def small_sums(parts, lengths, mark):
    devices = lax.axis_size(every)
    packed = jnp.concatenate([part.reshape(devices, -1) for part in parts], axis=1)
    packed = jnp.pad(after(packed, mark), ((0, 0), (0, -packed.shape[1] % 128)))
    packed = lax.all_to_all(
        packed.reshape(devices, -1, 128), every, split_axis=0, concat_axis=0, tiled=True
    )
    sums = jnp.sum(packed, axis=0).reshape(-1)
    out, at = [], 0
    for size in lengths:
        out.append(sums[at : at + size])
        at += size
    return out


def norm_backward(grad_out, grads, gain, unit, stat):
    unit_grad = grads * gain
    return grad_out + stat * (unit_grad - unit * jnp.mean(unit_grad * unit, axis=-1, keepdims=True))


def halves_of(array, axis, which):
    size = array.shape[axis] // 2
    return lax.dynamic_slice_in_dim(array, which * size, size, axis)


def entry(array, which):
    return lax.dynamic_index_in_dim(array, which, 0, keepdims=False)


def shards_by_heads(
    tokens,
    cotangent,
    segments,
    expert_ids,
    slot_order,
    gate_weights,
    qkv_weight,
    qkv_bias,
    out_weight,
    norm_attn,
    norm_ffn,
    shared_gate_up,
    shared_down,
    shared_gate,
    expert_gate_up,
    expert_down,
):
    count = lax.axis_size(group)
    core = lax.axis_index("context")
    place = lax.axis_index("dp")
    index = lax.axis_index(group)
    tok_count, width = tokens.shape[1:]
    pairs = tok_count * expert_ids.shape[2]
    experts = expert_gate_up.shape[0] * lax.axis_size("expert")
    capacity = (9 * pairs + 8 * experts - 1) // (8 * experts)
    length = count * tok_count
    core_at = jnp.stack([core, lax.axis_index("expert")]).astype(jnp.int32)
    vectors = [norm_attn, norm_ffn, shared_gate, qkv_bias]
    lengths = [vector.shape[0] for vector in vectors]
    own_tokens = tokens[0]
    resid_in = own_tokens.astype(floats)

    cut = head_cut(qkv_weight, out_weight, vectors)
    all_tokens = lax.all_gather(after(own_tokens, cut), group, axis=0, tiled=True)
    cut_x, cut_y = near_blocks(cut)
    eu_both = both_cores(entry(expert_gate_up, core), entry(expert_gate_up, 1 - core))
    half = count // 2
    cut_far = (
        dp_step(after(cut_x[:half], eu_both), 2),
        dp_step(after(cut_y[half:], eu_both), 1),
    )
    blocks = [cut, cut_x, cut_y, *cut_far]
    places = [place, place ^ 1, place ^ 2, place ^ 3, place ^ 3]
    gain_attn, gain_ffn, gate_vector, bias = head_vectors(blocks, places)
    expert_up = gather_rows(eu_both)
    grads_mine = line_gather(after(cotangent[0], cut))
    routes = routing_of(expert_ids, slot_order, gate_weights, count, cut)
    rank, kept, gate = slots_of(routes, index, capacity)
    slot = further_on(jnp.where(kept, rank, -1).reshape(-1, 2, tok_count))
    slot = slot + jnp.where(slot < 0, 0, jnp.arange(2, dtype=jnp.int32)[:, None] * capacity)
    gate = further_on(gate.reshape(-1, 2, tok_count))
    all_tokens = after(all_tokens, slot, gate)

    piece = width // count
    positions = jnp.arange(length, dtype=jnp.int32)
    cosine, sine = rope_tables(positions, HEAD_DIM // 2)
    cosine = jnp.concatenate([cosine, cosine], axis=-1)
    sine = jnp.concatenate([-sine, sine], axis=-1)
    seg_row = segments.astype(jnp.int32)
    seg_col = seg_row.reshape(length, 1)
    own_bias = lax.dynamic_index_in_dim(bias.reshape(3, count, piece), index, 1, keepdims=False)
    weight, out_rows, normed, query, key, value, lse, attended, mine, other = attention_forward(
        core_at,
        jnp.stack(places).astype(jnp.int32),
        all_tokens,
        gain_attn.reshape(1, width),
        blocks,
        own_bias.reshape(1, 3 * piece),
        cosine,
        sine,
        seg_col,
        seg_row,
    )

    ed_first = after(entry(expert_down, core), *cut_far)
    ed_second = after(other_core(entry(expert_down, 1 - core)), *cut_far)
    ed_first_x, ed_first_y = near_blocks(ed_first)
    ed_second_x, ed_second_y = near_blocks(ed_second)
    other = other_core(after(other, grads_mine))
    mixed = line_sum(mine, other, ed_first_x, ed_first_y, ed_second_x, ed_second_y)
    ed_first_far, ed_second_far = dp_step(ed_first_x, 2), dp_step(ed_second_y, 1)
    units = shared_down.shape[0] // 2
    sh_pack = pack_shared(core_at, shared_gate_up, shared_down)
    sh_both = both_cores(sh_pack[0], sh_pack[1])
    shared_weights = gather_rows(after(sh_both, attended))

    resid_mid = resid_in + mixed
    stat_ffn = lax.rsqrt(jnp.mean(resid_mid * resid_mid, axis=-1, keepdims=True) + eps_norm)
    unit_ffn = resid_mid * stat_ffn
    normed_ffn = (unit_ffn * gain_ffn).astype(halves)
    grad_out = cotangent[0].astype(floats)
    all_grads = (grads_mine, other_core(after(grads_mine, mine)))
    normed_mine = line_gather(normed_ffn, ed_first_far, ed_second_far, all_grads[1])
    all_normed = (normed_mine, other_core(normed_mine))

    slot_in, slot_grad, hidden, pre_grad, expert_out, expert_grad = expert_pass(
        slot.reshape(count // 2, 1, 2 * tok_count),
        gate.reshape(count // 2, 1, 2 * tok_count),
        all_normed,
        all_grads,
        expert_up,
        [ed_first, ed_first_x, ed_first_y, ed_first_far]
        + [ed_second, ed_second_x, ed_second_y, ed_second_far],
        jnp.stack(
            [4 * which + (place ^ step) for which in (core, 1 - core) for step in range(4)]
        ).astype(jnp.int32),
        2 * capacity,
    )
    eu_term = weight_grad([slot_in], pre_grad)
    ed_term = weight_grad([hidden], slot_grad)
    ffn_mine, ffn_other, out_mine, out_other, sh_pre_grad, sh_hidden, sh_grad, logit_part = shared_pass(
        slot.reshape(length, 1),
        gate.reshape(length, 1),
        (after(all_normed[0], eu_term, ed_term), all_normed[1]),
        all_grads,
        shared_weights,
        gate_vector.reshape(1, width),
        expert_out,
        expert_grad,
    )
    wide = shared_weights.shape[1]
    sh_term = weight_grad(all_normed, sh_pre_grad, None, 0, wide)
    sh_term = weight_grad([sh_grad], sh_hidden, sh_term, sh_pre_grad.shape[1], wide)
    eu_sum, sh_sum = sum_weight(eu_term), sum_weight(sh_term)

    ffn_other = other_core(ffn_other)
    ffn_grad = line_sum(ffn_mine, ffn_other)
    logit_part = further_on(logit_part.reshape(-1, 2, tok_count), True)
    logit_sums = lax.all_to_all(
        after(logit_part.reshape(count, 1, tok_count), ffn_other),
        group,
        split_axis=0,
        concat_axis=0,
        tiled=True,
    )
    own_gate = jax.nn.sigmoid(
        jnp.sum(normed_ffn.astype(floats) * gate_vector, axis=-1, keepdims=True)
    )
    logit_grad = jnp.sum(logit_sums, axis=0).reshape(tok_count, 1) * own_gate * (1.0 - own_gate)
    ffn_grad = ffn_grad + logit_grad * gate_vector
    gain_ffn_part = jnp.sum(ffn_grad * unit_ffn, axis=0)
    gate_vector_part = jnp.sum(logit_grad * normed_ffn.astype(floats), axis=0)
    mid_grad = norm_backward(grad_out, ffn_grad, gain_ffn, unit_ffn, stat_ffn)
    mid_low = after(mid_grad.astype(halves), sh_term)

    out_got = other_core(out_other)
    mid_mine = line_gather(mid_low, eu_sum, out_got)
    mid_other = other_core(mid_mine)
    proj_grad, mine, other, gain_attn_part, bias_part, out_part = attention_backward(
        core_at, mid_mine, mid_other, all_tokens, weight, cosine, sine, seg_col, seg_row, out_rows,
        query, key, value, lse, attended,
    )
    layer_sum = line_sum(out_mine, after(out_got, mid_mine))
    other = other_core(after(other, layer_sum))
    attn_in_grad = line_sum(mine, other)
    rows = other
    weight_part = weight_grad([normed], proj_grad).reshape(count, -1, 3 * piece)
    out_part = out_part.reshape(-1, count, piece).transpose(1, 0, 2)
    total = lax.psum_scatter(
        jnp.concatenate([weight_part, out_part], axis=-1), "dp", scatter_dimension=1, tiled=True
    )
    ed_sum = sum_weight(after(ed_term, sh_term))
    qkv_total = lax.all_to_all(
        after(total[..., : 3 * piece], attn_in_grad), group, split_axis=0, concat_axis=0, tiled=True
    )
    each = qkv_weight.shape[0]
    qkv_out = (
        qkv_total.reshape(count, each, 3, piece)
        .transpose(1, 2, 0, 3)
        .reshape(each, 3 * width)
        .astype(floats)
    )
    out_weight_out = total[..., 3 * piece :].transpose(1, 0, 2).reshape(each, width).astype(floats)
    bias_part = lax.dynamic_update_slice(
        jnp.zeros((3, count, piece), floats), bias_part.reshape(3, 1, piece), (0, index, 0)
    ).reshape(-1)
    layer_sum = resid_mid + layer_sum
    stat_attn = lax.rsqrt(jnp.mean(resid_in * resid_in, axis=-1, keepdims=True) + eps_norm)
    unit_attn = resid_in * stat_attn
    input_grad = norm_backward(mid_grad, attn_in_grad, gain_attn, unit_attn, stat_attn)

    eu_sum, sh_sum, ed_sum = (after(total, rows) for total in (eu_sum, sh_sum, ed_sum))
    got = other_core(entry(sh_sum, 1 - core))
    shared_up_out, shared_down_out = unpack_shared(core_at, sh_sum, got, units)
    gain_attn_out, gain_ffn_out, gate_vector_out, bias_out = small_sums(
        [gain_attn_part, gain_ffn_part, gate_vector_part, bias_part], lengths, attn_in_grad
    )
    return (
        layer_sum.astype(halves)[None],
        input_grad[None],
        qkv_out,
        bias_out,
        out_weight_out,
        gain_attn_out,
        gain_ffn_out,
        shared_up_out,
        shared_down_out,
        gate_vector_out,
        jnp.stack(cores_in_order(eu_sum)).astype(floats),
        jnp.stack(cores_in_order(ed_sum)).astype(floats),
    )


def shards_by_rows(
    tokens,
    cotangent,
    segments,
    expert_ids,
    slot_order,
    gate_weights,
    qkv_weight,
    qkv_bias,
    out_weight,
    norm_attn,
    norm_ffn,
    shared_gate_up,
    shared_down,
    shared_gate,
    expert_gate_up,
    expert_down,
):
    count = lax.axis_size(group)
    core = lax.axis_index("context")
    index = lax.axis_index(group)
    tok_count, width = tokens.shape[1:]
    pairs = tok_count * expert_ids.shape[2]
    experts = expert_gate_up.shape[0] * lax.axis_size("expert")
    capacity = (9 * pairs + 8 * experts - 1) // (8 * experts)
    length = count * tok_count
    vectors = [norm_attn, norm_ffn, shared_gate, qkv_bias]
    lengths = [vector.shape[0] for vector in vectors]
    payload = jnp.concatenate([vector.astype(floats) for vector in vectors])
    small = spread(jnp.pad(payload, (0, -payload.shape[0] % 128)))
    gathered = []
    for at, size in enumerate(lengths):
        first = sum(lengths[:at])
        gathered.append(small[:, first : first + size].reshape(-1))
    gain_attn, gain_ffn, gate_vector, bias = gathered
    routes = routing_of(expert_ids, slot_order, gate_weights, count, small)

    resid_in = tokens[0].astype(floats)
    weights = rows_weights(qkv_weight, out_weight)
    mixed, saved = rows_forward(tokens[0], gain_attn, bias, weights, segments[0])

    def gate_up_half(which):
        part = halves_of(shared_gate_up, 2, which)
        return jnp.concatenate([part[0], part[1]], axis=-1)

    def down_half(which):
        return halves_of(shared_down, 0, which).T

    expert_up = gather_rows(both_cores(entry(expert_gate_up, core), entry(expert_gate_up, 1 - core)))
    expert_dn = gather_rows(both_cores(entry(expert_down, core), entry(expert_down, 1 - core)))
    shared_up = gather_rows(both_cores(gate_up_half(core), gate_up_half(1 - core)))
    shared_dn = gather_rows(both_cores(down_half(core), down_half(1 - core)))
    ff_width = expert_dn.shape[0]
    units = shared_dn.shape[1]

    resid_mid = resid_in + mixed
    stat_ffn = lax.rsqrt(jnp.mean(resid_mid * resid_mid, axis=-1, keepdims=True) + eps_norm)
    unit_ffn = resid_mid * stat_ffn
    normed_ffn = (unit_ffn * gain_ffn).astype(halves)
    grad_out = cotangent[0].astype(floats)
    all_grads = gather_cores(gather_line(cotangent[0]))
    all_normed = gather_cores(gather_line(normed_ffn))

    rank, kept, gate = slots_of(routes, index, capacity)
    slots = jnp.arange(capacity, dtype=jnp.int32)
    select = (rank[:, None, :] == slots[None, :, None]) & kept[:, None, :]
    slot_gate = jnp.sum(jnp.where(select, gate[:, None, :], 0.0), axis=-1).reshape(-1, 1)
    select = select.astype(halves)

    def to_slots(rows):
        rows = rows.reshape(count, tok_count, width)
        got = jnp.einsum("brt,btd->brd", select, rows, preferred_element_type=floats)
        return got.reshape(count * capacity, width)

    def from_slots(rows):
        rows = rows.reshape(count, capacity, width)
        got = jnp.einsum("brt,brd->btd", select, rows, preferred_element_type=floats)
        return got.reshape(length, width)

    slot_in = to_slots(all_normed).astype(halves)
    slot_grad = (to_slots(all_grads) * slot_gate).astype(halves)
    expert_pre = dot(slot_in, expert_up)
    expert_g, expert_u = expert_pre[:, :ff_width], expert_pre[:, ff_width:]
    expert_hidden = (jax.nn.silu(expert_g) * expert_u).astype(halves)
    hidden_grad = dot_nt(slot_grad, expert_dn)
    expert_pre_grad = jnp.concatenate(
        silu_parts(hidden_grad, expert_g, expert_u), axis=-1
    ).astype(halves)
    expert_out = dot(expert_hidden, expert_dn).astype(halves)
    slot_in_grad = dot_nt(expert_pre_grad, expert_up).astype(halves)
    eu_sum = sum_weight(dot_tn(slot_in, expert_pre_grad).astype(halves))
    ed_sum = sum_weight(dot_tn(expert_hidden, slot_grad).astype(halves))

    shared_pre = dot(all_normed, shared_up)
    shared_g, shared_u = shared_pre[:, :units], shared_pre[:, units:]
    shared_hidden = (jax.nn.silu(shared_g) * shared_u).astype(halves)
    gate_shared = jax.nn.sigmoid(
        jnp.sum(all_normed.astype(floats) * gate_vector, axis=-1, keepdims=True)
    )
    shared_grad = (gate_shared * all_grads.astype(floats)).astype(halves)
    hidden_grad = dot(shared_grad, shared_dn)
    shared_pre_grad = jnp.concatenate(
        silu_parts(hidden_grad, shared_g, shared_u), axis=-1
    ).astype(halves)
    shared_part = dot_nt(shared_hidden, shared_dn)
    logit_part = jnp.sum(all_grads.astype(floats) * shared_part, axis=-1)
    su_sum = sum_weight(dot_tn(all_normed, shared_pre_grad).astype(halves))
    sd_sum = sum_weight(dot_tn(shared_grad, shared_hidden).astype(halves))
    ffn_part = dot_nt(shared_pre_grad, shared_up) + from_slots(slot_in_grad)
    out_part = gate_shared * shared_part + gate.reshape(length, 1) * from_slots(expert_out)

    logit_sums = lax.all_to_all(
        logit_part.reshape(count, 1, tok_count), group, split_axis=0, concat_axis=0, tiled=True
    )
    own_gate = jax.nn.sigmoid(
        jnp.sum(normed_ffn.astype(floats) * gate_vector, axis=-1, keepdims=True)
    )
    logit_grad = jnp.sum(logit_sums, axis=0).reshape(tok_count, 1) * own_gate * (1.0 - own_gate)

    def own_sum(part):
        part = part.reshape(-1, 2, tok_count, width)
        mine = lax.dynamic_index_in_dim(part, core, 1, keepdims=False)
        other = lax.dynamic_index_in_dim(part, 1 - core, 1, keepdims=False)
        return group_sum(mine, other.astype(halves))

    layer_sum = resid_mid + own_sum(out_part)
    ffn_grad = own_sum(ffn_part) + logit_grad * gate_vector
    gain_ffn_part = jnp.sum(ffn_grad * unit_ffn, axis=0)
    gate_vector_part = jnp.sum(logit_grad * normed_ffn.astype(floats), axis=0)
    mid_grad = norm_backward(grad_out, ffn_grad, gain_ffn, unit_ffn, stat_ffn)
    mid_low = mid_grad.astype(halves)

    attn_in_grad, gain_attn_part, bias_part, qkv_out, out_weight_out = rows_backward(
        weights, saved, mid_low
    )
    stat_attn = lax.rsqrt(jnp.mean(resid_in * resid_in, axis=-1, keepdims=True) + eps_norm)
    unit_attn = resid_in * stat_attn
    input_grad = norm_backward(mid_grad, attn_in_grad, gain_attn, unit_attn, stat_attn)
    shared_up_out = jnp.concatenate(
        [
            array.reshape(-1, 2, units).transpose(1, 0, 2) for array in cores_in_order(su_sum)
        ],
        axis=-1,
    )
    gain_attn_out, gain_ffn_out, gate_vector_out, bias_out = small_sums(
        [gain_attn_part, gain_ffn_part, gate_vector_part, bias_part], lengths, attn_in_grad
    )
    return (
        layer_sum.astype(halves)[None],
        input_grad[None],
        qkv_out,
        bias_out,
        out_weight_out,
        gain_attn_out,
        gain_ffn_out,
        shared_up_out.astype(floats),
        jnp.concatenate(cores_in_order(sd_sum), axis=-1).T.astype(floats),
        gate_vector_out,
        jnp.stack(cores_in_order(eu_sum)).astype(floats),
        jnp.stack(cores_in_order(ed_sum)).astype(floats),
    )


def shards(*arrays):
    if HEADS % lax.axis_size(group) == 0 and lax.axis_size("dp") == 4 and lax.axis_size("expert") == 4:
        return shards_by_heads(*arrays)
    return shards_by_rows(*arrays)


def solution(mesh):
    placed = (
        P("dp", ("expert", "context"), None),
        P("dp", ("expert", "context"), None),
        P("dp", None),
        P("dp", ("expert", "context"), None),
        P("dp", ("expert", "context"), None),
        P("dp", ("expert", "context"), None),
        P(("expert", "context", "dp"), None),
        P(("expert", "context", "dp")),
        P(("expert", "context", "dp"), None),
        P(("expert", "context", "dp")),
        P(("expert", "context", "dp")),
        P(None, ("context", "dp"), "expert"),
        P("expert", ("context", "dp")),
        P(("expert", "context", "dp")),
        P("expert", ("context", "dp"), None),
        P("expert", ("context", "dp"), None),
    )
    return jax.shard_map(
        shards,
        mesh=mesh,
        in_specs=placed,
        out_specs=(
            P("dp", ("expert", "context"), None),
            P("dp", ("expert", "context"), None),
            P(("expert", "context", "dp"), None),
            P(("expert", "context", "dp")),
            P(("expert", "context", "dp"), None),
            P(("expert", "context", "dp")),
            P(("expert", "context", "dp")),
            P(None, ("context", "dp"), "expert"),
            P("expert", ("context", "dp")),
            P(("expert", "context", "dp")),
            P("expert", ("context", "dp"), None),
            P("expert", ("context", "dp"), None),
        ),
        check_vma=False,
    )
```

time: 828 us -> 754 us (0.911)
  matrix products: 180 us -> 0 us
  Pallas kernels: 5.12 us -> 177 us
  local copies, waits for them, and re-layouts: 95.3 us -> 48.4 us
  other arithmetic: 119 us -> 77.5 us
  starting transfers between devices: 67.4 us -> 94 us
    all_to_all x11 -> x4, waiting for transfers between devices: 256 us -> 45.9 us  [the longest x1 22 us: shards_by_heads(): lax.all_to_all(after(logit_part.reshape(count, 1, tok_count), ffn_other),...]
    ppermute x0 -> x28, waiting for transfers between devices: none -> 182 us  [the longest x3 60.6 us: line_gather(): second = lax.ppermute(block, 'expert', cross_line)]
    dot_general x28 -> x0, matrix products: 180 us -> none  [the longest x6 55 us: dot(): return jnp.dot(left, right, preferred_element_type=floats)]
    pallas_call x0 -> x11, Pallas kernels: none -> 176 us  [the longest x5 56.1 us: weight_grad(): kernel_call(kernel, jax.ShapeDtypeStruct((rows, wide), halves), [pl.Block...]
    ppermute x0 -> x28, starting transfers between devices: none -> 58.9 us  [the longest x3 14.1 us: line_gather(): lower = lax.ppermute(block, 'expert', up_line)]
    all_to_all x11 -> x4, starting transfers between devices: 47.4 us -> 14.1 us  [the longest x1 4.21 us: shards_by_heads(): lax.all_to_all(after(total[..., :3 * piece], attn_in_grad), group, split_...]
    convert_element_type x10 -> x5, local copies, waits for them, and re-layouts: 31.9 us -> 5.96 us  [the longest x2 3.43 us: shards_by_heads(): qkv_out = qkv_total.reshape(count, each, 3, piece).transpose(1, 2, 0, 3)....]
    convert_element_type x18 -> x10, other arithmetic: 36.9 us -> 12.3 us  [the longest x4 5.88 us: line_sum(): passed = (rows[2].astype(floats) + corner.astype(floats)).astype(halves)]
  transfers between devices with their start and end apart: 46 -> 63, of which waited for: 20 -> 34; matrix products, arithmetic and copies ran while one was open for 45% -> 15% of each run, Pallas kernels for 1% -> 24%
where the time goes in v3:
time: 754 us; the launch traced here: 744 us
  waiting for transfers between devices  332 us (44%)
  Pallas kernels  177 us (23%)
  starting transfers between devices  94 us (12%)
  other arithmetic  77.5 us (10%)
  local copies, waits for them, and re-layouts  48.4 us (6%)
  between operations  15.4 us (2%)
    ppermute x3, waiting for transfers between devices, line_gather(): second = lax.ppermute(block, 'expert', cross_line)  60.6 us
    pallas_call x5, Pallas kernels, weight_grad(): kernel_call(kernel, jax.ShapeDtypeStruct((rows, wide), halves), [pl.Block...  56.1 us
    ppermute x10, waiting for transfers between devices, dp_step(): return lax.ppermute(value, 'dp', [(i, i ^ step) for i in range(count)])  54.3 us
    ppermute x4, waiting for transfers between devices, line_sum(): second = lax.ppermute(passed, 'expert', cross_line)  47.7 us
    pallas_call x1, Pallas kernels, expert_pass(): kernel_call(kernel, (shape((count, width), halves), shape((count, width),...  37.5 us
    pallas_call x1, Pallas kernels, shared_pass(): kernel_call(kernel, (half_shape,) * 4 + (shape((length, 2 * units), halve...  33.7 us
    ppermute x3, waiting for transfers between devices, line_gather(): third = lax.ppermute(second, 'expert', [(2, 3), (1, 0)])  26.7 us
    ppermute x3, waiting for transfers between devices, line_gather(): upper = lax.ppermute(block, 'expert', down_line)  24.1 us
  transfers between devices with their start and end apart: 63, of which 34 were waited for; matrix products, arithmetic and copies ran while one was open for 15% of the time, Pallas kernels for 24%

profile of v3, /device:TPU:0, one launch (start us, length us, event | category | flops | bytes accessed | tf_op | source)
XLA Modules:
  0.0 744.4 jit_solution(17899139273678078825)
XLA Ops:
  11.2 6.3 all-to-all-start
  17.6 23.7 %all-to-all-done = bf16[8,64,896]{2,1,0:T(8,128)(2,1)S(1)} async-done(((bf16[8,64,896]{2,1,0:T(8,128)(2,1)}), bf16[8,64,896]{2,1,0:T(8,128)(2,1)S(1)}, u32[]{:S(2)}, u32[]{:S(2)}) %all-to-all-start) | async-done | bytes 917536 | tf_op jit(solution)/shard_map/all_to_all | solution.py:705
  104.3 20.2 %collective-permute-done.4.refs_4_ = bf16[4,64,1152]{2,1,0:T(8,128)(2,1)} collective-permute-done((bf16[4,64,1152]{2,1,0:T(8,128)(2,1)}, bf16[4,64,1152]{2,1,0:T(8,128)(2,1)}, u32[]{:S(2)}, u32[]{:S(2)}) %collective-permute-start.4) | collective-permute-done | bytes 589856 | tf_op jit(solution)/shard_map/ppermute | solution.py:76
  133.1 18.9 %shard_map.248 = (bf16[2048,768]{1,0:T(8,128)(2,1)}, bf16[256,2048]{1,0:T(8,128)(2,1)}, bf16[1024,2048]{1,0:T(8,128)(2,1)}, bf16[1024,256]{1,0:T(8,128)(2,1)}, b...) custom-call(s32[2]{0:T(128)} %pad_add_fusion.core_ref, ...), custom_call_target="tpu_custom_call" | custom-call | bytes 1024 | tf_op jit(solution)/shard_map/pallas_call | solution.py:391
  159.1 13.8 %collective-permute-done.5 = bf16[128,2048]{1,0:T(8,128)(2,1)S(1)} collective-permute-done((bf16[128,2048]{1,0:T(8,128)(2,1)S(1)}, bf16[128,2048]{1,0:T(8,128)(2,1)S(1)}, u32[]{:S(2)}, u32[]{:S(2)}) %collective-permute-start.5) | collective-permute-done | bytes 524320 | tf_op jit(solution)/shard_map/ppermute | solution.py:185
  177.9 11.0 %collective-permute-done.6 = bf16[128,2048]{1,0:T(8,128)(2,1)S(1)} collective-permute-done((bf16[128,2048]{1,0:T(8,128)(2,1)S(1)}, bf16[128,2048]{1,0:T(8,128)(2,1)S(1)}, u32[]{:S(2)}, u32[]{:S(2)}) %collective-permute-start.6) | collective-permute-done | bytes 524320 | tf_op jit(solution)/shard_map/ppermute | solution.py:188
  202.7 6.9 collective-permute-done.12
  212.5 16.3 %collective-permute-done.18.refs_6_ = bf16[176,2048]{1,0:T(8,128)(2,1)S(1)} collective-permute-done((bf16[176,2048]{1,0:T(8,128)(2,1)S(1)}, bf16[176,2048]{1,0:T(8,128)(2,1)S(1)}, u32[]{:S(2)}, u32[]{:S(2)}) %collective-permute-start.18) | collective-permute-done | bytes 720928 | tf_op jit(solution)/shard_map/ppermute | solution.py:76
  234.2 11.1 %collective-permute-done.17.refs_5_ = bf16[176,2048]{1,0:T(8,128)(2,1)S(1)} collective-permute-done((bf16[176,2048]{1,0:T(8,128)(2,1)S(1)}, bf16[176,2048]{1,0:T(8,128)(2,1)S(1)}, u32[]{:S(2)}, u32[]{:S(2)}) %collective-permute-start.17) | collective-permute-done | bytes 720928 | tf_op jit(solution)/shard_map/ppermute | solution.py:76
  254.3 21.5 %collective-permute-done.19 = bf16[128,2048]{1,0:T(8,128)(2,1)S(1)} collective-permute-done((bf16[128,2048]{1,0:T(8,128)(2,1)S(1)}, bf16[128,2048]{1,0:T(8,128)(2,1)S(1)}, u32[]{:S(2)}, u32[]{:S(2)}) %collective-permute-start.19) | collective-permute-done | bytes 524320 | tf_op jit(solution)/shard_map/ppermute | solution.py:185
  284.8 7.7 %collective-permute-done.20 = bf16[128,2048]{1,0:T(8,128)(2,1)S(1)} collective-permute-done((bf16[128,2048]{1,0:T(8,128)(2,1)S(1)}, bf16[128,2048]{1,0:T(8,128)(2,1)S(1)}, u32[]{:S(2)}, u32[]{:S(2)}) %collective-permute-start.20) | collective-permute-done | bytes 524320 | tf_op jit(solution)/shard_map/ppermute | solution.py:188
  292.5 9.9 %collective-permute-done.24 = bf16[128,2048]{1,0:T(8,128)(2,1)S(1)} collective-permute-done((bf16[128,2048]{1,0:T(8,128)(2,1)S(1)}, bf16[128,2048]{1,0:T(8,128)(2,1)S(1)}, u32[]{:S(2)}, u32[]{:S(2)}) %collective-permute-start.24) | collective-permute-done | bytes 524320 | tf_op jit(solution)/shard_map/ppermute | solution.py:187
  307.2 37.5 %shard_map.249 = (bf16[576,2048]{1,0:T(8,128)(2,1)}, bf16[576,2048]{1,0:T(8,128)(2,1)}, bf16[576,1408]{1,0:T(8,128)(2,1)}, bf16[576,2816]{1,0:T(8,128)(2,1)}, bf...) custom-call(s32[8]{0:T(128)} %stack.168.place_ref, s32[4,1,256]{2,1,0:T(1,128)} %bitcast.275, f32[4,1,256]{2,1,0:T(1,128)} %bitcast.273, ...), custom_call_target="tpu_custom_call" | custom-call | bytes 1024 | tf_op jit(solution)/shard_map/pallas_call | solution.py:573
  344.8 15.5 %shard_map.250 = bf16[2048,2816]{1,0:T(8,128)(2,1)} custom-call(bf16[576,2048]{1,0:T(8,128)(2,1)} %get-tuple-element.83.refs_0_, bf16[576,2816]{1,0:T(8,128)(2,1)} %get-tuple-element.84.refs_1_), custom_call_target="tpu_custom_call" | custom-call | bytes 1024 | tf_op jit(solution)/shard_map/pallas_call | solution.py:682
  363.7 10.4 %shard_map.251 = bf16[1408,2048]{1,0:T(8,128)(2,1)} custom-call(bf16[576,1408]{1,0:T(8,128)(2,1)} %get-tuple-element.85.refs_0_, bf16[576,2048]{1,0:T(8,128)(2,1)} %get-tuple-element.86.refs_1_), custom_call_target="tpu_custom_call" | custom-call | bytes 1024 | tf_op jit(solution)/shard_map/pallas_call | solution.py:682
  374.1 33.7 %shard_map.253 = (bf16[4,128,2048]{2,1,0:T(8,128)(2,1)}, bf16[4,128,2048]{2,1,0:T(8,128)(2,1)}, bf16[4,128,2048]{2,1,0:T(8,128)(2,1)}, bf16[4,128,2048]{2,1,0:T(...) custom-call(s32[1024,1]{1,0:T(8,128)} %copy.116.slot_ref, ...), custom_call_target="tpu_custom_call" | custom-call | bytes 1024 | tf_op jit(solution)/shard_map/pallas_call | solution.py:638
  407.8 12.8 %shard_map.254.refs_2_ = bf16[2048,2304]{1,0:T(8,128)(2,1)} custom-call(bf16[4,128,2048]{2,1,0:T(8,128)(2,1)} %copy-done.4, bf16[4,128,2048]{2,1,0:T(8,128)(2,1)} %collective-permute-done.26.x_other.refs_1_, bf16[1024,1536]{1,0:T(8,128)(2,1)} %get-tuple-element.100.refs_2_), custom_call_target="tpu_custom_call" | custom-call | bytes 1024 | tf_op jit(solution)/shard_map/pallas_call | solution.py:682
  420.6 8.7 %shard_map.255 = bf16[2048,2304]{1,0:T(8,128)(2,1)} custom-call(bf16[1024,2048]{1,0:T(8,128)(2,1)} %get-tuple-element.98.refs_0_, bf16[1024,768]{1,0:T(8,128)(2,1)} %get-tuple-element.99.refs_1_, bf16[2048,2304]{1,0:T(8,128)(2,1)} %shard_map.254.refs_2_), custom_call_target="tpu_custom_call", output_to_operand_aliasing={{}: (2, {})} | custom-call | bytes 1024 | tf_op jit(solution)/shard_map/pallas_call | solution.py:682
  442.6 7.8 %collective-permute-done.32 = bf16[128,2048]{1,0:T(8,128)(2,1)} collective-permute-done((bf16[128,2048]{1,0:T(8,128)(2,1)}, bf16[128,2048]{1,0:T(8,128)(2,1)}, u32[]{:S(2)}, u32[]{:S(2)}) %collective-permute-start.32) | collective-permute-done | bytes 524320 | tf_op jit(solution)/shard_map/ppermute | solution.py:201
  460.2 22.0 %all-to-all-done.2 = f32[8,1,128]{2,1,0:T(1,128)S(1)} async-done(((f32[8,1,128]{2,1,0:T(1,128)}), f32[8,1,128]{2,1,0:T(1,128)S(1)}, u32[]{:S(2)}, u32[]{:S(2)}) %all-to-all-start.2) | async-done | bytes 4128 | tf_op jit(solution)/shard_map/all_to_all | solution.py:1010
  486.1 25.3 %collective-permute-done.34 = bf16[128,2048]{1,0:T(8,128)(2,1)S(1)} collective-permute-done((bf16[128,2048]{1,0:T(8,128)(2,1)S(1)}, bf16[128,2048]{1,0:T(8,128)(2,1)S(1)}, u32[]{:S(2)}, u32[]{:S(2)}) %collective-permute-start.34) | collective-permute-done | bytes 524320 | tf_op jit(solution)/shard_map/ppermute | solution.py:185
  514.0 6.0 collective-permute-start.37
  520.0 8.1 %collective-permute-done.35 = bf16[128,2048]{1,0:T(8,128)(2,1)S(1)} collective-permute-done((bf16[128,2048]{1,0:T(8,128)(2,1)S(1)}, bf16[128,2048]{1,0:T(8,128)(2,1)S(1)}, u32[]{:S(2)}, u32[]{:S(2)}) %collective-permute-start.35) | collective-permute-done | bytes 524320 | tf_op jit(solution)/shard_map/ppermute | solution.py:188
  528.1 10.4 %collective-permute-done.36 = bf16[128,2048]{1,0:T(8,128)(2,1)} collective-permute-done((bf16[128,2048]{1,0:T(8,128)(2,1)S(1)}, bf16[128,2048]{1,0:T(8,128)(2,1)}, u32[]{:S(2)}, u32[]{:S(2)}) %collective-permute-start.36) | collective-permute-done | bytes 524320 | tf_op jit(solution)/shard_map/ppermute | solution.py:187
  551.9 21.2 %shard_map.256 = (bf16[1024,768]{1,0:T(8,128)(2,1)}, bf16[4,128,2048]{2,1,0:T(8,128)(2,1)}, bf16[4,128,2048]{2,1,0:T(8,128)(2,1)}, f32[1,2048]{1,0:T(1,128)}, f3...) custom-call(s32[2]{0:T(128)} %pad_add_fusion.core_ref, bf16[4,128,2048]{2,1,0:T(8,128)(2,1)} %copy-done.10, ...), custom_call_target="tpu_custom_call" | custom-call | bytes 1024 | tf_op jit(solution)/shard_map/pallas_call | solution.py:482
  574.5 8.7 %shard_map.257 = bf16[2048,768]{1,0:T(8,128)(2,1)} custom-call(bf16[1024,2048]{1,0:T(8,128)(2,1)} %get-tuple-element.113.refs_0_, bf16[1024,768]{1,0:T(8,128)(2,1)} %get-tuple-element.114.refs_1_), custom_call_target="tpu_custom_call" | custom-call | bytes 1024 | tf_op jit(solution)/shard_map/pallas_call | solution.py:682
  583.1 4.8 pad_maximum_fusion
  590.9 24.4 %collective-permute-done.41 = bf16[128,2048]{1,0:T(8,128)(2,1)S(1)} collective-permute-done((bf16[128,2048]{1,0:T(8,128)(2,1)S(1)}, bf16[128,2048]{1,0:T(8,128)(2,1)S(1)}, u32[]{:S(2)}, u32[]{:S(2)}) %collective-permute-start.41) | collective-permute-done | bytes 524320 | tf_op jit(solution)/shard_map/ppermute | solution.py:205
  631.3 9.2 %reduce-scatter.9.cloned.1.call-done.sums_ref = bf16[2,256,2304]{2,1,0:T(8,128)(2,1)} async-done(((bf16[2,1024,2304]{2,1,0:T(8,128)(2,1)}), bf16[2,256,2304]{2,1,0:T(8,128)(2,1)}) %reduce-scatter.9.cloned.1.call-update) | async-done | bytes 2359312 | tf_op jit(solution)/shard_map/reduce_scatter | solution.py:135
  662.3 23.4 %collective-permute-done.47 = bf16[128,2048]{1,0:T(8,128)(2,1)S(1)} collective-permute-done((bf16[128,2048]{1,0:T(8,128)(2,1)S(1)}, bf16[128,2048]{1,0:T(8,128)(2,1)S(1)}, u32[]{:S(2)}, u32[]{:S(2)}) %collective-permute-start.47) | collective-permute-done | bytes 524320 | tf_op jit(solution)/shard_map/ppermute | solution.py:205
  694.4 4.7 all-to-all-done.4
  717.7 14.6 %all-to-all-done.3 = bf16[8,64,768]{2,1,0:T(8,128)(2,1)} async-done(((bf16[8,64,768]{2,1,0:T(8,128)(2,1)}), bf16[8,64,768]{2,1,0:T(8,128)(2,1)}, u32[]{:S(2)}, u32[]{:S(2)}) %all-to-all-start.3) | async-done | bytes 786464 | tf_op jit(solution)/shard_map/all_to_all | solution.py:1044
  (354 shorter events, 252.6 us)
Async XLA Ops:
  11.2 30.1 %all-to-all-start = ((bf16[8,64,896]{2,1,0:T(8,128)(2,1)}), bf16[8,64,896]{2,1,0:T(8,128)(2,1)S(1)}, u32[]{:S(2)}, u32[]{:S(2)}) async-start(bf16[8,64,896]{2,1,0:T(8,128)(2,1)} %pad_maximum_fusion.7), calls=%async_computation | async-start | bytes 1835008 | tf_op jit(solution)/shard_map/all_to_all | solution.py:705
  17.5 115.6 %all-gather.4.cloned.1.call-start = ((), (), s32[]{:S(2)}) async-start(), calls=%async_computation.9 | async-start | bytes 4718592 | tf_op jit(solution)/shard_map/all_gather | solution.py:915
  41.5 265.7 %all-gather.6.cloned.1.call-start = ((), (), s32[]{:S(2)}) async-start(), calls=%async_computation.10 | async-start | bytes 14417920 | tf_op jit(solution)/shard_map/all_gather | solution.py:147
  68.6 28.2 %collective-permute-start.1 = (bf16[8,64,1152]{2,1,0:T(8,128)(2,1)S(1)}, bf16[8,64,1152]{2,1,0:T(8,128)(2,1)S(1)}, u32[]{:S(2)}, u32[]{:S(2)}) collective-permute-start(bf16[8,64,1152]{2,1,0:T(8,128)(2,1)S(1)} %pad_maximum_fusion.6.refs_0_), channel_id=1, source_target_pairs={{0,2},{1,3},{2,0},{3,1},{4,6},{5,7},{6,4},{7,5},{8,10},{9,11},{10,... | collective-permute-start | bytes 3538952 | tf_op jit(solution)/shard_map/ppermute | solution.py:76
  70.1 29.1 %collective-permute-start = (bf16[8,64,1152]{2,1,0:T(8,128)(2,1)S(1)}, bf16[8,64,1152]{2,1,0:T(8,128)(2,1)S(1)}, u32[]{:S(2)}, u32[]{:S(2)}) collective-permute-start(bf16[8,64,1152]{2,1,0:T(8,128)(2,1)S(1)} %pad_maximum_fusion.6.refs_0_), channel_id=1, source_target_pairs={{0,1},{1,0},{2,3},{3,2},{4,5},{5,4},{6,7},{7,6},{8,9},{9,8},{10,11... | collective-permute-start | bytes 3538952 | tf_op jit(solution)/shard_map/ppermute | solution.py:76
  76.3 297.8 %all-gather.8.cloned.1.call-start = ((), (), s32[]{:S(2)}) async-start(), calls=%async_computation.11 | async-start | bytes 11796480 | tf_op jit(solution)/shard_map/all_gather | solution.py:147
  97.8 26.7 %collective-permute-start.4 = (bf16[4,64,1152]{2,1,0:T(8,128)(2,1)}, bf16[4,64,1152]{2,1,0:T(8,128)(2,1)}, u32[]{:S(2)}, u32[]{:S(2)}) collective-permute-start(bf16[4,64,1152]{2,1,0:T(8,128)(2,1)} %slice.224), channel_id=1, source_target_pairs={{0,1},{1,0},{2,3},{3,2},{4,5},{5,4},{6,7},{7,6},{8,9},{9,8},{10,11... | collective-permute-start | bytes 1769480 | tf_op jit(solution)/shard_map/ppermute | solution.py:76
  100.2 27.5 %collective-permute-start.3 = (bf16[4,64,1152]{2,1,0:T(8,128)(2,1)}, bf16[4,64,1152]{2,1,0:T(8,128)(2,1)}, u32[]{:S(2)}, u32[]{:S(2)}) collective-permute-start(bf16[4,64,1152]{2,1,0:T(8,128)(2,1)} %slice.223), channel_id=1, source_target_pairs={{0,2},{1,3},{2,0},{3,1},{4,6},{5,7},{6,4},{7,5},{8,10},{9,11},{10,... | collective-permute-start | bytes 1769480 | tf_op jit(solution)/shard_map/ppermute | solution.py:76
  152.0 376.1 %reduce-scatter.5.cloned.1.call-start = ((), (), s32[]{:S(2)}) async-start(), calls=%async_computation.12 | async-start | bytes 14417920 | tf_op jit(solution)/shard_map/reduce_scatter | solution.py:135
  198.0 30.8 %collective-permute-start.18 = (bf16[176,2048]{1,0:T(8,128)(2,1)S(1)}, bf16[176,2048]{1,0:T(8,128)(2,1)S(1)}, u32[]{:S(2)}, u32[]{:S(2)}) collective-permute-start(bf16[176,2048]{1,0:T(8,128)(2,1)S(1)} %collective-permute-done.16.refs_4_), channel_id=1, source_target_pairs={{0,2},{1,3},{2,0},{3,1},{4,6},{5,7},{6,4},{7,5},{8,10},{9,11},{10,... | collective-permute-start | bytes 2162696 | tf_op jit(solution)/shard_map/ppermute | solution.py:76
  200.6 32.4 %collective-permute-start.14 = (bf16[176,2048]{1,0:T(8,128)(2,1)S(1)}, bf16[176,2048]{1,0:T(8,128)(2,1)S(1)}, u32[]{:S(2)}, u32[]{:S(2)}) collective-permute-start(bf16[176,2048]{1,0:T(8,128)(2,1)S(1)} %get-tuple-element.78.refs_0_), channel_id=1, source_target_pairs={{0,1},{1,0},{2,3},{3,2},{4,5},{5,4},{6,7},{7,6},{8,9},{9,8},{10,11... | collective-permute-start | bytes 2162696 | tf_op jit(solution)/shard_map/ppermute | solution.py:76
  200.6 44.8 %collective-permute-start.17 = (bf16[176,2048]{1,0:T(8,128)(2,1)S(1)}, bf16[176,2048]{1,0:T(8,128)(2,1)S(1)}, u32[]{:S(2)}, u32[]{:S(2)}) collective-permute-start(bf16[176,2048]{1,0:T(8,128)(2,1)S(1)} %collective-permute-done.16.refs_4_), channel_id=1, source_target_pairs={{0,1},{1,0},{2,3},{3,2},{4,5},{5,4},{6,7},{7,6},{8,9},{9,8},{10,11... | collective-permute-start | bytes 2162696 | tf_op jit(solution)/shard_map/ppermute | solution.py:76
  202.6 43.8 %collective-permute-start.15 = (bf16[176,2048]{1,0:T(8,128)(2,1)S(1)}, bf16[176,2048]{1,0:T(8,128)(2,1)}, u32[]{:S(2)}, u32[]{:S(2)}) collective-permute-start(bf16[176,2048]{1,0:T(8,128)(2,1)S(1)} %get-tuple-element.78.refs_0_), channel_id=1, source_target_pairs={{0,2},{1,3},{2,0},{3,1},{4,6},{5,7},{6,4},{7,5},{8,10},{9,11},{10,... | collective-permute-start | bytes 2162696 | tf_op jit(solution)/shard_map/ppermute | solution.py:76
  210.6 36.0 %collective-permute-start.13 = (bf16[128,2048]{1,0:T(8,128)(2,1)}, bf16[128,2048]{1,0:T(8,128)(2,1)}, u32[]{:S(2)}, u32[]{:S(2)}) collective-permute-start(bf16[128,2048]{1,0:T(8,128)(2,1)} %fusion.24), channel_id=1, source_target_pairs={{0,16},{8,24},{16,0},{24,8},{1,17},{9,25},{17,1},{25,9},{2,18},{10... | collective-permute-start | bytes 1572872 | tf_op jit(solution)/shard_map/ppermute | solution.py:205
  245.3 39.4 %collective-permute-start.23 = (bf16[4,128,2048]{2,1,0:T(8,128)(2,1)S(1)}, bf16[4,128,2048]{2,1,0:T(8,128)(2,1)}, u32[]{:S(2)}, u32[]{:S(2)}) collective-permute-start(bf16[4,128,2048]{2,1,0:T(8,128)(2,1)S(1)} %pad_maximum_fusion.3.g_mine), channel_id=1, source_target_pairs={{0,4},{4,0},{1,5},{5,1},{2,6},{6,2},{3,7},{7,3},{8,12},{12,8},{9,1... | collective-permute-start | bytes 6291464 | tf_op jit(solution)/shard_map/ppermute | solution.py:80
  246.4 34.2 %collective-permute-start.22 = (bf16[176,2048]{1,0:T(8,128)(2,1)}, bf16[176,2048]{1,0:T(8,128)(2,1)S(1)}, u32[]{:S(2)}, u32[]{:S(2)}) collective-permute-start(bf16[176,2048]{1,0:T(8,128)(2,1)} %copy-done.27), channel_id=1, source_target_pairs={{0,1},{1,0},{2,3},{3,2},{4,5},{5,4},{6,7},{7,6},{8,9},{9,8},{10,11... | collective-permute-start | bytes 2162696 | tf_op jit(solution)/shard_map/ppermute | solution.py:76
  253.0 31.8 %collective-permute-start.21 = (bf16[176,2048]{1,0:T(8,128)(2,1)S(1)}, bf16[176,2048]{1,0:T(8,128)(2,1)S(1)}, u32[]{:S(2)}, u32[]{:S(2)}) collective-permute-start(bf16[176,2048]{1,0:T(8,128)(2,1)S(1)} %copy-done.29), channel_id=1, source_target_pairs={{0,2},{1,3},{2,0},{3,1},{4,6},{5,7},{6,4},{7,5},{8,10},{9,11},{10,... | collective-permute-start | bytes 2162696 | tf_op jit(solution)/shard_map/ppermute | solution.py:76
  360.3 260.5 %reduce-scatter.11.cloned.1.call-start = ((), (), s32[]{:S(2)}) async-start(), calls=%async_computation.15 | async-start | bytes 7208960 | tf_op jit(solution)/shard_map/reduce_scatter | solution.py:135
  429.4 211.2 %reduce-scatter.9.cloned.1.call-start = ((), (), s32[]{:S(2)}) async-start(), calls=%async_computation.14 | async-start | bytes 11796480 | tf_op jit(solution)/shard_map/reduce_scatter | solution.py:135
  440.0 42.3 %collective-permute-start.30 = (bf16[128,2048]{1,0:T(8,128)(2,1)}, bf16[128,2048]{1,0:T(8,128)(2,1)S(1)}, u32[]{:S(2)}, u32[]{:S(2)}) collective-permute-start(bf16[128,2048]{1,0:T(8,128)(2,1)} %get-tuple-element.148), channel_id=1, source_target_pairs={{0,8},{8,16},{16,24},{1,9},{9,17},{17,25},{2,10},{10,18},{18,26},{... | collective-permute-start | bytes 1572872 | tf_op jit(solution)/shard_map/ppermute | solution.py:202
  441.3 41.0 %collective-permute-start.31 = (bf16[128,2048]{1,0:T(8,128)(2,1)}, bf16[128,2048]{1,0:T(8,128)(2,1)S(1)}, u32[]{:S(2)}, u32[]{:S(2)}) collective-permute-start(bf16[128,2048]{1,0:T(8,128)(2,1)} %get-tuple-element.147), channel_id=1, source_target_pairs={{8,0},{16,8},{24,16},{9,1},{17,9},{25,17},{10,2},{18,10},{26,18},{... | collective-permute-start | bytes 1572872 | tf_op jit(solution)/shard_map/ppermute | solution.py:203
  452.0 31.1 %collective-permute-start.33 = (bf16[128,2048]{1,0:T(8,128)(2,1)S(1)}, bf16[128,2048]{1,0:T(8,128)(2,1)}, u32[]{:S(2)}, u32[]{:S(2)}) collective-permute-start(bf16[128,2048]{1,0:T(8,128)(2,1)S(1)} %fusion.20), channel_id=1, source_target_pairs={{0,16},{8,24},{16,0},{24,8},{1,17},{9,25},{17,1},{25,9},{2,18},{10... | collective-permute-start | bytes 1572872 | tf_op jit(solution)/shard_map/ppermute | solution.py:205
  456.5 25.8 %all-to-all-start.2 = ((f32[8,1,128]{2,1,0:T(1,128)}), f32[8,1,128]{2,1,0:T(1,128)S(1)}, u32[]{:S(2)}, u32[]{:S(2)}) async-start(f32[8,1,128]{2,1,0:T(1,128)} %bitcast.61), calls=%async_computation.2 | async-start | bytes 8192 | tf_op jit(solution)/shard_map/all_to_all | solution.py:1010
  459.8 245.1 %reduce-scatter.7.cloned.1.call-start = ((), (), s32[]{:S(2)}) async-start(), calls=%async_computation.13 | async-start | bytes 5242880 | tf_op jit(solution)/shard_map/reduce_scatter | solution.py:1040
  459.8 60.2 %collective-permute-start.28 = (bf16[4,128,2048]{2,1,0:T(8,128)(2,1)}, bf16[4,128,2048]{2,1,0:T(8,128)(2,1)}, u32[]{:S(2)}, u32[]{:S(2)}) collective-permute-start(bf16[4,128,2048]{2,1,0:T(8,128)(2,1)} %get-tuple-element.93), channel_id=1, source_target_pairs={{0,4},{4,0},{1,5},{5,1},{2,6},{6,2},{3,7},{7,3},{8,12},{12,8},{9,1... | collective-permute-start | bytes 6291464 | tf_op jit(solution)/shard_map/ppermute | solution.py:80
  512.7 25.8 %collective-permute-start.36 = (bf16[128,2048]{1,0:T(8,128)(2,1)S(1)}, bf16[128,2048]{1,0:T(8,128)(2,1)}, u32[]{:S(2)}, u32[]{:S(2)}) collective-permute-start(bf16[128,2048]{1,0:T(8,128)(2,1)S(1)} %fusion.53), channel_id=1, source_target_pairs={{8,0},{16,8},{24,16},{9,1},{17,9},{25,17},{10,2},{18,10},{26,18},{... | collective-permute-start | bytes 1572872 | tf_op jit(solution)/shard_map/ppermute | solution.py:187
  544.5 43.4 %collective-permute-start.40 = (bf16[128,2048]{1,0:T(8,128)(2,1)}, bf16[128,2048]{1,0:T(8,128)(2,1)}, u32[]{:S(2)}, u32[]{:S(2)}) collective-permute-start(bf16[128,2048]{1,0:T(8,128)(2,1)} %get-tuple-element.140), channel_id=1, source_target_pairs={{24,16},{0,8},{25,17},{1,9},{26,18},{2,10},{27,19},{3,11},{28,20},... | collective-permute-start | bytes 1572872 | tf_op jit(solution)/shard_map/ppermute | solution.py:201
  546.8 44.0 %collective-permute-start.38 = (bf16[128,2048]{1,0:T(8,128)(2,1)S(1)}, bf16[128,2048]{1,0:T(8,128)(2,1)}, u32[]{:S(2)}, u32[]{:S(2)}) collective-permute-start(bf16[128,2048]{1,0:T(8,128)(2,1)S(1)} %get-tuple-element.142), channel_id=1, source_target_pairs={{0,8},{8,16},{16,24},{1,9},{9,17},{17,25},{2,10},{10,18},{18,26},{... | collective-permute-start | bytes 1572872 | tf_op jit(solution)/shard_map/ppermute | solution.py:202
  548.9 42.0 %collective-permute-start.39 = (bf16[128,2048]{1,0:T(8,128)(2,1)S(1)}, bf16[128,2048]{1,0:T(8,128)(2,1)}, u32[]{:S(2)}, u32[]{:S(2)}) collective-permute-start(bf16[128,2048]{1,0:T(8,128)(2,1)S(1)} %get-tuple-element.141), channel_id=1, source_target_pairs={{8,0},{16,8},{24,16},{9,1},{17,9},{25,17},{10,2},{18,10},{26,18},{... | collective-permute-start | bytes 1572872 | tf_op jit(solution)/shard_map/ppermute | solution.py:203
  630.9 80.4 %collective-permute-start.49 = (bf16[256,2816]{1,0:T(8,128)(2,1)}, bf16[256,2816]{1,0:T(8,128)(2,1)}, u32[]{:S(2)}, u32[]{:S(2)}) collective-permute-start(bf16[256,2816]{1,0:T(8,128)(2,1)} %select_bitcast_fusion), channel_id=1, source_target_pairs={{0,4},{4,0},{1,5},{5,1},{2,6},{6,2},{3,7},{7,3},{8,12},{12,8},{9,1... | collective-permute-start | bytes 4325384 | tf_op jit(solution)/shard_map/ppermute | solution.py:80
  642.9 57.4 %collective-permute-start.48 = (bf16[256,2304]{1,0:T(8,128)(2,1)}, bf16[256,2304]{1,0:T(8,128)(2,1)}, u32[]{:S(2)}, u32[]{:S(2)}) collective-permute-start(bf16[256,2304]{1,0:T(8,128)(2,1)} %dynamic-slice_bitcast_fusion.1), channel_id=1, source_target_pairs={{0,4},{4,0},{1,5},{5,1},{2,6},{6,2},{3,7},{7,3},{8,12},{12,8},{9,1... | collective-permute-start | bytes 3538952 | tf_op jit(solution)/shard_map/ppermute | solution.py:80
  649.3 36.4 %collective-permute-start.47 = (bf16[128,2048]{1,0:T(8,128)(2,1)S(1)}, bf16[128,2048]{1,0:T(8,128)(2,1)S(1)}, u32[]{:S(2)}, u32[]{:S(2)}) collective-permute-start(bf16[128,2048]{1,0:T(8,128)(2,1)S(1)} %fusion.14), channel_id=1, source_target_pairs={{0,16},{8,24},{16,0},{24,8},{1,17},{9,25},{17,1},{25,9},{2,18},{10... | collective-permute-start | bytes 1572872 | tf_op jit(solution)/shard_map/ppermute | solution.py:205
  (89 other events, 1723.2 us)
Sparse Core Ops, SparseCore 0:
  41.6 47.4 all-gather.3
  91.5 133.7 all-gather.5
  227.7 115.6 all-gather.7
  360.4 112.7 reduce-scatter.4
  476.7 65.8 reduce-scatter.10
  545.5 94.9 reduce-scatter.8
  643.5 52.7 reduce-scatter.6

commit v4 on v3

--- a/solution.py
+++ b/solution.py
@@ -2,6 +2,7 @@
 
 import jax
 import jax.numpy as jnp
+import numpy as np
 from jax import lax
 from jax.experimental import pallas as pl
 from jax.experimental.pallas import tpu as pltpu
@@ -175,38 +176,34 @@
     return jnp.sum(along_expert(rows).astype(floats), axis=0)
 
 
-up_line = [(0, 1), (1, 2), (2, 3)]
-down_line = [(1, 0), (2, 1), (3, 2)]
-cross_line = [(0, 2), (1, 3), (2, 0), (3, 1)]
+def along_line(value, step):
+    count = lax.axis_size("expert")
+    return lax.ppermute(value, "expert", [(i, (i + step) % count) for i in range(count)])
+
+
+def line_blocks(block):
+    count = lax.axis_size("expert")
+    return [block] + [along_line(block, count - k) for k in range(1, count)]
 
 
 def line_gather(block, *pins):
-    here = lax.axis_index("expert")
-    second = lax.ppermute(block, "expert", cross_line)
-    lower = lax.ppermute(block, "expert", up_line)
-    upper = lax.ppermute(block, "expert", down_line)
-    third = lax.ppermute(second, "expert", [(2, 3), (1, 0)])
-    third = after(third, *pins) if pins else third
-    mine = jnp.stack(
-        [block, jnp.where(here == 3, third, upper), second, jnp.where(here == 0, third, lower)]
-    )
-    return mine
+    got = line_blocks(block)
+    got[-1] = after(got[-1], *pins)
+    return jnp.stack(got)
 
 
 def line_sum(mine, other, *pins):
-    here = lax.axis_index("expert")
     rows = [
-        (mine[k].astype(floats) + other[k].astype(floats)).astype(halves) for k in range(4)
+        (mine[k].astype(floats) + other[k].astype(floats)).astype(halves)
+        for k in range(mine.shape[0])
     ]
-    corner = lax.ppermute(jnp.where(here == 3, rows[1], rows[3]), "expert", [(3, 2), (0, 1)])
-    lower = lax.ppermute(rows[1], "expert", up_line)
-    upper = lax.ppermute(rows[3], "expert", down_line)
-    passed = (rows[2].astype(floats) + corner.astype(floats)).astype(halves)
-    second = lax.ppermute(passed, "expert", cross_line)
-    second = after(second, *pins) if pins else second
-    return (
-        rows[0].astype(floats) + lower.astype(floats) + upper.astype(floats) + second.astype(floats)
-    )
+    got = [along_line(row, k) for k, row in enumerate(rows) if k > 0]
+    if pins:
+        got[-1] = after(got[-1], *pins)
+    total = rows[0].astype(floats)
+    for row in got:
+        total = total + row.astype(floats)
+    return total
 
 
 def further_on(array, back=False):
@@ -233,7 +230,7 @@
         out_specs=out_specs,
         scratch_shapes=list(scratch),
         input_output_aliases=aliases or {},
-        compiler_params=pltpu.CompilerParams(vmem_limit_bytes=56 * 1024 * 1024),
+        compiler_params=pltpu.CompilerParams(vmem_limit_bytes=58 * 1024 * 1024),
         cost_estimate=pl.CostEstimate(
             flops=int(flops * cost_scale), bytes_accessed=1024, transcendentals=0
         ),
@@ -254,65 +251,88 @@
     return jnp.where(core == 0, first, second), jnp.where(core == 0, second, first)
 
 
-def pack_shared(core, gate_up, down):
-    rows, both = gate_up.shape[1:]
-    units = both // 2
-    full = units + -units % 128
-
-    def kernel(core_ref, up_ref, down_ref, out):
-        keep = lax.broadcasted_iota(jnp.int32, (rows, full), 1) < units
-        fill = jnp.zeros((rows, full - units), floats)
-        for at in range(3):
-            if at < 2:
-                part = up_ref[at].astype(floats)
-                low = part[:, :full]
-                high = pltpu.roll(part, units, 1)[:, :full]
-            else:
-                low = jnp.concatenate([down_ref[:units, :].astype(floats).T, fill], axis=1)
-                high = jnp.concatenate([down_ref[units:, :].astype(floats).T, fill], axis=1)
-            low, high = jnp.where(keep, low, 0.0), jnp.where(keep, high, 0.0)
-            mine, other = ordered(core_ref[0], low, high)
-            columns = slice(at * full, (at + 1) * full)
-            out[0, :, columns] = mine.astype(halves)
-            out[1, :, columns] = other.astype(halves)
-
-    vmem = pl.BlockSpec(memory_space=pltpu.VMEM)
-    return kernel_call(
-        kernel,
-        jax.ShapeDtypeStruct((2, rows, 3 * full), halves),
-        [pl.BlockSpec(memory_space=pltpu.SMEM), vmem, vmem],
-        vmem,
-        0,
-    )(core, gate_up, down)
-
-
 def unpack_shared(core, sums, got, units):
     rows, wide = got.shape
     full = wide // 3
+    cut = 2 * full - units
 
     def kernel(core_ref, sums_ref, got_ref, up_out, down_out):
         low, high = ordered(core_ref[0], sums_ref[core_ref[0]], got_ref[...])
-        fill = jnp.zeros((rows, 2 * units - full), floats)
         for at in range(2):
-            columns = slice(at * full, (at + 1) * full)
-            first = jnp.concatenate([low[:, columns].astype(floats), fill], axis=1)
-            second = jnp.concatenate([high[:, columns].astype(floats), fill], axis=1)
-            up_out[at] = first + pltpu.roll(second, units, 1)
-        down_out[:units, :] = low[:, 2 * full :].astype(floats).T[:units]
-        down_out[units:, :] = high[:, 2 * full :].astype(floats).T[:units]
+            up_out[at, :, :full] = low[:, at * full : (at + 1) * full].astype(floats)
+            up_out[at, :, full:] = high[:, at * full + cut : (at + 1) * full].astype(floats)
+        down_out[:full, :] = low[:, 2 * full :].astype(floats).T
+        down_out[full:, :] = high[:, 2 * full :].astype(floats).T[cut:]
 
     vmem = pl.BlockSpec(memory_space=pltpu.VMEM)
     shape = jax.ShapeDtypeStruct
     return kernel_call(
         kernel,
-        (shape((2, rows, 2 * units), floats), shape((2 * units, rows), floats)),
+        (shape((2, rows, units), floats), shape((units, rows), floats)),
         [pl.BlockSpec(memory_space=pltpu.SMEM), vmem, vmem],
         (vmem, vmem),
         0,
     )(core, sums, got)
 
 
-def attention_forward(core, places, tokens, gain, blocks, bias, cosine, sine, seg_col, seg_row):
+def slot_table(place, routing, capacity):
+    blocks, lines, tokens = routing.shape
+    choices = lines // 6
+    pairs = blocks // 2
+
+    def kernel(place_ref, routing_ref, slot_row, gate_row, slot_col, gate_col, slots, gates):
+        expert = place_ref[2].astype(floats)
+        has = jnp.zeros((blocks, tokens), floats)
+        order = jnp.zeros((blocks, tokens), floats)
+        gate = jnp.zeros((blocks, tokens), floats)
+        for k in range(choices):
+            parts = [routing_ref[:, at * choices + k, :] for at in range(6)]
+            chosen = parts[0] == expert
+            has = jnp.where(chosen, 1.0, has)
+            order = jnp.where(chosen, parts[1] * 16.0 + parts[2], order)
+            gate = jnp.where(chosen, (parts[3] + parts[4]) + parts[5], gate)
+        none = has == 0.0
+        order = jnp.where(none, 1e9, order)
+        turned = order.T
+        for b in range(blocks):
+            earlier = turned[:, b : b + 1] < order[b : b + 1, :]
+            rank = jnp.sum(jnp.where(earlier, 1.0, 0.0), axis=0, keepdims=True)
+            kept = (rank < capacity) & (has[b : b + 1, :] > 0.0)
+            slots[b : b + 1, :] = jnp.where(kept, rank, -1.0)
+            gates[b : b + 1, :] = jnp.where(kept, gate[b : b + 1, :], 0.0)
+        for p in range(pairs):
+            span = lax.rem(place_ref[1] + p, pairs)
+            for at in range(2):
+                row = 2 * span + lax.rem(place_ref[0] + at, 2)
+                slot = slots[pl.ds(row, 1), :]
+                slot = jnp.where(slot < 0.0, slot, slot + at * capacity)
+                columns = slice(at * tokens, (at + 1) * tokens)
+                slot_row[p, :, columns] = slot.astype(jnp.int32)
+                gate_row[p, :, columns] = gates[pl.ds(row, 1), :]
+                lines = slice((2 * p + at) * tokens, (2 * p + at + 1) * tokens)
+                wide = jnp.broadcast_to(slot, (8, tokens)).T
+                slot_col[lines, :] = wide[:, :1].astype(jnp.int32)
+                wide = jnp.broadcast_to(gates[pl.ds(row, 1), :], (8, tokens)).T
+                gate_col[lines, :] = wide[:, :1]
+
+    vmem = pl.BlockSpec(memory_space=pltpu.VMEM)
+    shape = jax.ShapeDtypeStruct
+    return kernel_call(
+        kernel,
+        (
+            shape((pairs, 1, 2 * tokens), jnp.int32),
+            shape((pairs, 1, 2 * tokens), floats),
+            shape((blocks * tokens, 1), jnp.int32),
+            shape((blocks * tokens, 1), floats),
+        ),
+        [pl.BlockSpec(memory_space=pltpu.SMEM), vmem],
+        (vmem,) * 4,
+        0,
+        scratch=[pltpu.VMEM((blocks, tokens), floats), pltpu.VMEM((blocks, tokens), floats)],
+    )(place, routing)
+
+
+def attention_project(places, tokens, gain, blocks, bias, cosine, sine):
     length, width = tokens.shape
     count, rows_each, wide = blocks[0].shape
     piece = (wide - 128) // 4
@@ -323,10 +343,10 @@
     tile = 256
 
     def kernel(
-        core_ref, place_ref, tok, gain_ref, bias_ref, cos_ref, sin_ref, segc, segr, *refs
+        place_ref, tok, gain_ref, bias_ref, cos_ref, sin_ref, *refs
     ):
         pieces, refs = refs[:5], refs[5:]
-        w, wout, normed, query, key, value, lse, attended, mine, other, sems = refs
+        w, wout, normed, query, key, value, sems = refs
         copies = []
         for i, (first, last) in enumerate(spans):
             for g in range(first, last):
@@ -365,6 +385,35 @@
                 k = proj[:, piece + h * HEAD_DIM : piece + (h + 1) * HEAD_DIM]
                 key[rows, at] = (k * c + pltpu.roll(k, 64, 1) * s).astype(halves)
             value[rows, :] = proj[:, 2 * piece :].astype(halves)
+
+    vmem = pl.BlockSpec(memory_space=pltpu.VMEM)
+    shape = jax.ShapeDtypeStruct
+    return kernel_call(
+        kernel,
+        (
+            shape((width, 3 * piece), halves),
+            shape((piece, width), halves),
+            shape((length, width), halves),
+            shape((length, piece), halves),
+            shape((length, piece), halves),
+            shape((length, piece), halves),
+        ),
+        [pl.BlockSpec(memory_space=pltpu.SMEM)]
+        + [vmem] * 5
+        + [pl.BlockSpec(memory_space=pl.ANY)] * 5,
+        (vmem,) * 6,
+        0,
+        scratch=[pltpu.SemaphoreType.DMA((8 * count,))],
+    )(places, tokens, gain, bias, cosine, sine, *blocks)
+
+
+def attention_mix(core, query, key, value, seg_col, seg_row, out_rows):
+    length, piece = query.shape
+    width = out_rows.shape[1]
+    heads = piece // HEAD_DIM
+    tile = 256
+
+    def kernel(core_ref, query, key, value, segc, segr, wout, lse, attended, mine, other):
         for t in range(length // tile):
             rows = pl.ds(t * tile, tile)
             seen = (t + 1) * tile
@@ -391,24 +440,15 @@
     return kernel_call(
         kernel,
         (
-            shape((width, 3 * piece), halves),
-            shape((piece, width), halves),
-            shape((length, width), halves),
-            shape((length, piece), halves),
-            shape((length, piece), halves),
-            shape((length, piece), halves),
             shape((length, heads), floats),
             shape((length, piece), halves),
             shape((length // tile, tile // 2, width), halves),
             shape((length // tile, tile // 2, width), halves),
         ),
-        [pl.BlockSpec(memory_space=pltpu.SMEM)] * 2
-        + [vmem] * 7
-        + [pl.BlockSpec(memory_space=pl.ANY)] * 5,
-        (vmem,) * 10,
-        2 * length * width * 4 * piece + 2 * length * length * 2 * piece,
-        scratch=[pltpu.SemaphoreType.DMA((8 * count,))],
-    )(core, places, tokens, gain, bias, cosine, sine, seg_col, seg_row, *blocks)
+        [pl.BlockSpec(memory_space=pltpu.SMEM)] + [vmem] * 6,
+        (vmem,) * 4,
+        0,
+    )(core, query, key, value, seg_col, seg_row, out_rows)
 
 
 def attention_backward(
@@ -510,19 +550,28 @@
     pair = 2 * half
     count = pairs * capacity
     wide = 2 * ff
-
-    def kernel(
-        place_ref, slot_ref, gate_ref, x_mine, x_other, g_mine, g_other, up_hbm, *refs
-    ):
+    chunk = 256
+    chunks = wide // chunk
+
+    def kernel(place_ref, slot_ref, gate_ref, x_mine, x_other, g_mine, g_other, up_hbm, *refs):
         downs_hbm, refs = refs[: len(downs)], refs[len(downs) :]
-        slot_in, slot_grad, hidden, pre_grad, out, in_grad, w_up, w_down, pre, up_sems, down_sems = refs
-        chunk = 256
-        chunks = wide // chunk
+        out, in_grad, up_grad, down_grad, *refs = refs
+        x, g, w_up, w_down, pre, slot_in, slot_grad, hidden, pre_grad, stage, result, *sems = refs
+        row_sems, up_sems, down_sems, stage_sems, result_sems = sems
+        row_loads = []
+        for p in range(pairs):
+            for i, (source, target) in enumerate(((x_mine, x), (x_other, x), (g_mine, g), (g_other, g))):
+                rows = pl.ds(p * pair + (i % 2) * half, half)
+                row_loads.append(
+                    pltpu.make_async_copy(source.at[p], target.at[rows], row_sems.at[4 * p + i])
+                )
         loads = [
             pltpu.make_async_copy(
-                up_hbm.at[:, pl.ds(j * chunk, chunk)], w_up.at[:, pl.ds(j * chunk, chunk)], up_sems.at[j]
+                up_hbm.at[place_ref[len(downs)], pl.ds(j * chunk, chunk)],
+                w_up.at[pl.ds(j * chunk, chunk)],
+                up_sems.at[j],
             )
-            for j in range(chunks)
+            for j in range(width // chunk)
         ]
         down_loads = [
             pltpu.make_async_copy(
@@ -532,26 +581,28 @@
             )
             for i, block in enumerate(downs_hbm)
         ]
-        for load in loads + down_loads:
+        for load in row_loads + loads + down_loads:
             load.start()
         for p in range(pairs):
+            for load in row_loads[4 * p : 4 * p + 4]:
+                load.wait()
+            rows = pl.ds(p * pair, pair)
             slots = pl.ds(p * capacity, capacity)
             picks = lax.broadcasted_iota(jnp.int32, (capacity, pair), 0) == slot_ref[p]
             pick = jnp.where(picks, 1.0, 0.0).astype(halves)
             gates = jnp.sum(jnp.where(picks, gate_ref[p], 0.0), axis=-1, keepdims=True)
-            x = jnp.concatenate([x_mine[p], x_other[p]])
-            slot_in[slots, :] = kdot(pick, x, nn).astype(halves)
-            g = jnp.concatenate([g_mine[p], g_other[p]])
-            slot_grad[slots, :] = (kdot(pick, g, nn) * gates).astype(halves)
+            slot_in[slots, :] = kdot(pick, x[rows, :], nn).astype(halves)
+            slot_grad[slots, :] = (kdot(pick, g[rows, :], nn) * gates).astype(halves)
+        for load in loads:
+            load.wait()
         for j in range(chunks):
-            loads[j].wait()
             at = pl.ds(j * chunk, chunk)
             pre[:, at] = kdot(slot_in[...], w_up[:, at], nn)
         for load in down_loads:
             load.wait()
         start = 0
         while start < ff:
-            size = min(256, ff - start)
+            size = min(chunk, ff - start)
             at = slice(start, start + size)
             up_at = slice(ff + start, ff + start + size)
             grad = kdot(slot_grad[...], w_down[at, :], nt)
@@ -562,48 +613,121 @@
             pre_grad[:, at] = (grad * up_pre * sigma * (1.0 + gate_pre * (1.0 - sigma))).astype(halves)
             pre_grad[:, up_at] = (grad * act).astype(halves)
             start += size
-        for j in range(width // 512):
-            at = pl.ds(j * 512, 512)
-            out[:, at] = kdot(hidden[...], w_down[:, at], nn).astype(halves)
-            in_grad[:, at] = kdot(pre_grad[...], w_up[at, :], nt).astype(halves)
+        stores, results = [], []
+
+        def store(value, buffers, sems, target, first):
+            slot = len(stores) % 3
+            if len(stores) > 2:
+                stores[-3].wait()
+            rows, columns = value.shape
+            buffers[slot, :rows, :columns] = value.astype(halves)
+            stores.append(
+                pltpu.make_async_copy(
+                    buffers.at[slot, pl.ds(0, rows), pl.ds(0, columns)],
+                    target.at[pl.ds(first, rows)],
+                    sems.at[slot],
+                )
+            )
+            stores[-1].start()
+
+        for j in range(width // chunk):
+            at = pl.ds(j * chunk, chunk)
+            store(kdot(slot_in[:, at], pre_grad[...], tn), stage, stage_sems, up_grad, j * chunk)
+        start = 0
+        while start < ff:
+            size = min(chunk, ff - start)
+            at = slice(start, start + size)
+            store(kdot(hidden[:, at], slot_grad[...], tn), stage, stage_sems, down_grad, start)
+            start += size
+        for copy in stores[-3:]:
+            copy.wait()
+        for j in range(2):
+            rows = pl.ds(j * (count // 2), count // 2)
+            for i, target in enumerate((out, in_grad)):
+                if i == 0:
+                    value = kdot(hidden[rows, :], w_down[...], nn)
+                else:
+                    value = kdot(pre_grad[rows, :], w_up[...], nt)
+                result[2 * j + i] = value.astype(halves)
+                copy = pltpu.make_async_copy(
+                    result.at[2 * j + i], target.at[rows], result_sems.at[2 * j + i]
+                )
+                copy.start()
+                results.append(copy)
+        for copy in results:
+            copy.wait()
 
     vmem = pl.BlockSpec(memory_space=pltpu.VMEM)
     hbm = pl.BlockSpec(memory_space=pl.ANY)
     shape = jax.ShapeDtypeStruct
+    dma = pltpu.SemaphoreType.DMA
     return kernel_call(
         kernel,
         (
             shape((count, width), halves),
             shape((count, width), halves),
-            shape((count, ff), halves),
-            shape((count, wide), halves),
-            shape((count, width), halves),
-            shape((count, width), halves),
+            shape((width, wide), halves),
+            shape((ff, width), halves),
         ),
-        [pl.BlockSpec(memory_space=pltpu.SMEM)] + [vmem] * 6 + [hbm] * (1 + len(downs)),
-        (vmem,) * 6,
-        2 * count * width * ff * 6,
+        [pl.BlockSpec(memory_space=pltpu.SMEM)] + [vmem] * 2 + [hbm] * (5 + len(downs)),
+        (hbm,) * 4,
+        2 * count * width * ff * 9,
         scratch=[
-            pltpu.VMEM(up.shape, halves),
+            pltpu.VMEM((pairs * pair, width), halves),
+            pltpu.VMEM((pairs * pair, width), halves),
+            pltpu.VMEM((width, wide), halves),
             pltpu.VMEM((ff, width), halves),
             pltpu.VMEM((count, wide), floats),
-            pltpu.SemaphoreType.DMA((wide // 256,)),
-            pltpu.SemaphoreType.DMA((len(downs),)),
+            pltpu.VMEM((count, width), halves),
+            pltpu.VMEM((count, width), halves),
+            pltpu.VMEM((count, ff), halves),
+            pltpu.VMEM((count, wide), halves),
+            pltpu.VMEM((3, chunk, wide), halves),
+            pltpu.VMEM((4, count // 2, width), halves),
+            dma((4 * pairs,)),
+            dma((width // chunk,)),
+            dma((len(downs),)),
+            dma((3,)),
+            dma((4,)),
         ],
     )(places, slot_row, gate_row, *rows_in, *grads_in, up, *downs)
 
 
-def shared_pass(slot_col, gate_col, rows_in, grads_in, weights, vector, expert_out, expert_grad):
+def shared_pass(core, slot_col, gate_col, rows_in, grads_in, up, down, vector, expert_out, expert_grad):
     pairs, half, width = rows_in[0].shape
     tile = 2 * half
     length = pairs * tile
-    units = weights.shape[1] // 3
+    all_units = up.shape[2]
+    units = (all_units // 2 + 127) // 128 * 128
+    cut = 2 * units - all_units
     capacity = expert_out.shape[0] * tile // length
 
     def kernel(
-        slot_ref, gate_ref, x_mine, x_other, g_mine, g_other, up_ref, down_ref, vec_ref, eout_ref, egrad_ref,
-        ffn_mine, ffn_other, out_mine, out_other, pre_grad, hidden, shared_grad, logit,
+        core_ref, slot_ref, gate_ref, x_mine, x_other, g_mine, g_other, up_hbm, down_hbm, vec_ref, eout_ref,
+        egrad_ref, ffn_mine, ffn_other, out_mine, out_other, pre_grad, hidden, shared_grad, logit,
+        up_ref, down_ref, sems,
     ):
+        @pl.when(pl.program_id(0) == 0)
+        def _():
+            first = pl.multiple_of(core_ref[0] * (units - cut), 128)
+            copies = [
+                pltpu.make_async_copy(
+                    up_hbm.at[at, :, pl.ds(first, units)],
+                    up_ref.at[:, pl.ds(at * units, units)],
+                    sems.at[at],
+                )
+                for at in range(2)
+            ]
+            copies.append(
+                pltpu.make_async_copy(down_hbm.at[pl.ds(first, units)], down_ref, sems.at[2])
+            )
+            for copy in copies:
+                copy.start()
+            for copy in copies:
+                copy.wait()
+
+        unit = lax.broadcasted_iota(jnp.int32, (tile, units), 1)
+        ours = (unit >= cut) | (core_ref[0] == 0)
         x = jnp.concatenate([x_mine[0], x_other[0]])
         pre = kdot(x, up_ref[...], nn)
         gate_shared = jax.nn.sigmoid(
@@ -612,11 +736,11 @@
         grads = jnp.concatenate([g_mine[0], g_other[0]]).astype(floats)
         low_grad = (gate_shared * grads).astype(halves)
         shared_grad[...] = low_grad
-        grad = kdot(low_grad, down_ref[...], nn)
+        grad = jnp.where(ours, kdot(low_grad, down_ref[...], nt), 0.0)
         gate_pre, up_pre = pre[:, :units], pre[:, units:]
         sigma = jax.nn.sigmoid(gate_pre)
         act = gate_pre * sigma
-        hid = (act * up_pre).astype(halves)
+        hid = jnp.where(ours, act * up_pre, 0.0).astype(halves)
         hidden[...] = hid
         pre_grad[:, :units] = (grad * up_pre * sigma * (1.0 + gate_pre * (1.0 - sigma))).astype(halves)
         pre_grad[:, units:] = (grad * act).astype(halves)
@@ -624,7 +748,7 @@
         pick = jnp.where(picks, 1.0, 0.0).astype(halves)
         ffn = kdot(pre_grad[...], up_ref[...], nt) + kdot(pick, egrad_ref[...], nn)
         ffn_mine[0], ffn_other[0] = ffn[:half].astype(halves), ffn[half:].astype(halves)
-        shared_out = kdot(hid, down_ref[...], nt)
+        shared_out = kdot(hid, down_ref[...], nn)
         logit[...] = jnp.sum(grads * shared_out, axis=-1, keepdims=True)
         out = gate_shared * shared_out + gate_ref[...] * kdot(pick, eout_ref[...], nn)
         out_mine[0], out_other[0] = out[:half].astype(halves), out[half:].astype(halves)
@@ -645,63 +769,110 @@
             shape((length, 1), floats),
         ),
         [
+            pl.BlockSpec(memory_space=pltpu.SMEM),
             rows(1), rows(1), halfs, halfs, halfs, halfs,
-            pl.BlockSpec((width, 2 * units), lambda i: (0, 0)),
-            pl.BlockSpec((width, units), lambda i: (0, 2)),
+            pl.BlockSpec(memory_space=pl.ANY),
+            pl.BlockSpec(memory_space=pl.ANY),
             whole(vector), slots, slots,
         ],
         (halfs,) * 4 + (rows(2 * units), rows(units), rows(width), rows(1)),
         2 * length * width * units * 6,
         grid=(pairs,),
-    )(slot_col, gate_col, *rows_in, *grads_in, weights, weights, vector, expert_out, expert_grad)
-
-
-def weight_grad(lefts, right, into=None, at=0, wide=None):
-    rows = lefts[0].shape[-1]
-    depth, each = right.shape[0], lefts[0].shape[-2]
+        scratch=[
+            pltpu.VMEM((width, 2 * units), halves),
+            pltpu.VMEM((units, width), halves),
+            pltpu.SemaphoreType.DMA((3,)),
+        ],
+    )(core, slot_col, gate_col, *rows_in, *grads_in, up, down, vector, expert_out, expert_grad)
+
+
+def weight_grad(*pairs):
     tile = 256
-    first = at // tile
-    wide = right.shape[1] if wide is None else wide
+    lefts = [left if isinstance(left, tuple) else (left,) for left, _ in pairs]
+    rights = [right for _, right in pairs]
+    rows = lefts[0][0].shape[-1]
+    depth = rights[0].shape[0]
+    steps = [right.shape[1] // tile for right in rights]
+    starts = [sum(steps[:i]) for i in range(len(steps))]
 
     def kernel(*refs):
-        left_refs, right_ref = refs[: len(lefts)], refs[len(lefts)]
         out, turned = refs[-2:]
-
-        @pl.when(pl.program_id(0) == 0)
-        def _():
-            if len(lefts) == 1:
-                turned[...] = left_refs[0][...].T
-            else:
-                for block in range(depth // each):
-                    rows_low = left_refs[block % 2][block // 2]
-                    turned[:, block * each : (block + 1) * each] = rows_low.T
-
-        out[...] = kdot(turned[...], right_ref[...], nn).astype(halves)
-
-    more = [] if into is None else [into]
+        step = pl.program_id(0)
+        at = 0
+        for i, left in enumerate(lefts):
+            left_refs, right_ref = refs[at : at + len(left)], refs[at + len(left)]
+            at += len(left) + 1
+
+            @pl.when(step == starts[i])
+            def _():
+                if len(left_refs) == 1:
+                    turned[...] = left_refs[0][...].T
+                else:
+                    each = left_refs[0].shape[1]
+                    for block in range(depth // each):
+                        part = left_refs[block % 2][block // 2]
+                        turned[:, block * each : (block + 1) * each] = part.T
+
+            @pl.when((step >= starts[i]) & (step < starts[i] + steps[i]))
+            def _():
+                out[...] = kdot(turned[...], right_ref[...], nn).astype(halves)
+
+    specs, arrays = [], []
+    for left, right, start, count in zip(lefts, rights, starts, steps):
+        specs += [pl.BlockSpec(part.shape, lambda j, n=part.ndim: (0,) * n) for part in left]
+        specs.append(
+            pl.BlockSpec(
+                (depth, tile), lambda j, a=start, n=count: (0, jnp.clip(j - a, 0, n - 1))
+            )
+        )
+        arrays += [*left, right]
     return kernel_call(
         kernel,
-        jax.ShapeDtypeStruct((rows, wide), halves),
-        [pl.BlockSpec(left.shape, lambda j, n=left.ndim: (0,) * n) for left in lefts]
-        + [pl.BlockSpec((depth, tile), lambda j: (0, j))]
-        + [pl.BlockSpec(memory_space=pl.ANY)] * len(more),
-        pl.BlockSpec((rows, tile), lambda j: (0, first + j)),
-        2 * depth * rows * right.shape[1],
-        grid=(right.shape[1] // tile,),
+        jax.ShapeDtypeStruct((rows, sum(steps) * tile), halves),
+        specs,
+        pl.BlockSpec((rows, tile), lambda j: (0, j)),
+        2 * depth * rows * sum(steps) * tile,
+        grid=(sum(steps),),
         scratch=[pltpu.VMEM((rows, depth), halves)],
-        aliases={len(lefts) + 1: 0} if more else {},
-    )(*lefts, right, *more)
-
-
-def head_cut(qkv_weight, out_weight, vectors):
+    )(*arrays)
+
+
+def head_cut(qkv_weight, out_weight, vectors, ids, orders, gates):
     count = lax.axis_size(group)
     rows, wide = qkv_weight.shape
-    piece = wide // (3 * count)
-    cut = qkv_weight.reshape(rows, 3, count, piece).transpose(2, 0, 1, 3).reshape(count, rows, 3 * piece)
-    columns = jnp.concatenate([vector.reshape(-1, rows) for vector in vectors]).T
-    columns = jnp.pad(columns, ((0, 0), (0, 128 - columns.shape[1])))
-    columns = jnp.broadcast_to(columns[None], (count,) + columns.shape)
-    cut = jnp.concatenate([cut, columns], axis=-1)
+    width = wide // 3
+    piece = width // count
+    tokens, choices = ids.shape
+
+    def kernel(weight_ref, ids_ref, orders_ref, gates_ref, vectors_ref, out):
+        for g in range(count):
+            for at in range(3):
+                out[g, :, at * piece : (at + 1) * piece] = weight_ref[
+                    :, at * width + g * piece : at * width + (g + 1) * piece
+                ]
+        order = orders_ref[...]
+        gate = gates_ref[...]
+        first = gate.astype(halves).astype(floats)
+        second = (gate - first).astype(halves).astype(floats)
+        parts = (ids_ref[...], order // 16, order % 16, first, second, gate - first - second)
+        fill = jnp.zeros((tokens, 128 - choices * len(parts)), floats)
+        turned = jnp.concatenate([part.astype(floats) for part in parts] + [fill], axis=1).T
+        tile = jnp.concatenate(
+            [turned[: choices * len(parts)], vectors_ref[...], jnp.zeros((32, 128), floats)]
+        ).astype(halves)
+        for g in range(count):
+            out[g, :, 3 * piece :] = tile
+
+    stacked = jnp.concatenate([vector.reshape(-1, rows).astype(floats) for vector in vectors])
+    stacked = jnp.pad(stacked, ((0, 8 - stacked.shape[0]), (0, 128 - rows)))
+    vmem = pl.BlockSpec(memory_space=pltpu.VMEM)
+    cut = kernel_call(
+        kernel,
+        jax.ShapeDtypeStruct((count, rows, 3 * piece + 128), halves),
+        [vmem] * 5,
+        vmem,
+        0,
+    )(qkv_weight, ids, orders, gates, stacked)
     cut = lax.all_to_all(cut, group, split_axis=0, concat_axis=0, tiled=True)
     out = out_weight.reshape(rows, count, piece).transpose(1, 0, 2)
     return jnp.concatenate([cut, out], axis=-1)
@@ -717,9 +888,9 @@
     packed = place_blocks(
         blocks, places, (count, 4, rows, 128), [whole] * 3 + [low, high], (3 * piece, 128)
     )
-    columns = packed[..., :6].astype(floats)
-    vectors = [columns[..., at].reshape(-1) for at in range(3)]
-    vectors.append(columns[..., 3:].transpose(0, 1, 3, 2).reshape(-1))
+    lines = packed[..., 24:30, :rows].astype(floats)
+    vectors = [lines[..., at, :].reshape(-1) for at in range(3)]
+    vectors.append(lines[..., 3:, :].reshape(-1))
     return vectors
 
 
@@ -911,37 +1082,42 @@
     own_tokens = tokens[0]
     resid_in = own_tokens.astype(floats)
 
-    cut = head_cut(qkv_weight, out_weight, vectors)
-    all_tokens = lax.all_gather(after(own_tokens, cut), group, axis=0, tiled=True)
+    both = ("context", "dp")
+    shared_dn = lax.all_gather(shared_down, both, axis=1, tiled=True)
+    ed_first = entry(expert_down, core)
+    ed_second = other_core(entry(expert_down, 1 - core))
+    ed_first_x, ed_first_y = near_blocks(ed_first)
+    cut = after(
+        head_cut(
+            qkv_weight,
+            out_weight,
+            vectors,
+            expert_ids[0],
+            slot_order.reshape(tok_count, -1),
+            gate_weights[0],
+        ),
+        ed_first_x,
+        ed_first_y,
+        ed_second,
+    )
+    all_tokens = lax.all_gather(after(own_tokens, cut, shared_dn), group, axis=0, tiled=True)
     cut_x, cut_y = near_blocks(cut)
-    eu_both = both_cores(entry(expert_gate_up, core), entry(expert_gate_up, 1 - core))
     half = count // 2
-    cut_far = (
-        dp_step(after(cut_x[:half], eu_both), 2),
-        dp_step(after(cut_y[half:], eu_both), 1),
-    )
+    cut_far = dp_step(cut_x[:half], 2), dp_step(cut_y[half:], 1)
     blocks = [cut, cut_x, cut_y, *cut_far]
     places = [place, place ^ 1, place ^ 2, place ^ 3, place ^ 3]
     gain_attn, gain_ffn, gate_vector, bias = head_vectors(blocks, places)
-    expert_up = gather_rows(eu_both)
-    grads_mine = line_gather(after(cotangent[0], cut))
-    routes = routing_of(expert_ids, slot_order, gate_weights, count, cut)
-    rank, kept, gate = slots_of(routes, index, capacity)
-    slot = further_on(jnp.where(kept, rank, -1).reshape(-1, 2, tok_count))
-    slot = slot + jnp.where(slot < 0, 0, jnp.arange(2, dtype=jnp.int32)[:, None] * capacity)
-    gate = further_on(gate.reshape(-1, 2, tok_count))
-    all_tokens = after(all_tokens, slot, gate)
-
+    grads_mine = line_blocks(after(cotangent[0], all_tokens))
+    expert_up = lax.all_gather(after(expert_gate_up, cut_x, cut_y), both, axis=1, tiled=True)
     piece = width // count
-    positions = jnp.arange(length, dtype=jnp.int32)
-    cosine, sine = rope_tables(positions, HEAD_DIM // 2)
-    cosine = jnp.concatenate([cosine, cosine], axis=-1)
-    sine = jnp.concatenate([-sine, sine], axis=-1)
+    inverse = rope_base ** (-2.0 * np.arange(HEAD_DIM // 2) / HEAD_DIM)
+    angle = np.arange(length)[:, None] * inverse[None, :]
+    cosine = np.concatenate([np.cos(angle), np.cos(angle)], axis=-1).astype(np.float32)
+    sine = np.concatenate([-np.sin(angle), np.sin(angle)], axis=-1).astype(np.float32)
     seg_row = segments.astype(jnp.int32)
     seg_col = seg_row.reshape(length, 1)
     own_bias = lax.dynamic_index_in_dim(bias.reshape(3, count, piece), index, 1, keepdims=False)
-    weight, out_rows, normed, query, key, value, lse, attended, mine, other = attention_forward(
-        core_at,
+    weight, out_rows, normed, query, key, value = attention_project(
         jnp.stack(places).astype(jnp.int32),
         all_tokens,
         gain_attn.reshape(1, width),
@@ -949,21 +1125,23 @@
         own_bias.reshape(1, 3 * piece),
         cosine,
         sine,
-        seg_col,
-        seg_row,
-    )
-
-    ed_first = after(entry(expert_down, core), *cut_far)
-    ed_second = after(other_core(entry(expert_down, 1 - core)), *cut_far)
-    ed_first_x, ed_first_y = near_blocks(ed_first)
-    ed_second_x, ed_second_y = near_blocks(ed_second)
-    other = other_core(after(other, grads_mine))
-    mixed = line_sum(mine, other, ed_first_x, ed_first_y, ed_second_x, ed_second_y)
-    ed_first_far, ed_second_far = dp_step(ed_first_x, 2), dp_step(ed_second_y, 1)
-    units = shared_down.shape[0] // 2
-    sh_pack = pack_shared(core_at, shared_gate_up, shared_down)
-    sh_both = both_cores(sh_pack[0], sh_pack[1])
-    shared_weights = gather_rows(after(sh_both, attended))
+    )
+    ed_first_far = dp_step(after(ed_first_x, *cut_far), 2)
+    ed_second_x, ed_second_y = near_blocks(after(ed_second, *cut_far))
+    lse, attended, mine, other = attention_mix(
+        core_at, after(query, *grads_mine, ed_first_far, ed_second_x, ed_second_y), key, value, seg_col, seg_row, out_rows
+    )
+    grads_mine = jnp.stack(grads_mine)
+
+    slot_row, gate_row, slot_col, gate_col = slot_table(
+        jnp.stack([after(core, query), lax.axis_index("expert"), index]).astype(jnp.int32),
+        cut[:, :24, 3 * piece : 3 * piece + 128].astype(floats),
+        capacity,
+    )
+    other = other_core(after(other, slot_row, slot_col, gate_row, gate_col))
+    ed_second_far = dp_step(ed_second_y, 1)
+    mixed = line_sum(mine, other)
+    shared_up = lax.all_gather(after(shared_gate_up, attended), both, axis=1, tiled=True)
 
     resid_mid = resid_in + mixed
     stat_ffn = lax.rsqrt(jnp.mean(resid_mid * resid_mid, axis=-1, keepdims=True) + eps_norm)
@@ -971,40 +1149,37 @@
     normed_ffn = (unit_ffn * gain_ffn).astype(halves)
     grad_out = cotangent[0].astype(floats)
     all_grads = (grads_mine, other_core(after(grads_mine, mine)))
-    normed_mine = line_gather(normed_ffn, ed_first_far, ed_second_far, all_grads[1])
+    normed_mine = line_gather(normed_ffn, ed_second_far, all_grads[1])
     all_normed = (normed_mine, other_core(normed_mine))
 
-    slot_in, slot_grad, hidden, pre_grad, expert_out, expert_grad = expert_pass(
-        slot.reshape(count // 2, 1, 2 * tok_count),
-        gate.reshape(count // 2, 1, 2 * tok_count),
+    expert_out, expert_grad, eu_term, ed_term = expert_pass(
+        slot_row,
+        gate_row,
         all_normed,
         all_grads,
         expert_up,
         [ed_first, ed_first_x, ed_first_y, ed_first_far]
         + [ed_second, ed_second_x, ed_second_y, ed_second_far],
         jnp.stack(
-            [4 * which + (place ^ step) for which in (core, 1 - core) for step in range(4)]
+            [4 * which + (place ^ step) for which in (core, 1 - core) for step in range(4)] + [core]
         ).astype(jnp.int32),
         2 * capacity,
     )
-    eu_term = weight_grad([slot_in], pre_grad)
-    ed_term = weight_grad([hidden], slot_grad)
     ffn_mine, ffn_other, out_mine, out_other, sh_pre_grad, sh_hidden, sh_grad, logit_part = shared_pass(
-        slot.reshape(length, 1),
-        gate.reshape(length, 1),
+        core_at,
+        slot_col,
+        gate_col,
         (after(all_normed[0], eu_term, ed_term), all_normed[1]),
         all_grads,
-        shared_weights,
+        shared_up,
+        shared_dn,
         gate_vector.reshape(1, width),
         expert_out,
         expert_grad,
     )
-    wide = shared_weights.shape[1]
-    sh_term = weight_grad(all_normed, sh_pre_grad, None, 0, wide)
-    sh_term = weight_grad([sh_grad], sh_hidden, sh_term, sh_pre_grad.shape[1], wide)
-    eu_sum, sh_sum = sum_weight(eu_term), sum_weight(sh_term)
-
     ffn_other = other_core(ffn_other)
+    eu_sum = sum_weight(eu_term)
+
     ffn_grad = line_sum(ffn_mine, ffn_other)
     logit_part = further_on(logit_part.reshape(-1, 2, tok_count), True)
     logit_sums = lax.all_to_all(
@@ -1022,25 +1197,38 @@
     gain_ffn_part = jnp.sum(ffn_grad * unit_ffn, axis=0)
     gate_vector_part = jnp.sum(logit_grad * normed_ffn.astype(floats), axis=0)
     mid_grad = norm_backward(grad_out, ffn_grad, gain_ffn, unit_ffn, stat_ffn)
-    mid_low = after(mid_grad.astype(halves), sh_term)
+    mid_low = mid_grad.astype(halves)
+    sh_term = weight_grad((all_normed, after(sh_pre_grad, mid_low)), (sh_grad, sh_hidden))
+    sh_sum = sum_weight(sh_term)
 
     out_got = other_core(out_other)
-    mid_mine = line_gather(mid_low, eu_sum, out_got)
+    mid_mine = line_gather(mid_low, eu_sum, out_got, sh_term)
     mid_other = other_core(mid_mine)
     proj_grad, mine, other, gain_attn_part, bias_part, out_part = attention_backward(
         core_at, mid_mine, mid_other, all_tokens, weight, cosine, sine, seg_col, seg_row, out_rows,
         query, key, value, lse, attended,
     )
-    layer_sum = line_sum(out_mine, after(out_got, mid_mine))
-    other = other_core(after(other, layer_sum))
-    attn_in_grad = line_sum(mine, other)
+    other = other_core(other)
     rows = other
-    weight_part = weight_grad([normed], proj_grad).reshape(count, -1, 3 * piece)
+    small = small_sums(
+        [
+            gain_attn_part,
+            gain_ffn_part,
+            gate_vector_part,
+            lax.dynamic_update_slice(
+                jnp.zeros((3, count, piece), floats), bias_part.reshape(3, 1, piece), (0, index, 0)
+            ),
+        ],
+        lengths,
+        rows,
+    )
+    attn_in_grad = line_sum(mine, other, *small)
+    weight_part = weight_grad((normed, after(proj_grad, other))).reshape(count, -1, 3 * piece)
     out_part = out_part.reshape(-1, count, piece).transpose(1, 0, 2)
+    ed_sum = sum_weight(after(ed_term, weight_part))
     total = lax.psum_scatter(
         jnp.concatenate([weight_part, out_part], axis=-1), "dp", scatter_dimension=1, tiled=True
     )
-    ed_sum = sum_weight(after(ed_term, sh_term))
     qkv_total = lax.all_to_all(
         after(total[..., : 3 * piece], attn_in_grad), group, split_axis=0, concat_axis=0, tiled=True
     )
@@ -1052,20 +1240,18 @@
         .astype(floats)
     )
     out_weight_out = total[..., 3 * piece :].transpose(1, 0, 2).reshape(each, width).astype(floats)
-    bias_part = lax.dynamic_update_slice(
-        jnp.zeros((3, count, piece), floats), bias_part.reshape(3, 1, piece), (0, index, 0)
-    ).reshape(-1)
-    layer_sum = resid_mid + layer_sum
+    layer_sum = resid_mid + line_sum(out_mine, after(out_got, attn_in_grad))
     stat_attn = lax.rsqrt(jnp.mean(resid_in * resid_in, axis=-1, keepdims=True) + eps_norm)
     unit_attn = resid_in * stat_attn
     input_grad = norm_backward(mid_grad, attn_in_grad, gain_attn, unit_attn, stat_attn)
 
-    eu_sum, sh_sum, ed_sum = (after(total, rows) for total in (eu_sum, sh_sum, ed_sum))
+    eu_sum, ed_sum = after(eu_sum, rows), after(ed_sum, attn_in_grad)
+    sh_sum = after(sh_sum, attn_in_grad)
     got = other_core(entry(sh_sum, 1 - core))
-    shared_up_out, shared_down_out = unpack_shared(core_at, sh_sum, got, units)
-    gain_attn_out, gain_ffn_out, gate_vector_out, bias_out = small_sums(
-        [gain_attn_part, gain_ffn_part, gate_vector_part, bias_part], lengths, attn_in_grad
-    )
+    shared_up_out, shared_down_out = unpack_shared(
+        core_at, sh_sum, got, shared_gate_up.shape[2]
+    )
+    gain_attn_out, gain_ffn_out, gate_vector_out, bias_out = small
     return (
         layer_sum.astype(halves)[None],
         input_grad[None],

time: 754 us -> 720 us (0.955)
  blocking collectives: 0 us -> 45.6 us
  other arithmetic: 77.5 us -> 55.9 us
  waiting for transfers between devices: 332 us -> 317 us
  starting transfers between devices: 94 us -> 79.7 us
  local copies, waits for them, and re-layouts: 48.4 us -> 35.9 us
  Pallas kernels: 177 us -> 167 us
    all_to_all x0 -> x1, blocking collectives: none -> 45.6 us  [shards_by_heads(): lax.all_to_all(after(logit_part.reshape(count, 1, tok_count), ffn_other),...]
    all_to_all x2 -> x0, waiting for transfers between devices: 26.6 us -> none  [the longest x1 22 us: shards_by_heads(): lax.all_to_all(after(logit_part.reshape(count, 1, tok_count), ffn_other),...]
    pallas_call x8 -> x7, Pallas kernels: 83.3 us -> 58.8 us  [the longest x2 28.2 us: weight_grad(): kernel_call(kernel, jax.ShapeDtypeStruct((rows, sum(steps) * tile), halve...]
    all_to_all x1, waiting for transfers between devices: 4.69 us -> 28.4 us  [small_sums(): lax.all_to_all(packed.reshape(devices, -1, 128), every, split_axis=0, con...]
    ppermute x28 -> x21, waiting for transfers between devices: 182 us -> 164 us  [along_line(): lax.ppermute(value, 'expert', [(i, (i + step) % count) for i in range(cou...]
    ppermute x10, waiting for transfers between devices: 54.3 us -> 68.5 us  [dp_step(): return lax.ppermute(value, 'dp', [(i, i ^ step) for i in range(count)])]
    pallas_call x1, Pallas kernels: 37.5 us -> 51 us  [expert_pass(): kernel_call(kernel, (shape((count, width), halves), shape((count, width),...]
    all_gather x3 -> x4, waiting for transfers between devices: 0.01 us -> 10.8 us  [the longest x1 10.8 us: shards_by_heads(): shared_dn = lax.all_gather(shared_down, both, axis=1, tiled=True)]
  transfers between devices with their start and end apart: 63 -> 53, of which waited for: 34 -> 27; matrix products, arithmetic and copies ran while one was open for 15% -> 11% of each run, Pallas kernels for 24% -> 23%
where the time goes in v4:
time: 720 us; the launch traced here: 716 us
  waiting for transfers between devices  317 us (44%)
  Pallas kernels  167 us (23%)
  starting transfers between devices  79.7 us (11%)
  other arithmetic  55.9 us (8%)
  blocking collectives  45.6 us (6%)
  local copies, waits for them, and re-layouts  35.9 us (5%)
  between operations  14.9 us (2%)
    ppermute x21, waiting for transfers between devices, along_line(): lax.ppermute(value, 'expert', [(i, (i + step) % count) for i in range(cou...  164 us
    ppermute x10, waiting for transfers between devices, dp_step(): return lax.ppermute(value, 'dp', [(i, i ^ step) for i in range(count)])  68.5 us
    ppermute x21, starting transfers between devices, along_line(): lax.ppermute(value, 'expert', [(i, (i + step) % count) for i in range(cou...  52.8 us
    pallas_call x1, Pallas kernels, expert_pass(): kernel_call(kernel, (shape((count, width), halves), shape((count, width),...  51 us
    all_to_all x1, blocking collectives, shards_by_heads(): lax.all_to_all(after(logit_part.reshape(count, 1, tok_count), ffn_other),...  45.6 us
    pallas_call x1, Pallas kernels, shared_pass(): kernel_call(kernel, (half_shape,) * 4 + (shape((length, 2 * units), halve...  34.3 us
    all_to_all x1, waiting for transfers between devices, small_sums(): lax.all_to_all(packed.reshape(devices, -1, 128), every, split_axis=0, con...  28.4 us
    pallas_call x2, Pallas kernels, weight_grad(): kernel_call(kernel, jax.ShapeDtypeStruct((rows, sum(steps) * tile), halve...  28.2 us
  transfers between devices with their start and end apart: 53, of which 27 were waited for; matrix products, arithmetic and copies ran while one was open for 11% of the time, Pallas kernels for 23%

profile of v4, /device:TPU:0, one launch (start us, length us, event | category | flops | bytes accessed | tf_op | source)
XLA Modules:
  0.0 716.0 jit_solution(18091151956285561880)
XLA Ops:
  17.7 6.5 all-to-all-start
  29.6 18.4 %all-to-all-done = bf16[8,64,896]{2,1,0:T(8,128)(2,1)S(1)} async-done(((bf16[8,64,896]{2,1,0:T(8,128)(2,1)}), bf16[8,64,896]{2,1,0:T(8,128)(2,1)S(1)}, u32[]{:S(2)}, u32[]{:S(2)}) %all-to-all-start) | async-done | bytes 917536 | tf_op jit(solution)/shard_map/all_to_all | solution.py:876
  48.1 4.7 collective-permute-done.refs_1_
  54.0 10.8 %all-gather.5.cloned.1.call-done.down_hbm = bf16[1408,2048]{1,0:T(8,128)(2,1)} async-done(((bf16[1408,256]{1,0:T(8,128)(2,1)}), bf16[1408,2048]{1,0:T(8,128)(2,1)}) %all-gather.5.cloned.1.call-update) | async-done | bytes 5767184 | tf_op jit(solution)/shard_map/all_gather | solution.py:1086
  67.0 26.1 %collective-permute-done.3.refs_1_ = bf16[8,64,1152]{2,1,0:T(8,128)(2,1)S(1)} collective-permute-done((bf16[8,64,1152]{2,1,0:T(8,128)(2,1)S(1)}, bf16[8,64,1152]{2,1,0:T(8,128)(2,1)S(1)}, u32[]{:S(2)}, u32[]{:S(2)}) %collective-permute-start.3) | collective-permute-done | bytes 1179680 | tf_op jit(solution)/shard_map/ppermute | solution.py:77
  96.5 12.5 %collective-permute-done.5.refs_3_ = bf16[4,64,1152]{2,1,0:T(8,128)(2,1)S(1)} collective-permute-done((bf16[4,64,1152]{2,1,0:T(8,128)(2,1)S(1)}, bf16[4,64,1152]{2,1,0:T(8,128)(2,1)S(1)}, u32[]{:S(2)}, u32[]{:S(2)}) %collective-permute-start.5) | collective-permute-done | bytes 589856 | tf_op jit(solution)/shard_map/ppermute | solution.py:77
  122.6 9.8 %collective-permute-done.10.refs_3_ = bf16[176,2048]{1,0:T(8,128)(2,1)} collective-permute-done((bf16[176,2048]{1,0:T(8,128)(2,1)}, bf16[176,2048]{1,0:T(8,128)(2,1)}, u32[]{:S(2)}, u32[]{:S(2)}) %collective-permute-start.10) | collective-permute-done | bytes 720928 | tf_op jit(solution)/shard_map/ppermute | solution.py:77
  136.5 11.2 %shard_map.267 = (bf16[2048,768]{1,0:T(8,128)(2,1)}, bf16[256,2048]{1,0:T(8,128)(2,1)}, bf16[1024,2048]{1,0:T(8,128)(2,1)}, bf16[1024,256]{1,0:T(8,128)(2,1)}, b...) custom-call(s32[5]{0:T(128)} %copy-done.8, bf16[1024,2048]{1,0:T(8,128)(2,1)} %all-gather.7.cloned.1.call-done.tok, ...), custom_call_target="tpu_custom_call" | custom-call | bytes 1024 | tf_op jit(solution)/shard_map/pallas_call | solution.py:391
  147.7 13.0 %collective-permute-done.12.refs_6_ = bf16[176,2048]{1,0:T(8,128)(2,1)} collective-permute-done((bf16[176,2048]{1,0:T(8,128)(2,1)}, bf16[176,2048]{1,0:T(8,128)(2,1)}, u32[]{:S(2)}, u32[]{:S(2)}) %collective-permute-start.12) | collective-permute-done | bytes 720928 | tf_op jit(solution)/shard_map/ppermute | solution.py:77
  160.7 4.6 collective-permute-done.8
  165.3 9.9 %shard_map.268 = (f32[1024,2]{1,0:T(8,128)}, bf16[1024,256]{1,0:T(8,128)(2,1)}, bf16[4,128,2048]{2,1,0:T(8,128)(2,1)}, bf16[4,128,2048]{2,1,0:T(8,128)(2,1)}) custom-call(s32[2]{0:T(128)} %pad_add_fusion.core_ref, bf16[1024,256]{1,0:T(8,128)(2,1)} %get-tuple-element.77.query.q_ref, bf16[1024,256]{1,0:T(8,128)(2,1)} %get-tuple-element.78.key.k_ref, ...), custom_call_target="tpu_custom_call" | custom-call | bytes 1024 | tf_op jit(solution)/shard_map/pallas_call | solution.py:440
  182.5 6.8 collective-permute-done.13
  197.1 8.2 %collective-permute-done.16 = bf16[128,2048]{1,0:T(8,128)(2,1)S(1)} collective-permute-done((bf16[128,2048]{1,0:T(8,128)(2,1)}, bf16[128,2048]{1,0:T(8,128)(2,1)S(1)}, u32[]{:S(2)}, u32[]{:S(2)}) %collective-permute-start.16) | collective-permute-done | bytes 524320 | tf_op jit(solution)/shard_map/ppermute | solution.py:181
  205.3 34.2 %collective-permute-done.15 = bf16[128,2048]{1,0:T(8,128)(2,1)S(1)} collective-permute-done((bf16[128,2048]{1,0:T(8,128)(2,1)}, bf16[128,2048]{1,0:T(8,128)(2,1)S(1)}, u32[]{:S(2)}, u32[]{:S(2)}) %collective-permute-start.15) | collective-permute-done | bytes 524320 | tf_op jit(solution)/shard_map/ppermute | solution.py:181
  247.3 12.5 %collective-permute-done.19 = bf16[128,2048]{1,0:T(8,128)(2,1)S(1)} collective-permute-done((bf16[128,2048]{1,0:T(8,128)(2,1)S(1)}, bf16[128,2048]{1,0:T(8,128)(2,1)S(1)}, u32[]{:S(2)}, u32[]{:S(2)}) %collective-permute-start.19) | collective-permute-done | bytes 524320 | tf_op jit(solution)/shard_map/ppermute | solution.py:181
  259.8 21.2 %collective-permute-done.18 = bf16[128,2048]{1,0:T(8,128)(2,1)S(1)} collective-permute-done((bf16[128,2048]{1,0:T(8,128)(2,1)S(1)}, bf16[128,2048]{1,0:T(8,128)(2,1)S(1)}, u32[]{:S(2)}, u32[]{:S(2)}) %collective-permute-start.18) | collective-permute-done | bytes 524320 | tf_op jit(solution)/shard_map/ppermute | solution.py:181
  285.7 51.0 %shard_map.270 = (bf16[576,2048]{1,0:T(8,128)(2,1)}, bf16[576,2048]{1,0:T(8,128)(2,1)}, bf16[2048,2816]{1,0:T(8,128)(2,1)}, bf16[1408,2048]{1,0:T(8,128)(2,1)}) custom-call(s32[9]{0:T(128)} %stack.161.place_ref, s32[4,1,256]{2,1,0:T(1,128)} %get-tuple-element.84.slot_ref, f32[4,1,256]{2,1,0:T(1,128)} %get-tuple-element.86.gate_ref, ...), custom_call_target="tpu_custom_call" | custom-call | bytes 1024 | tf_op jit(solution)/shard_map/pallas_call | solution.py:664
  337.7 34.3 %shard_map.271 = (bf16[4,128,2048]{2,1,0:T(8,128)(2,1)}, bf16[4,128,2048]{2,1,0:T(8,128)(2,1)}, bf16[4,128,2048]{2,1,0:T(8,128)(2,1)}, bf16[4,128,2048]{2,1,0:T(...) custom-call(s32[2]{0:T(128)} %pad_add_fusion.core_ref, ...), custom_call_target="tpu_custom_call" | custom-call | bytes 1024 | tf_op jit(solution)/shard_map/pallas_call | solution.py:762
  381.2 12.7 %collective-permute-start.27 = (bf16[128,2048]{1,0:T(8,128)(2,1)}, bf16[128,2048]{1,0:T(8,128)(2,1)S(1)}, u32[]{:S(2)}, u32[]{:S(2)}) collective-permute-start(bf16[128,2048]{1,0:T(8,128)(2,1)} %get-tuple-element.151), channel_id=1, source_target_pairs={{0,24},{8,0},{16,8},{24,16},{1,25},{9,1},{17,9},{25,17},{2,26},{10... | collective-permute-start | bytes 1572872 | tf_op jit(solution)/shard_map/ppermute | solution.py:181
  395.1 45.6 %all_to_all.20 = f32[8,1,128]{2,1,0:T(1,128)S(1)} all-to-all(f32[8,1,128]{2,1,0:T(1,128)S(1)} %bitcast.200), channel_id=1, replica_groups=mesh['expert'=4,'context'=2,'dp'=4] {'expert','context'}, dimensions={0} | all-to-all | bytes 8192 | tf_op jit(solution)/shard_map/all_to_all | solution.py:1185
  445.4 19.6 %shard_map.272 = bf16[2048,2304]{1,0:T(8,128)(2,1)} custom-call(bf16[4,128,2048]{2,1,0:T(8,128)(2,1)} %copy-done.9, bf16[4,128,2048]{2,1,0:T(8,128)(2,1)} %collective-permute-done.22.x_other.refs_1_, bf16[1024,1536]{1,0:T(8,128)(2,1)} %get-tuple-element.106.refs_2_, bf16[1024,2048]{1,0:T(8,128)(2,1)} %get-tuple-element.107.refs_3_, ...), custom_call_target="tpu_custom_call" | custom-call | bytes 1024 | tf_op jit(solution)/shard_map/pallas_call | solution.py:829
  470.0 12.0 %collective-permute-done.30 = bf16[128,2048]{1,0:T(8,128)(2,1)} collective-permute-done((bf16[128,2048]{1,0:T(8,128)(2,1)S(1)}, bf16[128,2048]{1,0:T(8,128)(2,1)}, u32[]{:S(2)}, u32[]{:S(2)}) %collective-permute-start.30) | collective-permute-done | bytes 524320 | tf_op jit(solution)/shard_map/ppermute | solution.py:181
  482.0 22.0 %collective-permute-done.29 = bf16[128,2048]{1,0:T(8,128)(2,1)} collective-permute-done((bf16[128,2048]{1,0:T(8,128)(2,1)S(1)}, bf16[128,2048]{1,0:T(8,128)(2,1)}, u32[]{:S(2)}, u32[]{:S(2)}) %collective-permute-start.29) | collective-permute-done | bytes 524320 | tf_op jit(solution)/shard_map/ppermute | solution.py:181
  511.2 21.6 %shard_map.273 = (bf16[1024,768]{1,0:T(8,128)(2,1)}, bf16[4,128,2048]{2,1,0:T(8,128)(2,1)}, bf16[4,128,2048]{2,1,0:T(8,128)(2,1)}, f32[1,2048]{1,0:T(1,128)}, f3...) custom-call(s32[2]{0:T(128)} %pad_add_fusion.core_ref, bf16[4,128,2048]{2,1,0:T(8,128)(2,1)} %copy-done.13, ...), custom_call_target="tpu_custom_call" | custom-call | bytes 1024 | tf_op jit(solution)/shard_map/pallas_call | solution.py:522
  537.3 8.6 %shard_map.274 = bf16[2048,768]{1,0:T(8,128)(2,1)} custom-call(bf16[1024,2048]{1,0:T(8,128)(2,1)} %get-tuple-element.119.refs_0_, bf16[1024,768]{1,0:T(8,128)(2,1)} %get-tuple-element.121.refs_1_), custom_call_target="tpu_custom_call" | custom-call | bytes 1024 | tf_op jit(solution)/shard_map/pallas_call | solution.py:829
  546.0 4.8 pad_maximum_fusion
  556.6 11.6 %collective-permute-start.35 = (bf16[128,2048]{1,0:T(8,128)(2,1)}, bf16[128,2048]{1,0:T(8,128)(2,1)}, u32[]{:S(2)}, u32[]{:S(2)}) collective-permute-start(bf16[128,2048]{1,0:T(8,128)(2,1)} %get-tuple-element.148), channel_id=1, source_target_pairs={{0,24},{8,0},{16,8},{24,16},{1,25},{9,1},{17,9},{25,17},{2,26},{10... | collective-permute-start | bytes 1572872 | tf_op jit(solution)/shard_map/ppermute | solution.py:181
  579.0 28.4 %all-to-all-done.2 = f32[32,3,128]{2,1,0:T(4,128)S(1)} async-done(((f32[32,3,128]{2,1,0:T(4,128)}), f32[32,3,128]{2,1,0:T(4,128)S(1)}, u32[]{:S(2)}, u32[]{:S(2)}) %all-to-all-start.2) | async-done | bytes 49184 | tf_op jit(solution)/shard_map/all_to_all | solution.py:1027
  608.6 7.3 %collective-permute-done.34 = bf16[128,2048]{1,0:T(8,128)(2,1)} collective-permute-done((bf16[128,2048]{1,0:T(8,128)(2,1)}, bf16[128,2048]{1,0:T(8,128)(2,1)}, u32[]{:S(2)}, u32[]{:S(2)}) %collective-permute-start.34) | collective-permute-done | bytes 524320 | tf_op jit(solution)/shard_map/ppermute | solution.py:181
  629.0 6.2 collective-permute-done.38
  635.2 35.4 %collective-permute-done.37 = bf16[128,2048]{1,0:T(8,128)(2,1)} collective-permute-done((bf16[128,2048]{1,0:T(8,128)(2,1)}, bf16[128,2048]{1,0:T(8,128)(2,1)}, u32[]{:S(2)}, u32[]{:S(2)}) %collective-permute-start.37) | collective-permute-done | bytes 524320 | tf_op jit(solution)/shard_map/ppermute | solution.py:181
  697.4 4.5 all-to-all-done.3
  (249 shorter events, 165.0 us)
Async XLA Ops:
  7.2 57.7 %all-gather.5.cloned.1.call-start = ((), (), s32[]{:S(2)}) async-start(), calls=%async_computation.8 | async-start | bytes 6488064 | tf_op jit(solution)/shard_map/all_gather | solution.py:1086
  24.2 94.9 %all-gather.7.cloned.1.call-start = ((), (), s32[]{:S(2)}) async-start(), calls=%async_computation.9 | async-start | bytes 4718592 | tf_op jit(solution)/shard_map/all_gather | solution.py:1103
  64.9 220.8 %all-gather.9.cloned.1.call-start = ((), (), s32[]{:S(2)}) async-start(), calls=%async_computation.10 | async-start | bytes 25952256 | tf_op jit(solution)/shard_map/all_gather | solution.py:1111
  94.4 243.3 %all-gather.11.cloned.1.call-start = ((), (), s32[]{:S(2)}) async-start(), calls=%async_computation.11 | async-start | bytes 12976128 | tf_op jit(solution)/shard_map/all_gather | solution.py:1144
  111.7 36.0 %collective-permute-start.11 = (bf16[176,2048]{1,0:T(8,128)(2,1)}, bf16[176,2048]{1,0:T(8,128)(2,1)}, u32[]{:S(2)}, u32[]{:S(2)}) collective-permute-start(bf16[176,2048]{1,0:T(8,128)(2,1)} %collective-permute-done.2.refs_4_), channel_id=1, source_target_pairs={{0,1},{1,0},{2,3},{3,2},{4,5},{5,4},{6,7},{7,6},{8,9},{9,8},{10,11... | collective-permute-start | bytes 2162696 | tf_op jit(solution)/shard_map/ppermute | solution.py:77
  112.5 48.2 %collective-permute-start.12 = (bf16[176,2048]{1,0:T(8,128)(2,1)}, bf16[176,2048]{1,0:T(8,128)(2,1)}, u32[]{:S(2)}, u32[]{:S(2)}) collective-permute-start(bf16[176,2048]{1,0:T(8,128)(2,1)} %collective-permute-done.2.refs_4_), channel_id=1, source_target_pairs={{0,2},{1,3},{2,0},{3,1},{4,6},{5,7},{6,4},{7,5},{8,10},{9,11},{10,... | collective-permute-start | bytes 2162696 | tf_op jit(solution)/shard_map/ppermute | solution.py:77
  119.1 41.6 %collective-permute-start.7 = (bf16[128,2048]{1,0:T(8,128)(2,1)}, bf16[128,2048]{1,0:T(8,128)(2,1)S(1)}, u32[]{:S(2)}, u32[]{:S(2)}) collective-permute-start(bf16[128,2048]{1,0:T(8,128)(2,1)} %bitcast.174), channel_id=1, source_target_pairs={{0,24},{8,0},{16,8},{24,16},{1,25},{9,1},{17,9},{25,17},{2,26},{10... | collective-permute-start | bytes 1572872 | tf_op jit(solution)/shard_map/ppermute | solution.py:181
  122.6 42.7 %collective-permute-start.8 = (bf16[128,2048]{1,0:T(8,128)(2,1)}, bf16[128,2048]{1,0:T(8,128)(2,1)S(1)}, u32[]{:S(2)}, u32[]{:S(2)}) collective-permute-start(bf16[128,2048]{1,0:T(8,128)(2,1)} %bitcast.175), channel_id=1, source_target_pairs={{0,16},{8,24},{16,0},{24,8},{1,17},{9,25},{17,1},{25,9},{2,18},{10... | collective-permute-start | bytes 1572872 | tf_op jit(solution)/shard_map/ppermute | solution.py:181
  132.4 32.9 %collective-permute-start.9 = (bf16[128,2048]{1,0:T(8,128)(2,1)}, bf16[128,2048]{1,0:T(8,128)(2,1)S(1)}, u32[]{:S(2)}, u32[]{:S(2)}) collective-permute-start(bf16[128,2048]{1,0:T(8,128)(2,1)} %bitcast.176), channel_id=1, source_target_pairs={{0,8},{8,16},{16,24},{24,0},{1,9},{9,17},{17,25},{25,1},{2,10},{10... | collective-permute-start | bytes 1572872 | tf_op jit(solution)/shard_map/ppermute | solution.py:181
  175.2 306.8 %reduce-scatter.5.cloned.1.call-start = ((), (), s32[]{:S(2)}) async-start(), calls=%async_computation.12 | async-start | bytes 14417920 | tf_op jit(solution)/shard_map/reduce_scatter | solution.py:136
  181.9 65.4 %collective-permute-start.21 = (bf16[4,128,2048]{2,1,0:T(8,128)(2,1)S(1)}, bf16[4,128,2048]{2,1,0:T(8,128)(2,1)}, u32[]{:S(2)}, u32[]{:S(2)}) collective-permute-start(bf16[4,128,2048]{2,1,0:T(8,128)(2,1)S(1)} %pad_maximum_fusion.1.g_mine), channel_id=1, source_target_pairs={{0,4},{4,0},{1,5},{5,1},{2,6},{6,2},{3,7},{7,3},{8,12},{12,8},{9,1... | collective-permute-start | bytes 6291464 | tf_op jit(solution)/shard_map/ppermute | solution.py:81
  191.1 48.4 %collective-permute-start.15 = (bf16[128,2048]{1,0:T(8,128)(2,1)}, bf16[128,2048]{1,0:T(8,128)(2,1)S(1)}, u32[]{:S(2)}, u32[]{:S(2)}) collective-permute-start(bf16[128,2048]{1,0:T(8,128)(2,1)} %get-tuple-element.155), channel_id=1, source_target_pairs={{0,16},{8,24},{16,0},{24,8},{1,17},{9,25},{17,1},{25,9},{2,18},{10... | collective-permute-start | bytes 1572872 | tf_op jit(solution)/shard_map/ppermute | solution.py:181
  193.4 46.9 %collective-permute-start.14 = (bf16[128,2048]{1,0:T(8,128)(2,1)}, bf16[128,2048]{1,0:T(8,128)(2,1)}, u32[]{:S(2)}, u32[]{:S(2)}) collective-permute-start(bf16[128,2048]{1,0:T(8,128)(2,1)} %get-tuple-element.153), channel_id=1, source_target_pairs={{0,8},{8,16},{16,24},{24,0},{1,9},{9,17},{17,25},{25,1},{2,10},{10... | collective-permute-start | bytes 1572872 | tf_op jit(solution)/shard_map/ppermute | solution.py:181
  195.5 51.8 %collective-permute-start.20 = (bf16[176,2048]{1,0:T(8,128)(2,1)}, bf16[176,2048]{1,0:T(8,128)(2,1)S(1)}, u32[]{:S(2)}, u32[]{:S(2)}) collective-permute-start(bf16[176,2048]{1,0:T(8,128)(2,1)} %collective-permute-done.12.refs_6_), channel_id=1, source_target_pairs={{0,1},{1,0},{2,3},{3,2},{4,5},{5,4},{6,7},{7,6},{8,9},{9,8},{10,11... | collective-permute-start | bytes 2162696 | tf_op jit(solution)/shard_map/ppermute | solution.py:77
  243.1 37.9 %collective-permute-start.18 = (bf16[128,2048]{1,0:T(8,128)(2,1)S(1)}, bf16[128,2048]{1,0:T(8,128)(2,1)S(1)}, u32[]{:S(2)}, u32[]{:S(2)}) collective-permute-start(bf16[128,2048]{1,0:T(8,128)(2,1)S(1)} %get-tuple-element.139), channel_id=1, source_target_pairs={{0,16},{8,24},{16,0},{24,8},{1,17},{9,25},{17,1},{25,9},{2,18},{10... | collective-permute-start | bytes 1572872 | tf_op jit(solution)/shard_map/ppermute | solution.py:181
  243.2 37.8 %collective-permute-start.17 = (bf16[128,2048]{1,0:T(8,128)(2,1)S(1)}, bf16[128,2048]{1,0:T(8,128)(2,1)S(1)}, u32[]{:S(2)}, u32[]{:S(2)}) collective-permute-start(bf16[128,2048]{1,0:T(8,128)(2,1)S(1)} %get-tuple-element.139), channel_id=1, source_target_pairs={{0,24},{8,0},{16,8},{24,16},{1,25},{9,1},{17,9},{25,17},{2,26},{10... | collective-permute-start | bytes 1572872 | tf_op jit(solution)/shard_map/ppermute | solution.py:181
  336.7 289.8 %reduce-scatter.9.cloned.1.call-start = ((), (), s32[]{:S(2)}) async-start(), calls=%async_computation.14 | async-start | bytes 11796480 | tf_op jit(solution)/shard_map/reduce_scatter | solution.py:136
  381.2 59.6 %collective-permute-start.27 = (bf16[128,2048]{1,0:T(8,128)(2,1)}, bf16[128,2048]{1,0:T(8,128)(2,1)S(1)}, u32[]{:S(2)}, u32[]{:S(2)}) collective-permute-start(bf16[128,2048]{1,0:T(8,128)(2,1)} %get-tuple-element.151), channel_id=1, source_target_pairs={{0,24},{8,0},{16,8},{24,16},{1,25},{9,1},{17,9},{25,17},{2,26},{10... | collective-permute-start | bytes 1572872 | tf_op jit(solution)/shard_map/ppermute | solution.py:181
  393.9 47.0 %collective-permute-start.26 = (bf16[128,2048]{1,0:T(8,128)(2,1)}, bf16[128,2048]{1,0:T(8,128)(2,1)S(1)}, u32[]{:S(2)}, u32[]{:S(2)}) collective-permute-start(bf16[128,2048]{1,0:T(8,128)(2,1)} %get-tuple-element.152), channel_id=1, source_target_pairs={{0,16},{8,24},{16,0},{24,8},{1,17},{9,25},{17,1},{25,9},{2,18},{10... | collective-permute-start | bytes 1572872 | tf_op jit(solution)/shard_map/ppermute | solution.py:181
  394.7 47.7 %collective-permute-start.25 = (bf16[128,2048]{1,0:T(8,128)(2,1)}, bf16[128,2048]{1,0:T(8,128)(2,1)}, u32[]{:S(2)}, u32[]{:S(2)}) collective-permute-start(bf16[128,2048]{1,0:T(8,128)(2,1)} %get-tuple-element.150), channel_id=1, source_target_pairs={{0,8},{8,16},{16,24},{24,0},{1,9},{9,17},{17,25},{25,1},{2,10},{10... | collective-permute-start | bytes 1572872 | tf_op jit(solution)/shard_map/ppermute | solution.py:181
  465.0 209.5 %reduce-scatter.7.cloned.1.call-start = ((), (), s32[]{:S(2)}) async-start(), calls=%async_computation.13 | async-start | bytes 5242880 | tf_op jit(solution)/shard_map/reduce_scatter | solution.py:1229
  466.0 38.0 %collective-permute-start.29 = (bf16[128,2048]{1,0:T(8,128)(2,1)S(1)}, bf16[128,2048]{1,0:T(8,128)(2,1)}, u32[]{:S(2)}, u32[]{:S(2)}) collective-permute-start(bf16[128,2048]{1,0:T(8,128)(2,1)S(1)} %fusion.56), channel_id=1, source_target_pairs={{0,16},{8,24},{16,0},{24,8},{1,17},{9,25},{17,1},{25,9},{2,18},{10... | collective-permute-start | bytes 1572872 | tf_op jit(solution)/shard_map/ppermute | solution.py:181
  468.0 36.1 %collective-permute-start.28 = (bf16[128,2048]{1,0:T(8,128)(2,1)S(1)}, bf16[128,2048]{1,0:T(8,128)(2,1)}, u32[]{:S(2)}, u32[]{:S(2)}) collective-permute-start(bf16[128,2048]{1,0:T(8,128)(2,1)S(1)} %fusion.56), channel_id=1, source_target_pairs={{0,24},{8,0},{16,8},{24,16},{1,25},{9,1},{17,9},{25,17},{2,26},{10... | collective-permute-start | bytes 1572872 | tf_op jit(solution)/shard_map/ppermute | solution.py:181
  550.8 134.6 %reduce-scatter.11.cloned.1.call-start = ((), (), s32[]{:S(2)}) async-start(), calls=%async_computation.15 | async-start | bytes 7208960 | tf_op jit(solution)/shard_map/reduce_scatter | solution.py:136
  556.6 52.0 %collective-permute-start.35 = (bf16[128,2048]{1,0:T(8,128)(2,1)}, bf16[128,2048]{1,0:T(8,128)(2,1)}, u32[]{:S(2)}, u32[]{:S(2)}) collective-permute-start(bf16[128,2048]{1,0:T(8,128)(2,1)} %get-tuple-element.148), channel_id=1, source_target_pairs={{0,24},{8,0},{16,8},{24,16},{1,25},{9,1},{17,9},{25,17},{2,26},{10... | collective-permute-start | bytes 1572872 | tf_op jit(solution)/shard_map/ppermute | solution.py:181
  568.8 38.5 %all-to-all-start.2 = ((f32[32,3,128]{2,1,0:T(4,128)}), f32[32,3,128]{2,1,0:T(4,128)S(1)}, u32[]{:S(2)}, u32[]{:S(2)}) async-start(f32[32,3,128]{2,1,0:T(4,128)} %reshape.241), calls=%async_computation.3 | async-start | bytes 131072 | tf_op jit(solution)/shard_map/all_to_all | solution.py:1027
  571.7 44.2 %collective-permute-start.34 = (bf16[128,2048]{1,0:T(8,128)(2,1)}, bf16[128,2048]{1,0:T(8,128)(2,1)}, u32[]{:S(2)}, u32[]{:S(2)}) collective-permute-start(bf16[128,2048]{1,0:T(8,128)(2,1)} %get-tuple-element.149), channel_id=1, source_target_pairs={{0,16},{8,24},{16,0},{24,8},{1,17},{9,25},{17,1},{25,9},{2,18},{10... | collective-permute-start | bytes 1572872 | tf_op jit(solution)/shard_map/ppermute | solution.py:181
  574.4 41.5 %collective-permute-start.33 = (bf16[128,2048]{1,0:T(8,128)(2,1)}, bf16[128,2048]{1,0:T(8,128)(2,1)}, u32[]{:S(2)}, u32[]{:S(2)}) collective-permute-start(bf16[128,2048]{1,0:T(8,128)(2,1)} %get-tuple-element.147), channel_id=1, source_target_pairs={{0,8},{8,16},{16,24},{24,0},{1,9},{9,17},{17,25},{25,1},{2,10},{10... | collective-permute-start | bytes 1572872 | tf_op jit(solution)/shard_map/ppermute | solution.py:181
  579.0 102.0 %collective-permute-start.40 = (bf16[256,2816]{1,0:T(8,128)(2,1)}, bf16[256,2816]{1,0:T(8,128)(2,1)}, u32[]{:S(2)}, u32[]{:S(2)}) collective-permute-start(bf16[256,2816]{1,0:T(8,128)(2,1)} %select_bitcast_fusion), channel_id=1, source_target_pairs={{0,4},{4,0},{1,5},{5,1},{2,6},{6,2},{3,7},{7,3},{8,12},{12,8},{9,1... | collective-permute-start | bytes 4325384 | tf_op jit(solution)/shard_map/ppermute | solution.py:81
  621.9 48.8 %collective-permute-start.37 = (bf16[128,2048]{1,0:T(8,128)(2,1)}, bf16[128,2048]{1,0:T(8,128)(2,1)}, u32[]{:S(2)}, u32[]{:S(2)}) collective-permute-start(bf16[128,2048]{1,0:T(8,128)(2,1)} %get-tuple-element.146), channel_id=1, source_target_pairs={{0,16},{8,24},{16,0},{24,8},{1,17},{9,25},{17,1},{25,9},{2,18},{10... | collective-permute-start | bytes 1572872 | tf_op jit(solution)/shard_map/ppermute | solution.py:181
  624.5 46.2 %collective-permute-start.36 = (bf16[128,2048]{1,0:T(8,128)(2,1)}, bf16[128,2048]{1,0:T(8,128)(2,1)}, u32[]{:S(2)}, u32[]{:S(2)}) collective-permute-start(bf16[128,2048]{1,0:T(8,128)(2,1)} %get-tuple-element.144), channel_id=1, source_target_pairs={{0,8},{8,16},{16,24},{24,0},{1,9},{9,17},{17,25},{25,1},{2,10},{10... | collective-permute-start | bytes 1572872 | tf_op jit(solution)/shard_map/ppermute | solution.py:181
  629.0 62.2 %collective-permute-start.39 = (bf16[256,2304]{1,0:T(8,128)(2,1)}, bf16[256,2304]{1,0:T(8,128)(2,1)}, u32[]{:S(2)}, u32[]{:S(2)}) collective-permute-start(bf16[256,2304]{1,0:T(8,128)(2,1)} %dynamic-slice_bitcast_fusion), channel_id=1, source_target_pairs={{0,4},{4,0},{1,5},{5,1},{2,6},{6,2},{3,7},{7,3},{8,12},{12,8},{9,1... | collective-permute-start | bytes 3538952 | tf_op jit(solution)/shard_map/ppermute | solution.py:81
  (59 other events, 924.0 us)
Sparse Core Ops, SparseCore 0:
  9.9 54.9 all-gather.4
  66.5 47.1 all-gather.6
  115.5 144.9 all-gather.8
  262.3 67.6 all-gather.10
  336.8 121.3 reduce-scatter.4
  465.1 94.1 reduce-scatter.8
  562.3 53.4 reduce-scatter.6
  619.7 65.6 reduce-scatter.10
